TPU v7x, 32 devices: a whole 2x2x4 slice. The times are simulated.
32 devices in a mesh: clip: 4 (over x, core), seq: 8 (over z, y).
Axes of the slice: x: 2, y: 2, z: 4, core: 2. Of those that a mesh axis runs over, the one named last changes fastest.
Arguments:
- frames_in: bfloat16 [8, 4096, 1024], P('clip', 'seq')
- noise_level: int32 [8, 16], P('clip'), may hold values from 0 to 999
- frame_time: int32 [8, 16], P('clip'), may hold values from 0 to 45, as said below
- cotangent: bfloat16 [8, 4096, 1024], P('clip', 'seq'), may hold values from -6 to 6
- joint_weight: float32 [1024, 3072], P(('clip', 'seq')), may hold values from -0.1875 to 0.1875
- output_weight: float32 [1024, 1024], P(('clip', 'seq')), may hold values from -6 to 6
- up_weight: float32 [1024, 4096], P(('clip', 'seq')), may hold values from -0.1875 to 0.1875
- down_weight: float32 [4096, 1024], P(('clip', 'seq')), may hold values from -0.09375 to 0.09375
- modulation: float32 [1024, 6144], P(('clip', 'seq')), may hold values from -0.1875 to 0.1875
- modulation_bias: float32 [6144], P(('clip', 'seq')), may hold values from -3 to 3
- first_joint: float32 [1024, 3072], P(('clip', 'seq')), may hold values from -0.0014648438 to 0.0014648438
- first_output: float32 [1024, 1024], P(('clip', 'seq')), may hold values from -0.00024414062 to 0.00024414062
- first_up: float32 [1024, 4096], P(('clip', 'seq')), may hold values from -0.00030517578 to 0.00030517578
- first_down: float32 [4096, 1024], P(('clip', 'seq')), may hold values from -0.00036621094 to 0.00036621094
- first_modulation: float32 [1024, 6144], P(('clip', 'seq')), may hold values from -0.0014648438 to 0.0014648438
- first_bias: float32 [6144], P(('clip', 'seq')), may hold values from -0.005859375 to 0.005859375
- second_joint: float32 [1024, 3072], P(('clip', 'seq')), may hold values from 5.2964666e-08 to 2.1185866e-07
- second_output: float32 [1024, 1024], P(('clip', 'seq')), may hold values from 1.58894e-09 to 6.35576e-09
- second_up: float32 [1024, 4096], P(('clip', 'seq')), may hold values from 2.3304452e-09 to 9.321781e-09
- second_down: float32 [4096, 1024], P(('clip', 'seq')), may hold values from 4.2371733e-09 to 1.6948693e-08
- second_modulation: float32 [1024, 6144], P(('clip', 'seq')), may hold values from 5.2964666e-08 to 2.1185866e-07
- second_bias: float32 [6144], P(('clip', 'seq')), may hold values from 8.4743465e-07 to 3.3897386e-06
Outputs:
- mixed: bfloat16 [8, 4096, 1024], P('clip', 'seq')
- input_grad: float32 [8, 4096, 1024], P('clip', 'seq')
- grad_joint: float32 [1024, 3072], P(('clip', 'seq'))
- grad_output: float32 [1024, 1024], P(('clip', 'seq'))
- grad_up: float32 [1024, 4096], P(('clip', 'seq'))
- grad_down: float32 [4096, 1024], P(('clip', 'seq'))
- grad_modulation: float32 [1024, 6144], P(('clip', 'seq'))
- grad_bias: float32 [6144], P(('clip', 'seq'))
- grad_norm: float32 [], replicated
- new_first_joint: float32 [1024, 3072], P(('clip', 'seq'))
- new_first_output: float32 [1024, 1024], P(('clip', 'seq'))
- new_first_up: float32 [1024, 4096], P(('clip', 'seq'))
- new_first_down: float32 [4096, 1024], P(('clip', 'seq'))
- new_first_modulation: float32 [1024, 6144], P(('clip', 'seq'))
- new_first_bias: float32 [6144], P(('clip', 'seq'))
- new_second_joint: float32 [1024, 3072], P(('clip', 'seq'))
- new_second_output: float32 [1024, 1024], P(('clip', 'seq'))
- new_second_up: float32 [1024, 4096], P(('clip', 'seq'))
- new_second_down: float32 [4096, 1024], P(('clip', 'seq'))
- new_second_modulation: float32 [1024, 6144], P(('clip', 'seq'))
- new_second_bias: float32 [6144], P(('clip', 'seq'))
- new_joint: float32 [1024, 3072], P(('clip', 'seq'))
- new_output: float32 [1024, 1024], P(('clip', 'seq'))
- new_up: float32 [1024, 4096], P(('clip', 'seq'))
- new_down: float32 [4096, 1024], P(('clip', 'seq'))
- new_modulation: float32 [1024, 6144], P(('clip', 'seq'))
- new_bias: float32 [6144], P(('clip', 'seq'))
- copy_joint: bfloat16 [1024, 3072], P(('clip', 'seq'))
- copy_output: bfloat16 [1024, 1024], P(('clip', 'seq'))
- copy_up: bfloat16 [1024, 4096], P(('clip', 'seq'))
- copy_down: bfloat16 [4096, 1024], P(('clip', 'seq'))
- copy_modulation: bfloat16 [1024, 6144], P(('clip', 'seq'))
- copy_bias: bfloat16 [6144], P(('clip', 'seq'))
Inputs may be any that keep to these rules, and one draw needn't show every extreme that they name: `frame_time`: within each clip the first frame's time is 0 and each later frame's time exceeds the one before by 1 to 3; in some clip every step is 3, so that its last frame's time is 45.
All inputs are finite; a program needn't handle non-finite values.
Results may differ from a plain program's by a relative error of at most 0.015.
The roundings to bfloat16 on the way count: a program that leaves them out, or rounds other values in their place, can miss the bound.
Values may be sent and summed in bfloat16 or wider, within the bound.
No kernel may reach another device: no remote copies, remote signals or barrier semaphores. Data moves between devices by JAX's collectives and lax.ppermute only.
A program may use at most 384 MiB of HBM per device.

v0:
```python
from functools import partial
import math

import jax
import jax.numpy as jnp
from jax import lax
from jax.sharding import PartitionSpec as P

D = 1024
HEADS = 16
HEAD = 64
FF = 4096
FRAMES = 16
GRID_W = 16
STEP = 10
PATCHES = 256
LENGTH = 4096


norm_epsilon = 1e-06
adam_epsilon = 1e-08
first_decay = 0.5
second_decay = 0.5
weight_decay = 0.1
clip_limit = 1.0
highest = lax.Precision.HIGHEST


def sinusoid(levels):
    half_width = D // 2
    frequency = jnp.exp(-math.log(10000.0) * jnp.arange(half_width, dtype=jnp.float32) / half_width)
    angles = levels.astype(jnp.float32)[..., None] * frequency
    return jnp.concatenate([jnp.cos(angles), jnp.sin(angles)], axis=-1)


def rotary_angles(frame_time, first_place, number):
    places = first_place + jnp.arange(number, dtype=jnp.int32)
    frame_ids = places // PATCHES
    patch_row = (places % PATCHES // GRID_W).astype(jnp.float32)
    column = (places % GRID_W).astype(jnp.float32)
    matches = frame_ids[:, None] == jnp.arange(FRAMES, dtype=jnp.int32)[None, :]
    moment = jnp.sum(jnp.where(matches[None], frame_time[:, None, :], 0), axis=-1).astype(
        jnp.float32
    )
    pair_count = HEAD // 2
    time_pairs = HEAD // 8
    grid_pairs = 3 * HEAD // 16
    pair_ids = jnp.arange(pair_count, dtype=jnp.int32)
    offset = jnp.where(
        pair_ids < time_pairs,
        0,
        jnp.where(pair_ids < time_pairs + grid_pairs, time_pairs, time_pairs + grid_pairs),
    )
    length = jnp.where(pair_ids < time_pairs, time_pairs, grid_pairs)
    frequency = jnp.exp(
        -math.log(10000.0) * (pair_ids - offset).astype(jnp.float32) / length.astype(jnp.float32)
    )
    coordinate = jnp.where(
        pair_ids < time_pairs,
        moment[..., None],
        jnp.where(
            pair_ids < time_pairs + grid_pairs, patch_row[None, :, None], column[None, :, None]
        ),
    )
    angles = coordinate * frequency
    return (jnp.cos(angles), jnp.sin(angles))


def rotate(operand, cosines, sine_part):
    half_size = operand.shape[-1] // 2
    first_half = operand[..., :half_size]
    second_half = operand[..., half_size:]
    cosines = cosines[..., None, :]
    sine_part = sine_part[..., None, :]
    return jnp.concatenate(
        [
            first_half * cosines - second_half * sine_part,
            second_half * cosines + first_half * sine_part,
        ],
        axis=-1,
    )


def normalize(operand):
    centered = operand - jnp.mean(operand, axis=-1, keepdims=True)
    variance = jnp.mean(centered * centered, axis=-1, keepdims=True)
    return centered * lax.rsqrt(variance + norm_epsilon)


def modulate(operand, shift_by, scale_by):
    return normalize(operand) * (1.0 + scale_by) + shift_by


def contract_rows(left, right):
    return lax.dot_general(
        left, right, (((0,), (0,)), ((), ())), preferred_element_type=jnp.float32
    )


def contract_last(left, right):
    return lax.dot_general(
        left, right, (((1,), (1,)), ((), ())), preferred_element_type=jnp.float32
    )


def score_block(query_rows, key_rows):
    return jnp.einsum(
        "cqhe,ckhe->chqk", query_rows, key_rows, preferred_element_type=jnp.float32
    ) * HEAD ** (-0.5)


def adam_update(gradient, master, moment_one, moment_two, step_rate):
    moment_one = first_decay * moment_one + (1.0 - first_decay) * gradient
    moment_two = second_decay * moment_two + (1.0 - second_decay) * gradient * gradient
    corrected_one = moment_one / (1.0 - first_decay**STEP)
    corrected_two = moment_two / (1.0 - second_decay**STEP)
    master = master - step_rate * (
        corrected_one / (jnp.sqrt(corrected_two) + adam_epsilon) + weight_decay * master
    )
    return (moment_one, moment_two, master)


def per_device(
    frames_in,
    noise_level,
    frame_time,
    cotangent,
    joint_weight,
    output_weight,
    up_weight,
    down_weight,
    modulation,
    modulation_bias,
    first_joint,
    first_output,
    first_up,
    first_down,
    first_modulation,
    first_bias,
    second_joint,
    second_output,
    second_up,
    second_down,
    second_modulation,
    second_bias,
):
    masters = (joint_weight, output_weight, up_weight, down_weight, modulation, modulation_bias)
    joint_full, output_full, upward, downward, mod_full, bias_full = (
        lax.all_gather(joint_weight.astype(jnp.bfloat16), ("clip", "seq"), axis=0, tiled=True),
        lax.all_gather(output_weight.astype(jnp.bfloat16), ("clip", "seq"), axis=0, tiled=True),
        lax.all_gather(up_weight.astype(jnp.bfloat16), ("clip", "seq"), axis=0, tiled=True),
        lax.all_gather(down_weight.astype(jnp.bfloat16), ("clip", "seq"), axis=0, tiled=True),
        lax.all_gather(modulation.astype(jnp.bfloat16), ("clip", "seq"), axis=0, tiled=True),
        lax.all_gather(modulation_bias.astype(jnp.bfloat16), ("clip", "seq"), axis=0, tiled=True),
    )
    clip_count = frames_in.shape[0]
    local_rows = frames_in.shape[1]
    token_count = clip_count * local_rows
    first_place = lax.axis_index("seq") * local_rows
    frame_count = max(1, local_rows // PATCHES)
    per_frame = local_rows // frame_count
    levels = lax.dynamic_slice_in_dim(noise_level, first_place // PATCHES, frame_count, 1)
    condition_low = (
        jax.nn.silu(sinusoid(levels)).astype(jnp.bfloat16).reshape(clip_count * frame_count, D)
    )
    modulated = jnp.dot(
        condition_low, mod_full, preferred_element_type=jnp.float32
    ) + bias_full.astype(jnp.float32)
    pieces = modulated.reshape(clip_count, frame_count, 6, 1, D)
    shift_one = pieces[:, :, 0]
    scale_one = pieces[:, :, 1]
    gate_one = pieces[:, :, 2]
    shift_two = pieces[:, :, 3]
    scale_two = pieces[:, :, 4]
    gate_two = pieces[:, :, 5]
    tokens = frames_in.astype(jnp.float32).reshape(clip_count, frame_count, per_frame, D)
    normed_one = modulate(tokens, shift_one, scale_one)
    normed_one_low = normed_one.astype(jnp.bfloat16).reshape(token_count, D)
    joint_out = jnp.dot(normed_one_low, joint_full, preferred_element_type=jnp.float32).reshape(
        clip_count, local_rows, 3, HEADS, HEAD
    )
    cosines, sine_part = rotary_angles(frame_time, first_place, local_rows)
    queries = rotate(joint_out[:, :, 0], cosines, sine_part).astype(jnp.bfloat16)
    own_keys = rotate(joint_out[:, :, 1], cosines, sine_part).astype(jnp.bfloat16)
    own_values = joint_out[:, :, 2].astype(jnp.bfloat16)
    all_keys, all_values = (
        lax.all_gather(own_keys, "seq", axis=1, tiled=True),
        lax.all_gather(own_values, "seq", axis=1, tiled=True),
    )
    sequence = all_keys.shape[1]
    key_block = min(512, sequence)
    block_count = sequence // key_block

    def max_step(block_id, carried):
        running_max, running_sum = carried
        keys_here = lax.dynamic_slice_in_dim(all_keys, block_id * key_block, key_block, 1)
        scores = score_block(queries, keys_here)
        new_max = jnp.maximum(running_max, jnp.max(scores, axis=-1))
        running_sum = running_sum * jnp.exp(running_max - new_max) + jnp.sum(
            jnp.exp(scores - new_max[..., None]), axis=-1
        )
        return (new_max, running_sum)

    start_max = jnp.full((clip_count, HEADS, local_rows), -1e30, jnp.float32)
    running_max, running_sum = lax.fori_loop(
        0, block_count, max_step, (start_max, jnp.zeros_like(start_max))
    )
    log_total = running_max + jnp.log(running_sum)

    def value_step(block_id, accumulated):
        keys_here = lax.dynamic_slice_in_dim(all_keys, block_id * key_block, key_block, 1)
        values_here = lax.dynamic_slice_in_dim(all_values, block_id * key_block, key_block, 1)
        probs_low = jnp.exp(score_block(queries, keys_here) - log_total[..., None]).astype(
            jnp.bfloat16
        )
        return accumulated + jnp.einsum(
            "chqk,ckhe->cqhe", probs_low, values_here, preferred_element_type=jnp.float32
        )

    attended = lax.fori_loop(
        0, block_count, value_step, jnp.zeros((clip_count, local_rows, HEADS, HEAD), jnp.float32)
    )
    attended_low = attended.astype(jnp.bfloat16).reshape(token_count, D)
    projected = jnp.dot(attended_low, output_full, preferred_element_type=jnp.float32).reshape(
        clip_count, frame_count, per_frame, D
    )
    middle = tokens + gate_one * projected
    normed_two = modulate(middle, shift_two, scale_two)
    normed_two_low = normed_two.astype(jnp.bfloat16).reshape(token_count, D)
    upper_out = jnp.dot(normed_two_low, upward, preferred_element_type=jnp.float32)
    hidden_low = jax.nn.gelu(upper_out, approximate=True).astype(jnp.bfloat16)
    branch = jnp.dot(hidden_low, downward, preferred_element_type=jnp.float32).reshape(
        clip_count, frame_count, per_frame, D
    )
    result = middle + gate_two * branch
    mixed = result.astype(jnp.bfloat16).reshape(clip_count, local_rows, D)
    upstream = cotangent.astype(jnp.float32).reshape(clip_count, frame_count, per_frame, D)
    gate_two_grad = jnp.sum(upstream * branch, axis=2, keepdims=True)
    branch_grad = (gate_two * upstream).astype(jnp.bfloat16).reshape(token_count, D)
    down_grad = contract_rows(hidden_low, branch_grad)
    hidden_grad = contract_last(branch_grad, downward)
    gelu_pull = jax.vjp(partial(jax.nn.gelu, approximate=True), upper_out)[1]
    upper_grad = gelu_pull(hidden_grad)[0].astype(jnp.bfloat16)
    up_grad = contract_rows(normed_two_low, upper_grad)
    normed_two_grad = contract_last(upper_grad, upward).reshape(
        clip_count, frame_count, per_frame, D
    )
    middle_pull = jax.vjp(modulate, middle, shift_two, scale_two)[1]
    middle_grad, shift_two_grad, scale_two_grad = middle_pull(normed_two_grad)
    middle_grad = middle_grad + upstream
    gate_one_grad = jnp.sum(middle_grad * projected, axis=2, keepdims=True)
    projected_grad = (gate_one * middle_grad).astype(jnp.bfloat16).reshape(token_count, D)
    output_grad = contract_rows(attended_low, projected_grad)
    outer_grad = (
        contract_last(projected_grad, output_full)
        .astype(jnp.bfloat16)
        .reshape(clip_count, local_rows, HEADS, HEAD)
    )
    row_delta = jnp.swapaxes(jnp.sum(outer_grad.astype(jnp.float32) * attended, axis=-1), 1, 2)

    def grad_step(block_id, carried):
        query_grad, key_grads, value_grads = carried
        keys_here = lax.dynamic_slice_in_dim(all_keys, block_id * key_block, key_block, 1)
        values_here = lax.dynamic_slice_in_dim(all_values, block_id * key_block, key_block, 1)
        prob_values = jnp.exp(score_block(queries, keys_here) - log_total[..., None])
        value_part = jnp.einsum(
            "chqk,cqhe->ckhe",
            prob_values.astype(jnp.bfloat16),
            outer_grad,
            preferred_element_type=jnp.float32,
        )
        prob_grad = jnp.einsum(
            "cqhe,ckhe->chqk", outer_grad, values_here, preferred_element_type=jnp.float32
        )
        score_grad = (prob_values * (prob_grad - row_delta[..., None])).astype(jnp.bfloat16)
        query_grad = query_grad + jnp.einsum(
            "chqk,ckhe->cqhe", score_grad, keys_here, preferred_element_type=jnp.float32
        )
        key_part = jnp.einsum(
            "chqk,cqhe->ckhe", score_grad, queries, preferred_element_type=jnp.float32
        )
        key_grads = lax.dynamic_update_slice_in_dim(key_grads, key_part, block_id * key_block, 1)
        value_grads = lax.dynamic_update_slice_in_dim(
            value_grads, value_part, block_id * key_block, 1
        )
        return (query_grad, key_grads, value_grads)

    empty_full = jnp.zeros((clip_count, sequence, HEADS, HEAD), jnp.float32)
    query_grad, key_grads, value_grads = lax.fori_loop(
        0,
        block_count,
        grad_step,
        (jnp.zeros((clip_count, local_rows, HEADS, HEAD), jnp.float32), empty_full, empty_full),
    )
    key_grads, value_grads = (
        lax.psum_scatter(
            key_grads.astype(jnp.bfloat16), "seq", scatter_dimension=1, tiled=True
        ).astype(jnp.float32),
        lax.psum_scatter(
            value_grads.astype(jnp.bfloat16), "seq", scatter_dimension=1, tiled=True
        ).astype(jnp.float32),
    )
    query_grad = rotate(query_grad * HEAD ** (-0.5), cosines, -sine_part)
    key_grads = rotate(key_grads * HEAD ** (-0.5), cosines, -sine_part)
    joint_grad_rows = (
        jnp.stack([query_grad, key_grads, value_grads], axis=2)
        .astype(jnp.bfloat16)
        .reshape(token_count, 3 * D)
    )
    joint_grad = contract_rows(normed_one_low, joint_grad_rows)
    normed_one_grad = contract_last(joint_grad_rows, joint_full).reshape(
        clip_count, frame_count, per_frame, D
    )
    tokens_pull = jax.vjp(modulate, tokens, shift_one, scale_one)[1]
    token_grad, shift_one_grad, scale_one_grad = tokens_pull(normed_one_grad)
    input_grad = (token_grad + middle_grad).reshape(clip_count, local_rows, D)
    piece_grads = jnp.stack(
        [
            shift_one_grad,
            scale_one_grad,
            gate_one_grad,
            shift_two_grad,
            scale_two_grad,
            gate_two_grad,
        ],
        axis=2,
    ).reshape(clip_count * frame_count, 6 * D)
    mod_grad = jnp.dot(condition_low.astype(jnp.float32).T, piece_grads, precision=highest)
    bias_grad = jnp.sum(piece_grads, axis=0)
    summed = (
        lax.psum_scatter(joint_grad, ("clip", "seq"), scatter_dimension=0, tiled=True),
        lax.psum_scatter(output_grad, ("clip", "seq"), scatter_dimension=0, tiled=True),
        lax.psum_scatter(up_grad, ("clip", "seq"), scatter_dimension=0, tiled=True),
        lax.psum_scatter(down_grad, ("clip", "seq"), scatter_dimension=0, tiled=True),
        lax.psum_scatter(mod_grad, ("clip", "seq"), scatter_dimension=0, tiled=True),
        lax.psum_scatter(bias_grad, ("clip", "seq"), scatter_dimension=0, tiled=True),
    )
    local_squares = sum((jnp.sum(shard * shard) for shard in summed))
    grad_norm = jnp.sqrt(lax.psum(local_squares, ("clip", "seq")))
    factor = jnp.minimum(1.0, clip_limit / (grad_norm + 1e-06))
    step_rates = (
        D ** (-0.5),
        max(1, 2 * D // LENGTH) ** (-0.5),
        D ** (-0.5),
        FF ** (-0.5),
        D ** (-0.5),
        0.5,
    )
    firsts = (first_joint, first_output, first_up, first_down, first_modulation, first_bias)
    seconds = (second_joint, second_output, second_up, second_down, second_modulation, second_bias)
    clipped = [shard * factor for shard in summed]
    updates = [
        adam_update(clipped[slot], masters[slot], firsts[slot], seconds[slot], step_rates[slot])
        for slot in range(6)
    ]
    return (
        mixed,
        input_grad,
        clipped[0],
        clipped[1],
        clipped[2],
        clipped[3],
        clipped[4],
        clipped[5],
        grad_norm,
        updates[0][0],
        updates[1][0],
        updates[2][0],
        updates[3][0],
        updates[4][0],
        updates[5][0],
        updates[0][1],
        updates[1][1],
        updates[2][1],
        updates[3][1],
        updates[4][1],
        updates[5][1],
        updates[0][2],
        updates[1][2],
        updates[2][2],
        updates[3][2],
        updates[4][2],
        updates[5][2],
        updates[0][2].astype(jnp.bfloat16),
        updates[1][2].astype(jnp.bfloat16),
        updates[2][2].astype(jnp.bfloat16),
        updates[3][2].astype(jnp.bfloat16),
        updates[4][2].astype(jnp.bfloat16),
        updates[5][2].astype(jnp.bfloat16),
    )


def solution(mesh):
    in_specs = (
        P("clip", "seq", None),
        P("clip", None),
        P("clip", None),
        P("clip", "seq", None),
        P(("clip", "seq"), None),
        P(("clip", "seq"), None),
        P(("clip", "seq"), None),
        P(("clip", "seq"), None),
        P(("clip", "seq"), None),
        P(("clip", "seq")),
        P(("clip", "seq"), None),
        P(("clip", "seq"), None),
        P(("clip", "seq"), None),
        P(("clip", "seq"), None),
        P(("clip", "seq"), None),
        P(("clip", "seq")),
        P(("clip", "seq"), None),
        P(("clip", "seq"), None),
        P(("clip", "seq"), None),
        P(("clip", "seq"), None),
        P(("clip", "seq"), None),
        P(("clip", "seq")),
    )
    out_specs = (
        P("clip", "seq", None),
        P("clip", "seq", None),
        P(("clip", "seq"), None),
        P(("clip", "seq"), None),
        P(("clip", "seq"), None),
        P(("clip", "seq"), None),
        P(("clip", "seq"), None),
        P(("clip", "seq")),
        P(),
        P(("clip", "seq"), None),
        P(("clip", "seq"), None),
        P(("clip", "seq"), None),
        P(("clip", "seq"), None),
        P(("clip", "seq"), None),
        P(("clip", "seq")),
        P(("clip", "seq"), None),
        P(("clip", "seq"), None),
        P(("clip", "seq"), None),
        P(("clip", "seq"), None),
        P(("clip", "seq"), None),
        P(("clip", "seq")),
        P(("clip", "seq"), None),
        P(("clip", "seq"), None),
        P(("clip", "seq"), None),
        P(("clip", "seq"), None),
        P(("clip", "seq"), None),
        P(("clip", "seq")),
        P(("clip", "seq"), None),
        P(("clip", "seq"), None),
        P(("clip", "seq"), None),
        P(("clip", "seq"), None),
        P(("clip", "seq"), None),
        P(("clip", "seq")),
    )
    return jax.shard_map(
        per_device, mesh=mesh, in_specs=in_specs, out_specs=out_specs, check_vma=False
    )
```

profile of v0, /device:TPU:0, one launch (start us, length us, event | category | flops | bytes accessed | tf_op | source)
XLA Modules:
  0.0 3463.9 jit_solution(17810272773557185061)
XLA Ops:
  15.7 42.4 %all-reduce = bf16[6144]{0:T(1024)(128)(2,1)S(1)} all-reduce(bf16[6144]{0:T(1024)(128)(2,1)S(1)} %dynamic-update-slice), channel_id=1, replica_groups=mesh['clip'=4,'seq'=8] {'clip','seq'}, use_global_device_ids=true, to_apply=%add | all-reduce | flops 6144 | bytes 24576
  61.2 22.7 all-gather.11.cloned.1.call-done
  92.6 89.4 %all-gather.9.cloned.1.call-done = bf16[1024,6144]{1,0:T(8,128)(2,1)} async-done(((bf16[32,6144]{1,0:T(8,128)(2,1)}), bf16[1024,6144]{1,0:T(8,128)(2,1)}) %all-gather.9.cloned.1.call-update) | async-done | bytes 12582928 | tf_op jit(solution)/shard_map/all_gather | solution.py:153
  220.0 41.2 %all-gather.19.cloned.1.call-done = bf16[4096,1024]{1,0:T(8,128)(2,1)} async-done(((bf16[128,1024]{1,0:T(8,128)(2,1)}), bf16[4096,1024]{1,0:T(8,128)(2,1)}) %all-gather.19.cloned.1.call-update) | async-done | bytes 8388624 | tf_op jit(solution)/shard_map/all_gather | solution.py:152
  261.2 16.1 fusion.86
  277.3 212.2 %all-gather.13.cloned.1.call-done = bf16[2,4096,16,64]{1,3,2,0:T(8,128)(2,1)} async-done(((bf16[2,512,16,64]{1,3,2,0:T(8,128)(2,1)}), bf16[2,4096,16,64]{1,3,2,0:T(8,128)(2,1)}) %all-gather.13.cloned.1.call-update) | async-done | bytes 16777232 | tf_op jit(solution)/shard_map/all_gather | solution.py:187
  489.5 233.1 %while.48 = (s32[]{:T(128)}, f32[2,16,512]{2,1,0:T(8,128)S(1)}, f32[2,16,512]{2,1,0:T(8,128)S(1)}, bf16[2,4096,16,64]{1,3,2,0:T(8,128)(2,1)}, bf16[2,512,16,64]{...) while((s32[]{:T(128)}, f32[2,16,512]{2,1,0:T(8,128)S(1)}, ...), condition=%wide.region_6.7_spmd.clone, body=%wide.region_3.6_spmd.clone.sunk | while | flops 1115766784 | bytes 72155296 | solution.py:205
  489.5 16.7 bitcast_reduce_fusion.3
  577.6 15.8 bitcast_reduce_fusion.3
  722.6 108.5 %while.49 = (s32[]{:T(128)}, f32[2,512,16,64]{1,3,2,0:T(8,128)}, bf16[2,4096,16,64]{1,3,2,0:T(8,128)(2,1)}, bf16[2,4096,16,64]{1,3,2,0:T(8,128)(2,1)}, bf16[2,51...) while((s32[]{:T(128)}, f32[2,512,16,64]{1,3,2,0:T(8,128)}, ...), condition=%wide.region_8.9_spmd.clone, body=%wide.region_7.8_spmd.clone.sunk | while | flops 2174746624 | bytes 14747300 | solution.py:220
  857.1 27.4 fusion.34
  901.3 18.1 multiply_reduce_fusion
  963.6 588.4 %while.50 = (s32[]{:T(128)}, f32[2,512,16,64]{1,3,2,0:T(8,128)}, bf16[2,4096,16,64]{1,3,2,0:T(8,128)(2,1)}, bf16[2,4096,16,64]{1,3,2,0:T(8,128)(2,1)}, bf16[2,40...) while((s32[]{:T(128)}, f32[2,512,16,64]{1,3,2,0:T(8,128)}, ...), condition=%wide.region_15.16_spmd.clone, body=%wide.region_14.15_spmd.clone.sunk | while | flops 5437915136 | bytes 191037680 | solution.py:289
  978.8 20.5 multiply_convert_fusion.6
  1051.3 20.5 multiply_convert_fusion.6
  1125.0 20.5 multiply_convert_fusion.6
  1198.6 20.5 multiply_convert_fusion.6
  1272.3 20.5 multiply_convert_fusion.6
  1346.0 20.5 multiply_convert_fusion.6
  1419.7 20.5 multiply_convert_fusion.6
  1493.4 20.5 multiply_convert_fusion.6
  1578.5 18.6 fusion.71
  1602.8 230.4 %reduce-scatter.8.cloned.1.call-done = bf16[2,512,16,64]{1,3,2,0:T(8,128)(2,1)} async-done(((bf16[2,4096,16,64]{1,3,2,0:T(8,128)(2,1)}), bf16[2,512,16,64]{1,3,2,0:T(8,128)(2,1)}) %reduce-scatter.8.cloned.1.call-update) | async-done | bytes 2097168 | tf_op jit(solution)/shard_map/reduce_scatter | solution.py:296
  1839.2 280.0 %reduce-scatter.10.cloned.1.call-done = bf16[2,512,16,64]{1,3,2,0:T(8,128)(2,1)} async-done(((bf16[2,4096,16,64]{1,3,2,0:T(8,128)(2,1)}), bf16[2,512,16,64]{1,3,2,0:T(8,128)(2,1)}) %reduce-scatter.10.cloned.1.call-update) | async-done | bytes 2097168 | tf_op jit(solution)/shard_map/reduce_scatter | solution.py:299
  2154.0 16.5 reshape.503
  2209.9 54.1 %reduce-scatter.14.cloned.1.call-done = f32[32,1024]{1,0:T(8,128)} async-done(((f32[1024,1024]{1,0:T(8,128)}), f32[32,1024]{1,0:T(8,128)}) %reduce-scatter.14.cloned.1.call-update) | async-done | bytes 131088 | tf_op jit(solution)/shard_map/reduce_scatter | solution.py:332
  2265.6 48.5 %all-reduce.1 = f32[6144]{0:T(1024)S(1)} all-reduce(f32[6144]{0:T(1024)S(1)} %reduce_sum.276), channel_id=10, replica_groups=mesh['clip'=4,'seq'=8] {'clip','seq'}, use_global_device_ids=true, to_apply=%region_37.38.clone | all-reduce | flops 6144 | bytes 49152
  2314.8 308.2 %reduce-scatter.16.cloned.1.call-done = f32[32,4096]{1,0:T(8,128)} async-done(((f32[1024,4096]{1,0:T(8,128)}), f32[32,4096]{1,0:T(8,128)}) %reduce-scatter.16.cloned.1.call-update) | async-done | bytes 524304 | tf_op jit(solution)/shard_map/reduce_scatter | solution.py:333
  2624.7 357.8 %reduce-scatter.18.cloned.1.call-done = f32[128,1024]{1,0:T(8,128)} async-done(((f32[4096,1024]{1,0:T(8,128)}), f32[128,1024]{1,0:T(8,128)}) %reduce-scatter.18.cloned.1.call-update) | async-done | bytes 524304 | tf_op jit(solution)/shard_map/reduce_scatter | solution.py:334
  2984.9 158.3 %reduce-scatter.12.cloned.1.call-done = f32[32,3072]{1,0:T(8,128)} async-done(((f32[1024,3072]{1,0:T(8,128)}), f32[32,3072]{1,0:T(8,128)}) %reduce-scatter.12.cloned.1.call-update) | async-done | bytes 393232 | tf_op jit(solution)/shard_map/reduce_scatter | solution.py:331
  3147.5 247.7 %reduce-scatter.20.cloned.1.call-done = f32[32,6144]{1,0:T(8,128)} async-done(((f32[1024,6144]{1,0:T(8,128)}), f32[32,6144]{1,0:T(8,128)}) %reduce-scatter.20.cloned.1.call-update) | async-done | bytes 786448 | tf_op jit(solution)/shard_map/reduce_scatter | solution.py:335
  3404.2 40.2 %psum.7 = f32[]{:T(128)} all-reduce(f32[]{:T(128)S(6)} %add.439), channel_id=1, replica_groups=mesh['clip'=4,'seq'=8] {'clip','seq'}, use_global_device_ids=true, to_apply=%region_39.40 | all-reduce | flops 1 | bytes 8 | tf_op jit(solution)/shard_map/psum | solution.py:339
  (370 shorter events, 1016.0 us)
Async XLA Ops:
  7.2 50.9 %copy-start.4 = (bf16[2,512,1024]{2,1,0:T(8,128)(2,1)S(1)}, bf16[2,512,1024]{2,1,0:T(8,128)(2,1)}, u32[]{:S(2)}) copy-start(bf16[2,512,1024]{2,1,0:T(8,128)(2,1)} %param.28) | copy-start | bytes 6291460
  7.2 76.7 %all-gather.11.cloned.1.call-start = ((), (), s32[]{:S(2)}) async-start(), calls=%async_computation.8 | async-start | bytes 6488064 | tf_op jit(solution)/shard_map/all_gather | solution.py:149
  9.1 172.8 %all-gather.9.cloned.1.call-start = ((), (), s32[]{:S(2)}) async-start(), calls=%async_computation.7 | async-start | bytes 12976128 | tf_op jit(solution)/shard_map/all_gather | solution.py:153
  11.1 250.1 %all-gather.19.cloned.1.call-start = ((), (), s32[]{:S(2)}) async-start(), calls=%async_computation.12 | async-start | bytes 8650752 | tf_op jit(solution)/shard_map/all_gather | solution.py:152
  13.0 476.5 %all-gather.13.cloned.1.call-start = ((), (), s32[]{:S(2)}) async-start(), calls=%async_computation.9 | async-start | bytes 18874368 | tf_op jit(solution)/shard_map/all_gather | solution.py:187
  58.5 130.0 %copy-start.57 = (f32[2,512]{1,0:T(2,128)}, f32[2,512]{1,0:T(2,128)S(1)}, u32[]{:S(2)}) copy-start(f32[2,512]{1,0:T(2,128)S(1)} %broadcast_multiply_fusion.7) | copy-start | bytes 12292
  59.9 122.0 %copy-start.48 = (f32[4,512]{1,0:T(4,128)}, f32[4,512]{1,0:T(4,128)S(1)}, u32[]{:S(2)}) copy-start(f32[4,512]{1,0:T(4,128)S(1)} %get-tuple-element.651) | copy-start | bytes 24580
  59.9 122.0 %copy-start.50 = (f32[4,512]{1,0:T(4,128)}, f32[4,512]{1,0:T(4,128)S(1)}, u32[]{:S(2)}) copy-start(f32[4,512]{1,0:T(4,128)S(1)} %get-tuple-element.652) | copy-start | bytes 24580
  61.2 144.6 %copy-start.28 = (f32[2,512,32]{1,2,0:T(8,128)}, f32[2,512,32]{1,2,0:T(8,128)S(1)}, u32[]{:S(2)}) copy-start(f32[2,512,32]{1,2,0:T(8,128)S(1)} %get-tuple-element.646) | copy-start | bytes 393220
  209.8 512.8 %all-gather.21.cloned.1.call-start = ((), (), s32[]{:S(2)}) async-start(), calls=%async_computation.20 | async-start | bytes 18874368 | tf_op jit(solution)/shard_map/all_gather | solution.py:188
  213.9 625.3 %all-gather.15.cloned.1.call-start = ((), (), s32[]{:S(2)}) async-start(), calls=%async_computation.10 | async-start | bytes 2162688 | tf_op jit(solution)/shard_map/all_gather | solution.py:150
  214.6 642.5 %all-gather.17.cloned.1.call-start = ((), (), s32[]{:S(2)}) async-start(), calls=%async_computation.11 | async-start | bytes 8650752 | tf_op jit(solution)/shard_map/all_gather | solution.py:151
  216.5 1616.7 %reduce-scatter.8.cloned.1.call-start = ((), (), s32[]{:S(2)}) async-start(), calls=%async_computation.13 | async-start | bytes 18874368 | tf_op jit(solution)/shard_map/reduce_scatter | solution.py:296
  1552.0 567.1 %reduce-scatter.10.cloned.1.call-start = ((), (), s32[]{:S(2)}) async-start(), calls=%async_computation.14 | async-start | bytes 18874368 | tf_op jit(solution)/shard_map/reduce_scatter | solution.py:299
  1552.8 711.3 %reduce-scatter.14.cloned.1.call-start = ((), (), s32[]{:S(2)}) async-start(), calls=%async_computation.16 | async-start | bytes 4325376 | tf_op jit(solution)/shard_map/reduce_scatter | solution.py:332
  1560.8 1062.2 %reduce-scatter.16.cloned.1.call-start = ((), (), s32[]{:S(2)}) async-start(), calls=%async_computation.17 | async-start | bytes 17301504 | tf_op jit(solution)/shard_map/reduce_scatter | solution.py:333
  1576.9 1405.6 %reduce-scatter.18.cloned.1.call-start = ((), (), s32[]{:S(2)}) async-start(), calls=%async_computation.18 | async-start | bytes 17301504 | tf_op jit(solution)/shard_map/reduce_scatter | solution.py:334
  1597.1 1546.1 %reduce-scatter.12.cloned.1.call-start = ((), (), s32[]{:S(2)}) async-start(), calls=%async_computation.15 | async-start | bytes 12976128 | tf_op jit(solution)/shard_map/reduce_scatter | solution.py:331
  1597.7 583.9 %copy-start.59 = (f32[2,2,256]{2,1,0:T(2,128)}, f32[2,2,256]{2,1,0:T(2,128)S(1)}, u32[]{:S(2)}) copy-start(f32[2,2,256]{2,1,0:T(2,128)S(1)} %div.169) | copy-start | bytes 12292
  1602.8 232.8 %copy-start.29 = (f32[2,512,32]{1,2,0:T(8,128)S(1)}, f32[2,512,32]{1,2,0:T(8,128)}, u32[]{:S(2)}) copy-start(f32[2,512,32]{1,2,0:T(8,128)} %copy-done.28) | copy-start | bytes 393220
  1602.8 232.8 %copy-start.32 = (f32[2,512,32]{1,2,0:T(8,128)S(1)}, f32[2,512,32]{1,2,0:T(8,128)}, u32[]{:S(2)}) copy-start(f32[2,512,32]{1,2,0:T(8,128)} %get-tuple-element.644) | copy-start | bytes 393220
  2195.2 1200.0 %reduce-scatter.20.cloned.1.call-start = ((), (), s32[]{:S(2)}) async-start(), calls=%async_computation.19 | async-start | bytes 25952256 | tf_op jit(solution)/shard_map/reduce_scatter | solution.py:335
  2314.1 1083.7 %copy-start.62 = (f32[6144]{0:T(1024)}, f32[6144]{0:T(1024)S(1)}, u32[]{:S(2)}) copy-start(f32[6144]{0:T(1024)S(1)} %all-reduce.1) | copy-start | bytes 73732
  3398.4 48.1 %copy-start.38 = (f32[32,1024]{1,0:T(8,128)S(1)}, f32[32,1024]{1,0:T(8,128)}, u32[]{:S(2)}) copy-start(f32[32,1024]{1,0:T(8,128)} %param.33) | copy-start | bytes 393220
  3398.4 48.1 %copy-start.39 = (f32[32,1024]{1,0:T(8,128)S(1)}, f32[32,1024]{1,0:T(8,128)}, u32[]{:S(2)}) copy-start(f32[32,1024]{1,0:T(8,128)} %reduce-scatter.14.cloned.1.call-done) | copy-start | bytes 393220
  3398.4 50.1 %copy-start.26 = (f32[32,3072]{1,0:T(8,128)S(1)}, f32[32,3072]{1,0:T(8,128)}, u32[]{:S(2)}) copy-start(f32[32,3072]{1,0:T(8,128)} %param.32) | copy-start | bytes 1179652
  3398.5 50.1 %copy-start.27 = (f32[32,3072]{1,0:T(8,128)S(1)}, f32[32,3072]{1,0:T(8,128)}, u32[]{:S(2)}) copy-start(f32[32,3072]{1,0:T(8,128)} %reduce-scatter.12.cloned.1.call-done) | copy-start | bytes 1179652
  3398.5 50.1 %copy-start.41 = (f32[32,3072]{1,0:T(8,128)S(1)}, f32[32,3072]{1,0:T(8,128)}, u32[]{:S(2)}) copy-start(f32[32,3072]{1,0:T(8,128)} %param.44) | copy-start | bytes 1179652
  3404.2 46.6 %copy-start.20 = (f32[128,1024]{1,0:T(8,128)S(1)}, f32[128,1024]{1,0:T(8,128)}, u32[]{:S(2)}) copy-start(f32[128,1024]{1,0:T(8,128)} %param.35) | copy-start | bytes 1572868
  3404.2 46.6 %copy-start.23 = (f32[128,1024]{1,0:T(8,128)S(1)}, f32[128,1024]{1,0:T(8,128)}, u32[]{:S(2)}) copy-start(f32[128,1024]{1,0:T(8,128)} %reduce-scatter.18.cloned.1.call-done) | copy-start | bytes 1572868
  3404.2 46.6 %copy-start.33 = (f32[128,1024]{1,0:T(8,128)S(1)}, f32[128,1024]{1,0:T(8,128)}, u32[]{:S(2)}) copy-start(f32[128,1024]{1,0:T(8,128)} %param.47) | copy-start | bytes 1572868
  3404.2 46.6 %copy-start.34 = (f32[128,1024]{1,0:T(8,128)S(1)}, f32[128,1024]{1,0:T(8,128)}, u32[]{:S(2)}) copy-start(f32[128,1024]{1,0:T(8,128)} %param.41) | copy-start | bytes 1572868
  (55 other events, 353.2 us)
Sparse Core Ops, SparseCore 0:
  11.5 72.3 all-gather.10
  87.4 94.4 all-gather.8
  185.5 75.6 all-gather.18
  263.1 226.3 all-gather.12
  492.0 225.9 all-gather.20
  721.3 54.6 all-gather.14
  779.6 76.2 all-gather.16
  1552.2 281.0 reduce-scatter.7
  1837.5 281.6 reduce-scatter.9
  2121.3 142.6 reduce-scatter.13
  2266.3 356.5 reduce-scatter.15
  2625.1 357.3 reduce-scatter.17
  2988.6 154.5 reduce-scatter.11
  3150.6 244.5 reduce-scatter.19
where the time goes:
time: 3480 us; the launch traced here: 3460 us
  waiting for transfers between devices  2000 us (57%)
  matrix products  995 us (29%)
  other arithmetic  204 us (6%)
  blocking collectives  131 us (4%)
  local copies, waits for them, and re-layouts  108 us (3%)
    reduce_scatter x1, waiting for transfers between devices, per_device(): lax.psum_scatter(down_grad, ('clip', 'seq'), scatter_dimension=0, tiled=T...  358 us
    reduce_scatter x1, waiting for transfers between devices, per_device(): lax.psum_scatter(up_grad, ('clip', 'seq'), scatter_dimension=0, tiled=True)  308 us
    reduce_scatter x1, waiting for transfers between devices, per_device(): lax.psum_scatter(value_grads.astype(jnp.bfloat16), 'seq', scatter_dimensi...  280 us
    reduce_scatter x1, waiting for transfers between devices, per_device(): lax.psum_scatter(mod_grad, ('clip', 'seq'), scatter_dimension=0, tiled=True)  248 us
    dot_general x16, matrix products, score_block(): jnp.einsum('cqhe,ckhe->chqk', query_rows, key_rows, preferred_element_typ...  244 us
    reduce_scatter x1, waiting for transfers between devices, per_device(): lax.psum_scatter(key_grads.astype(jnp.bfloat16), 'seq', scatter_dimension...  230 us
    all_gather x1, waiting for transfers between devices, per_device(): lax.all_gather(own_keys, 'seq', axis=1, tiled=True)  212 us
    dot_general x8, matrix products, grad_step(): jnp.einsum('cqhe,ckhe->chqk', outer_grad, values_here, preferred_element_...  164 us
  transfers between devices with their start and end apart: 14, of which 11 were waited for; matrix products, arithmetic and copies ran while one was open for 17% of the time, Pallas kernels for 0%

commit v1 on v0

v1 whole, which is shorter than its diff:
```python
from functools import partial
import math

import jax
import jax.numpy as jnp
from jax import lax
from jax.experimental import pallas as pl
from jax.experimental.pallas import tpu as pltpu
from jax.sharding import PartitionSpec as P

D = 1024
HEADS = 16
HEAD = 64
FF = 4096
FRAMES = 16
GRID_W = 16
STEP = 10
PATCHES = 256
LENGTH = 4096

norm_epsilon = 1e-06
adam_epsilon = 1e-08
first_decay = 0.5
second_decay = 0.5
weight_decay = 0.1
clip_limit = 1.0
highest = lax.Precision.HIGHEST
AXES = ("clip", "seq")
LOW = jnp.bfloat16
WIDE = jnp.float32
SOFT = math.log2(math.e) * HEAD ** (-0.5)


def dot(left, right):
    return jnp.dot(left, right, preferred_element_type=WIDE)


def contract(left, right, left_dim, right_dim):
    return lax.dot_general(
        left, right, (((left_dim,), (right_dim,)), ((), ())), preferred_element_type=WIDE
    )


def normalize(operand):
    centered = operand - jnp.mean(operand, axis=-1, keepdims=True)
    variance = jnp.mean(centered * centered, axis=-1, keepdims=True)
    return centered * lax.rsqrt(variance + norm_epsilon)


def modulate(operand, shift_by, scale_by):
    return normalize(operand) * (1.0 + scale_by) + shift_by


def adam_update(gradient, master, moment_one, moment_two, step_rate):
    moment_one = first_decay * moment_one + (1.0 - first_decay) * gradient
    moment_two = second_decay * moment_two + (1.0 - second_decay) * gradient * gradient
    corrected_one = moment_one / (1.0 - first_decay**STEP)
    corrected_two = moment_two / (1.0 - second_decay**STEP)
    master = master - step_rate * (
        corrected_one / (jnp.sqrt(corrected_two) + adam_epsilon) + weight_decay * master
    )
    return (moment_one, moment_two, master)


def rotary_tables(times, places):
    frame_ids = places // PATCHES
    patch_row = (places % PATCHES // GRID_W).astype(WIDE)
    column = (places % GRID_W).astype(WIDE)
    matches = frame_ids[None, :] == jnp.arange(FRAMES, dtype=jnp.int32)[:, None]
    moment = jnp.sum(jnp.where(matches, times[:, None], 0), axis=0).astype(WIDE)
    time_pairs = HEAD // 8
    grid_pairs = 3 * HEAD // 16
    pair_ids = jnp.arange(HEAD // 2, dtype=jnp.int32)
    second = time_pairs + grid_pairs
    offset = jnp.where(pair_ids < time_pairs, 0, jnp.where(pair_ids < second, time_pairs, second))
    length = jnp.where(pair_ids < time_pairs, time_pairs, grid_pairs)
    frequency = jnp.exp(
        -math.log(10000.0) * (pair_ids - offset).astype(WIDE) / length.astype(WIDE)
    )
    ids = pair_ids[:, None]
    coordinate = jnp.where(
        ids < time_pairs, moment[None], jnp.where(ids < second, patch_row[None], column[None])
    )
    angles = coordinate * frequency[:, None]
    return jnp.cos(angles), jnp.sin(angles)


def project_kernel(pick, rows_ref, weight_ref, cos_ref, sin_ref, out_ref):
    turned = dot(rows_ref[...], weight_ref[...]).T
    group = pl.program_id(0)
    half = HEAD // 2

    @pl.when(group == 2)
    def _():
        out_ref[0] = turned.astype(LOW)

    @pl.when(group < 2)
    def _():
        cosines, sines = cos_ref[...], sin_ref[...]
        for head in range(turned.shape[0] // HEAD):
            start = head * HEAD
            one = turned[start : start + half]
            two = turned[start + half : start + HEAD]
            out_ref[0, start : start + half, :] = (one * cosines - two * sines).astype(LOW)
            out_ref[0, start + half : start + HEAD, :] = (two * cosines + one * sines).astype(LOW)


def project(pick, rows, weight, cosines, sines, members):
    tokens, width = rows.shape
    columns = D // members
    return pl.pallas_call(
        project_kernel,
        grid_spec=pltpu.PrefetchScalarGridSpec(
            num_scalar_prefetch=1,
            grid=(3,),
            in_specs=[
                pl.BlockSpec((tokens, width), lambda g, pick: (0, 0)),
                pl.BlockSpec((width, columns), lambda g, pick: (0, g * members + pick[0])),
                pl.BlockSpec((HEAD // 2, tokens), lambda g, pick: (0, 0)),
                pl.BlockSpec((HEAD // 2, tokens), lambda g, pick: (0, 0)),
            ],
            out_specs=pl.BlockSpec((1, columns, tokens), lambda g, pick: (g, 0, 0)),
        ),
        out_shape=jax.ShapeDtypeStruct((3, columns, tokens), LOW),
        compiler_params=pltpu.CompilerParams(vmem_limit_bytes=40 << 20),
        cost_estimate=pl.CostEstimate(
            flops=6 * tokens * width * columns,
            bytes_accessed=2 * (tokens * width + 3 * width * columns + 3 * tokens * columns),
            transcendentals=0,
        ),
        name="project",
    )(pick, rows, weight, cosines, sines)


def pick_rows(refs, step, per, size, target, index):
    start = 0 if per == 1 else pl.multiple_of(step % per * size, size)
    for member, ref in enumerate(refs):

        @pl.when(step // per == member)
        def _(ref=ref):
            target[...] = ref[index, :, pl.ds(start, size)]


def attend_kernel(*refs, members, tokens, size, block):
    parts = refs[:members]
    low_refs = refs[members : 2 * members]
    wide_ref, total_ref, key_rows, query_rows = refs[2 * members :]
    step = pl.program_id(1)
    per = tokens // size
    length = members * tokens

    @pl.when(step == 0)
    def _():
        for member in range(members):
            key_rows[member * tokens : (member + 1) * tokens, :] = parts[member][1].T

    pick_rows(parts, step, per, size, query_rows, 0)
    queries = query_rows[...]
    count = length // block
    inside = tokens // block
    gathered = jnp.zeros((HEAD, size), WIDE)
    highest_score = jnp.full((1, size), -1e30, WIDE)
    total = jnp.zeros((1, size), WIDE)
    following = dot(key_rows[0:block, :], queries)
    for number in range(count):
        scores = following
        if number + 1 < count:
            following = dot(key_rows[(number + 1) * block : (number + 2) * block, :], queries)
        raised = jnp.maximum(highest_score, jnp.max(scores, axis=0, keepdims=True))
        shrink = jnp.exp2((highest_score - raised) * SOFT)
        probs = jnp.exp2(scores * SOFT - raised * SOFT)
        total = total * shrink + jnp.sum(probs, axis=0, keepdims=True)
        start = number % inside * block
        values = parts[number // inside][2, :, start : start + block]
        gathered = gathered * shrink + dot(values, probs.astype(LOW))
        highest_score = raised
    attended = gathered / total
    wide_ref[...] = attended
    total_ref[0] = highest_score * SOFT + jnp.log2(total)
    low = attended.astype(LOW)
    start = 0 if per == 1 else pl.multiple_of(step % per * size, size)
    for member in range(members):

        @pl.when(step // per == member)
        def _(member=member):
            low_refs[member][:, pl.ds(start, size)] = low


def attend(parts):
    members = len(parts)
    _, rows, tokens = parts[0].shape
    heads = rows // HEAD
    size, block = min(1024, tokens), min(512, tokens)
    length = members * tokens
    part = pl.BlockSpec((3, HEAD, tokens), lambda h, i: (0, h, 0))
    return pl.pallas_call(
        partial(attend_kernel, members=members, tokens=tokens, size=size, block=block),
        grid=(heads, length // size),
        in_specs=[part] * members,
        out_specs=[pl.BlockSpec((HEAD, tokens), lambda h, i: (h, 0))] * members
        + [
            pl.BlockSpec((HEAD, size), lambda h, i: (h, i)),
            pl.BlockSpec((1, 1, size), lambda h, i: (h, 0, i)),
        ],
        out_shape=[jax.ShapeDtypeStruct((rows, tokens), LOW)] * members
        + [
            jax.ShapeDtypeStruct((rows, length), WIDE),
            jax.ShapeDtypeStruct((heads, 1, length), WIDE),
        ],
        scratch_shapes=[pltpu.VMEM((length, HEAD), LOW), pltpu.VMEM((HEAD, size), LOW)],
        compiler_params=pltpu.CompilerParams(vmem_limit_bytes=48 << 20),
        cost_estimate=pl.CostEstimate(
            flops=16 * heads * length * length * HEAD,
            bytes_accessed=8 * rows * length,
            transcendentals=heads * length * length,
        ),
        name="attend",
    )(*parts)


def turn_back(operand, cosines, sines):
    half = HEAD // 2
    one, two = operand[:half], operand[half:]
    return jnp.concatenate([one * cosines + two * sines, two * cosines - one * sines], axis=0)


def attend_back_kernel(*refs, members, tokens, size, block):
    parts = refs[:members]
    grads = refs[members : 2 * members]
    wide_ref, total_ref, cos_ref, sin_ref = refs[2 * members : 2 * members + 4]
    outs = refs[2 * members + 4 : 3 * members + 4]
    key_rows, query_columns, grad_columns, key_sum, value_sum = refs[3 * members + 4 :]
    step = pl.program_id(1)
    per = tokens // size
    length = members * tokens
    count = length // block
    inside = tokens // block
    back = HEAD ** (-0.5)

    @pl.when(step == 0)
    def _():
        for member in range(members):
            key_rows[member * tokens : (member + 1) * tokens, :] = parts[member][1].T
        key_sum[...] = jnp.zeros_like(key_sum)
        value_sum[...] = jnp.zeros_like(value_sum)

    pick_rows(parts, step, per, size, query_columns, 0)
    start = 0 if per == 1 else pl.multiple_of(step % per * size, size)
    for member in range(members):

        @pl.when(step // per == member)
        def _(member=member):
            grad_columns[...] = grads[member][:, pl.ds(start, size)]

    queries_across = query_columns[...]
    grads_across = grad_columns[...]
    queries = queries_across.T
    out_grads = grads_across.T
    delta = jnp.sum(grads_across.astype(WIDE) * wide_ref[...], axis=0, keepdims=True).T
    total = total_ref[0].T
    query_grad = jnp.zeros((size, HEAD), WIDE)

    def pair(number):
        member, at = number // inside, number % inside * block
        return (
            dot(queries, parts[member][1, :, at : at + block]),
            dot(out_grads, parts[member][2, :, at : at + block]),
        )

    following = pair(0)
    for number in range(count):
        scores, prob_grad = following
        if number + 1 < count:
            following = pair(number + 1)
        here = slice(number * block, (number + 1) * block)
        probs = jnp.exp2(scores * SOFT - total)
        score_grad = (probs * (prob_grad - delta)).astype(LOW)
        value_sum[:, here] += dot(grads_across, probs.astype(LOW))
        key_sum[:, here] += dot(queries_across, score_grad)
        query_grad += dot(score_grad, key_rows[here, :])

    where = pl.multiple_of(step * size, size)
    turned = turn_back(
        query_grad.T * back, cos_ref[:, pl.ds(where, size)], sin_ref[:, pl.ds(where, size)]
    ).astype(LOW)
    for member in range(members):

        @pl.when(step // per == member)
        def _(member=member):
            outs[member][0, :, pl.ds(start, size)] = turned

    @pl.when(step == length // size - 1)
    def _():
        for member in range(members):
            span = slice(member * tokens, (member + 1) * tokens)
            outs[member][1] = turn_back(
                key_sum[:, span] * back, cos_ref[:, span], sin_ref[:, span]
            ).astype(LOW)
            outs[member][2] = value_sum[:, span].astype(LOW)


def attend_back(parts, grads, wide, total, cosines, sines):
    members = len(parts)
    _, rows, tokens = parts[0].shape
    heads = rows // HEAD
    size, block = min(1024, tokens), min(512, tokens)
    length = members * tokens
    part = pl.BlockSpec((3, HEAD, tokens), lambda h, i: (0, h, 0))
    table = pl.BlockSpec((HEAD // 2, length), lambda h, i: (0, 0))
    return pl.pallas_call(
        partial(attend_back_kernel, members=members, tokens=tokens, size=size, block=block),
        grid=(heads, length // size),
        in_specs=[part] * members
        + [pl.BlockSpec((HEAD, tokens), lambda h, i: (h, 0))] * members
        + [
            pl.BlockSpec((HEAD, size), lambda h, i: (h, i)),
            pl.BlockSpec((1, 1, size), lambda h, i: (h, 0, i)),
            table,
            table,
        ],
        out_specs=[part] * members,
        out_shape=[jax.ShapeDtypeStruct((3, rows, tokens), LOW)] * members,
        scratch_shapes=[
            pltpu.VMEM((length, HEAD), LOW),
            pltpu.VMEM((HEAD, size), LOW),
            pltpu.VMEM((HEAD, size), LOW),
            pltpu.VMEM((HEAD, length), WIDE),
            pltpu.VMEM((HEAD, length), WIDE),
        ],
        compiler_params=pltpu.CompilerParams(vmem_limit_bytes=56 << 20),
        cost_estimate=pl.CostEstimate(
            flops=40 * heads * length * length * HEAD,
            bytes_accessed=16 * rows * length,
            transcendentals=heads * length * length,
        ),
        name="attend_back",
    )(*parts, *grads, wide, total, cosines, sines)


def per_device(
    clip_size,
    seq_size,
    frames_in,
    noise_level,
    frame_time,
    cotangent,
    joint_weight,
    output_weight,
    up_weight,
    down_weight,
    modulation,
    modulation_bias,
    first_joint,
    first_output,
    first_up,
    first_down,
    first_modulation,
    first_bias,
    second_joint,
    second_output,
    second_up,
    second_down,
    second_modulation,
    second_bias,
):
    total_devices = clip_size * seq_size
    masters = (joint_weight, output_weight, up_weight, down_weight, modulation, modulation_bias)
    firsts = (first_joint, first_output, first_up, first_down, first_modulation, first_bias)
    seconds = (second_joint, second_output, second_up, second_down, second_modulation, second_bias)
    clip_id, seq_id = lax.axis_index("clip"), lax.axis_index("seq")
    rank = clip_id * seq_size + seq_id
    half = seq_size // 2
    side = seq_id // half
    place = seq_id % half
    members = half

    def swap_with(value, mask):
        return lax.ppermute(value, AXES, [(i, i ^ mask) for i in range(total_devices)])

    def pick(value, index):
        return lax.dynamic_index_in_dim(value, index, 0, keepdims=False)

    core_mask = seq_size
    clip_masks = [seq_size << bit for bit in range(clip_size.bit_length() - 1)]
    seq_masks = [1 << bit for bit in range(seq_size.bit_length() - 1)]
    order = clip_masks + seq_masks

    joint_full, output_full, upward, downward = (
        lax.all_gather(weight.astype(LOW), AXES, axis=0, tiled=True) for weight in masters[:4]
    )

    local_rows = frames_in.shape[1]
    frame_count = max(1, local_rows // PATCHES)
    per_frame = local_rows // frame_count
    tokens_here = 2 * local_rows

    def to_one_clip(value):
        return jnp.stack([pick(value, side), swap_with(pick(value, 1 - side), half)])

    def to_two_clips(own, others):
        arrived = swap_with(others, half)
        return jnp.where(side == 0, jnp.stack([own, arrived]), jnp.stack([arrived, own]))

    tokens_low = to_one_clip(frames_in)
    upstream_low = to_one_clip(cotangent)
    shape = (2, frame_count, per_frame, D)
    tokens = tokens_low.astype(WIDE).reshape(shape)

    levels = noise_level.astype(WIDE)
    levels_of = [levels]
    for mask in clip_masks:
        levels_of = levels_of + [swap_with(jnp.stack(levels_of), mask)[i] for i in range(len(levels_of))]
    all_levels = jnp.concatenate(levels_of, axis=0).reshape(-1)
    masks = [0]
    for mask in reversed(order):
        masks = masks + [other ^ mask for other in masks]
    masks = jnp.array(masks, jnp.int32)
    seq_of = seq_id ^ (masks % seq_size)
    chunk = jnp.stack([seq_of, seq_of ^ half], axis=1)
    frame_of = (
        chunk[:, :, None] * local_rows // PATCHES + jnp.arange(frame_count, dtype=jnp.int32)
    )
    clip_of = masks // seq_size * 2 + seq_of // half
    level_ids = (clip_of[:, None, None] * FRAMES + frame_of).reshape(-1)
    level_of = jnp.sum(
        jnp.where(
            level_ids[:, None] == jnp.arange(all_levels.shape[0], dtype=jnp.int32), all_levels, 0.0
        ),
        axis=1,
    )
    own_width = modulation.shape[0]
    columns = rank * own_width + jnp.arange(own_width, dtype=jnp.int32)
    half_width = D // 2
    frequency = jnp.exp(-math.log(10000.0) * (columns % half_width).astype(WIDE) / half_width)
    angles = level_of[:, None] * frequency
    wave = jnp.where(columns < half_width, jnp.cos(angles), jnp.sin(angles))
    condition = jax.nn.silu(wave).astype(LOW)

    bias_width = modulation_bias.shape[0]
    bias_row = lax.dynamic_update_slice_in_dim(
        jnp.zeros((6 * D,), WIDE), modulation_bias.astype(LOW).astype(WIDE), rank * bias_width, 0
    )
    modulation_low = modulation.astype(LOW)

    def modulated_part(first, last):
        terms = dot(condition, modulation_low[:, first:last]) + bias_row[first:last]
        for mask in order:
            middle = terms.shape[0] // 2
            terms = terms[:middle] + swap_with(terms[middle:], mask)
        return terms.reshape(2, frame_count, 1, last - first)

    early = modulated_part(0, 2 * D)
    shift_one, scale_one = early[..., :D], early[..., D:]
    late = modulated_part(2 * D, 6 * D)
    gate_one, shift_two, scale_two, gate_two = (
        late[..., i * D : (i + 1) * D] for i in range(4)
    )

    member_seq = seq_id ^ jnp.arange(members, dtype=jnp.int32)
    starts = jnp.stack([member_seq, member_seq ^ half], axis=1) * local_rows
    places = (starts[:, :, None] + jnp.arange(local_rows, dtype=jnp.int32)).reshape(-1)
    cosines, sines = rotary_tables(pick(frame_time, side), places)

    normed_one_low = modulate(tokens, shift_one, scale_one).astype(LOW).reshape(tokens_here, D)
    own_tables = cosines[:, :tokens_here], sines[:, :tokens_here]

    def group_of(member):
        return (place ^ member).astype(jnp.int32).reshape(1)

    def project_group(member):
        if D // members % 128 == 0:
            return project(group_of(member), normed_one_low, joint_full, *own_tables, members)
        wide = [
            project(jnp.full((1,), i, jnp.int32), normed_one_low, joint_full, *own_tables, 4)
            for i in range(4)
        ]
        every = jnp.concatenate(wide, axis=1).reshape(3, members, D // members, tokens_here)
        return lax.dynamic_index_in_dim(every, place ^ member, 1, keepdims=False)

    parts = [None] * members
    for member in list(range(1, members)) + [0]:
        part = project_group(member)
        parts[member] = swap_with(part, member) if member else part
    *attended_parts, attended_wide, totals = attend(parts)

    def by_head(values):
        lead = values[0].shape[:-2]
        result = jnp.zeros(lead + (members,) + values[0].shape[-2:], values[0].dtype)
        for member, value in enumerate(values):
            result = lax.dynamic_update_slice_in_dim(
                result, jnp.expand_dims(value, -3), place ^ member, len(lead)
            )
        return result.reshape(-1, values[0].shape[-1])

    attended_across = by_head(
        [swap_with(value, member) if member else value for member, value in enumerate(attended_parts)]
    )
    projected = contract(attended_across, output_full, 0, 0).reshape(shape)
    middle = tokens + gate_one * projected
    normed_two_low = modulate(middle, shift_two, scale_two).astype(LOW).reshape(tokens_here, D)
    upper_out = dot(normed_two_low, upward)
    hidden_low = jax.nn.gelu(upper_out, approximate=True).astype(LOW)
    branch = dot(hidden_low, downward).reshape(shape)
    result = (middle + gate_two * branch).astype(LOW).reshape(2, local_rows, D)
    mixed = to_two_clips(result[0], result[1])

    def scatter_rows(gradient, masks):
        rows, width = gradient.shape
        bits = total_devices.bit_length() - 1
        value = gradient.reshape((2,) * bits + (rows // total_devices, width))
        left = list(range(bits - 1, -1, -1))
        for mask in masks:
            bit = mask.bit_length() - 1
            axis = left.index(bit)
            left.pop(axis)
            mine = rank // mask % 2
            sent = lax.dynamic_index_in_dim(value, 1 - mine, axis, keepdims=False).astype(LOW)
            kept = lax.dynamic_index_in_dim(value, mine, axis, keepdims=False)
            value = kept + swap_with(sent, mask).astype(WIDE)
        return value

    first_order = clip_masks + seq_masks
    second_order = [core_mask] + seq_masks[:1] + clip_masks[1:] + seq_masks[1:]

    def scatter(gradient):
        width = gradient.shape[1] // 2
        return jnp.concatenate(
            [
                scatter_rows(gradient[:, :width], first_order),
                scatter_rows(gradient[:, width:], second_order),
            ],
            axis=1,
        )

    upstream = upstream_low.astype(WIDE).reshape(shape)
    gate_two_grad = jnp.sum(upstream * branch, axis=2)
    branch_grad = (gate_two * upstream).astype(LOW).reshape(tokens_here, D)
    down_sum = scatter(contract(hidden_low, branch_grad, 0, 0))
    hidden_grad = contract(branch_grad, downward, 1, 1)
    gelu_pull = jax.vjp(partial(jax.nn.gelu, approximate=True), upper_out)[1]
    upper_grad = gelu_pull(hidden_grad)[0].astype(LOW)
    up_sum = scatter(contract(normed_two_low, upper_grad, 0, 0))
    normed_two_grad = contract(upper_grad, upward, 1, 1).reshape(shape)
    middle_pull = jax.vjp(modulate, middle, shift_two, scale_two)[1]
    middle_grad, shift_two_grad, scale_two_grad = middle_pull(normed_two_grad)
    middle_grad = middle_grad + upstream
    gate_one_grad = jnp.sum(middle_grad * projected, axis=2)
    projected_grad = (gate_one * middle_grad).astype(LOW).reshape(tokens_here, D)
    outer_across = contract(output_full, projected_grad, 1, 1).astype(LOW)
    outer_across = outer_across.reshape(members, D // members, tokens_here)
    outer_parts = []
    for member in range(members):
        outer = pick(outer_across, place ^ member)
        outer_parts.append(swap_with(outer, member) if member else outer)
    output_sum = scatter(dot(attended_across, projected_grad))

    def gather_frames(value):
        for mask in reversed(order):
            value = jnp.concatenate([value, swap_with(value, mask)], axis=0)
        return value

    def piece_rows(*pieces):
        return jnp.concatenate(
            [piece.reshape(2 * frame_count, D) for piece in pieces], axis=1
        )

    late_pieces = gather_frames(
        piece_rows(gate_one_grad, shift_two_grad, scale_two_grad, gate_two_grad)
    )
    joint_parts = attend_back(parts, outer_parts, attended_wide, totals, cosines, sines)
    joint_across = by_head(
        [swap_with(value, member) if member else value for member, value in enumerate(joint_parts)]
    )
    joint_sum = scatter(contract(normed_one_low, joint_across, 0, 1))
    normed_one_grad = contract(joint_across, joint_full, 0, 1).reshape(shape)
    tokens_pull = jax.vjp(modulate, tokens, shift_one, scale_one)[1]
    token_grad, shift_one_grad, scale_one_grad = tokens_pull(normed_one_grad)
    input_rows = (token_grad + middle_grad).reshape(2, local_rows, D)
    input_grad = to_two_clips(input_rows[0], input_rows[1].astype(LOW)).astype(WIDE)
    early_pieces = gather_frames(piece_rows(shift_one_grad, scale_one_grad))

    pieces = jnp.concatenate([early_pieces, late_pieces], axis=1)
    mod_sum = lax.dot_general(
        condition.astype(WIDE), pieces, (((0,), (0,)), ((), ())), precision=highest
    )
    bias_sum = lax.dynamic_slice_in_dim(
        jnp.sum(pieces, axis=0), rank * bias_width, bias_width, 0
    )

    summed = (joint_sum, output_sum, up_sum, down_sum, mod_sum, bias_sum)
    squares = sum(jnp.sum(shard * shard) for shard in summed).reshape(1, 1)
    for group in (
        [i * seq_size for i in range(1, clip_size)],
        list(range(1, seq_size)),
    ):
        squares = squares + sum(swap_with(squares, mask) for mask in group)
    grad_norm = jnp.sqrt(squares[0, 0])
    factor = jnp.minimum(1.0, clip_limit / (grad_norm + 1e-06))
    step_rates = (
        D ** (-0.5),
        max(1, 2 * D // LENGTH) ** (-0.5),
        D ** (-0.5),
        FF ** (-0.5),
        D ** (-0.5),
        0.5,
    )
    clipped = [shard * factor for shard in summed]
    updates = [
        adam_update(clipped[slot], masters[slot], firsts[slot], seconds[slot], step_rates[slot])
        for slot in range(6)
    ]
    return (
        mixed,
        input_grad,
        *clipped,
        grad_norm,
        *(update[0] for update in updates),
        *(update[1] for update in updates),
        *(update[2] for update in updates),
        *(update[2].astype(LOW) for update in updates),
    )


def solution(mesh):
    tokens = P("clip", "seq", None)
    rows = P(AXES, None)
    weights = (rows, rows, rows, rows, rows, P(AXES))
    in_specs = (tokens, P("clip", None), P("clip", None), tokens) + weights * 3
    out_specs = (tokens, tokens) + weights + (P(),) + weights * 4
    return jax.shard_map(
        partial(per_device, mesh.shape["clip"], mesh.shape["seq"]),
        mesh=mesh,
        in_specs=in_specs,
        out_specs=out_specs,
        check_vma=False,
    )
```

time: 3480 us -> 1160 us (0.33)
  waiting for transfers between devices: 2000 us -> 360 us
  matrix products: 995 us -> 144 us
  Pallas kernels: 0 us -> 281 us
  blocking collectives: 131 us -> 0 us
  other arithmetic: 204 us -> 96.1 us
  starting transfers between devices: 1.2 us -> 109 us
    reduce_scatter x7 -> x0, waiting for transfers between devices: 1640 us -> none  [the longest x1 358 us: per_device(): lax.psum_scatter(down_grad, ('clip', 'seq'), scatter_dimension=0, tiled=T...]
    dot_general x70 -> x14, matrix products: 995 us -> 144 us  [the longest x8 102 us: contract(): lax.dot_general(left, right, (((left_dim,), (right_dim,)), ((), ())), pre...]
    all_gather x7 -> x4, waiting for transfers between devices: 365 us -> 4.42 us  [per_device(): lax.all_gather(weight.astype(LOW), AXES, axis=0, tiled=True)]
    ppermute x0 -> x88, waiting for transfers between devices: none -> 356 us  [swap_with(): lax.ppermute(value, AXES, [(i, i ^ mask) for i in range(total_devices)])]
    pallas_call x0 -> x6, Pallas kernels: none -> 281 us  [the longest x1 168 us: attend_back(): pl.pallas_call(partial(attend_back_kernel, members=members, tokens=tokens...]
    reduce_sum x19 -> x9, other arithmetic: 134 us -> 10.2 us  [the longest x1 6.3 us: per_device(): gate_two_grad = jnp.sum(upstream * branch, axis=2)]
    ppermute x0 -> x88, starting transfers between devices: none -> 109 us  [swap_with(): lax.ppermute(value, AXES, [(i, i ^ mask) for i in range(total_devices)])]
    unnamed x2 -> x0, blocking collectives: 90.9 us -> none
  transfers between devices with their start and end apart: 14 -> 92, of which waited for: 11 -> 40; matrix products, arithmetic and copies ran while one was open for 17% -> 23% of each run, Pallas kernels for 0% -> 24%
where the time goes in v1:
time: 1160 us; the launch traced here: 1150 us
  waiting for transfers between devices  360 us (31%)
  Pallas kernels  281 us (24%)
  matrix products  144 us (12%)
  local copies, waits for them, and re-layouts  131 us (11%)
  starting transfers between devices  109 us (9%)
  other arithmetic  96.1 us (8%)
  between operations  27.7 us (2%)
    ppermute x88, waiting for transfers between devices, swap_with(): lax.ppermute(value, AXES, [(i, i ^ mask) for i in range(total_devices)])  356 us
    pallas_call x1, Pallas kernels, attend_back(): pl.pallas_call(partial(attend_back_kernel, members=members, tokens=tokens...  168 us
    ppermute x88, starting transfers between devices, swap_with(): lax.ppermute(value, AXES, [(i, i ^ mask) for i in range(total_devices)])  109 us
    dot_general x8, matrix products, contract(): lax.dot_general(left, right, (((left_dim,), (right_dim,)), ((), ())), pre...  102 us
    pallas_call x1, Pallas kernels, attend(): pl.pallas_call(partial(attend_kernel, members=members, tokens=tokens, siz...  98.4 us
    dot_general x5, matrix products, dot(): return jnp.dot(left, right, preferred_element_type=WIDE)  38.9 us
    slice x4, local copies, waits for them, and re-layouts, scatter(): gradient[:, :width]  33.7 us
    convert_element_type x40, local copies, waits for them, and re-layouts, scatter_rows(): lax.dynamic_index_in_dim(value, 1 - mine, axis, keepdims=False).astype(LOW)  27.7 us
  transfers between devices with their start and end apart: 92, of which 40 were waited for; matrix products, arithmetic and copies ran while one was open for 23% of the time, Pallas kernels for 24%

profile of v1, /device:TPU:0, one launch (start us, length us, event | category | flops | bytes accessed | tf_op | source)
XLA Modules:
  0.0 1149.8 jit_solution(15895379291539125732)
XLA Ops:
  32.1 6.9 collective-permute-done.9
  61.9 24.6 %collective-permute-done.12 = f32[4,2048]{1,0:T(4,128)S(1)} collective-permute-done((f32[4,2048]{1,0:T(4,128)S(1)}, f32[4,2048]{1,0:T(4,128)S(1)}, u32[]{:S(2)}, u32[]{:S(2)}) %collective-permute-start.12) | collective-permute-done | bytes 32800 | tf_op jit(solution)/shard_map/ppermute | solution.py:378
  90.1 21.3 %collective-permute-done.4 = f32[32,4096]{1,0:T(8,128)S(1)} collective-permute-done((f32[32,4096]{1,0:T(8,128)S(1)}, f32[32,4096]{1,0:T(8,128)S(1)}, u32[]{:S(2)}, u32[]{:S(2)}) %collective-permute-start.4) | collective-permute-done | bytes 524320 | tf_op jit(solution)/shard_map/ppermute | solution.py:378
  149.4 64.6 %collective-permute-done.7 = f32[4,4096]{1,0:T(4,128)} collective-permute-done((f32[4,4096]{1,0:T(4,128)}, f32[4,4096]{1,0:T(4,128)}, u32[]{:S(2)}, u32[]{:S(2)}) %collective-permute-start.7) | collective-permute-done | bytes 65568 | tf_op jit(solution)/shard_map/ppermute | solution.py:378
  222.2 14.5 %collective-permute-done.15.refs_3_ = bf16[3,256,1024]{2,1,0:T(8,128)(2,1)} collective-permute-done((bf16[3,256,1024]{2,1,0:T(8,128)(2,1)}, bf16[3,256,1024]{2,1,0:T(8,128)(2,1)}, u32[]{:S(2)}, u32[]{:S(2)}) %collective-permute-start.15) | collective-permute-done | bytes 1572896 | tf_op jit(solution)/shard_map/ppermute | solution.py:378
  236.7 98.4 %attend.1 = (bf16[256,1024]{1,0:T(8,128)(2,1)S(1)}, bf16[256,1024]{1,0:T(8,128)(2,1)S(1)}, bf16[256,1024]{1,0:T(8,128)(2,1)S(1)}, bf16[256,1024]{1,0:T(8,128)(2,...) custom-call(bf16[3,256,1024]{2,1,0:T(8,128)(2,1)S(1)} %project.4.refs_0_, ...), custom_call_target="tpu_custom_call" | custom-call | flops 68719476736 | bytes 8388608 | tf_op jit(solution)/shard_map/attend/pallas_call | solution.py:196
  355.1 21.4 %collective-permute-done.18 = bf16[256,1024]{1,0:T(8,128)(2,1)S(1)} collective-permute-done((bf16[256,1024]{1,0:T(8,128)(2,1)S(1)}, bf16[256,1024]{1,0:T(8,128)(2,1)S(1)}, u32[]{:S(2)}, u32[]{:S(2)}) %collective-permute-start.18) | collective-permute-done | bytes 524320 | tf_op jit(solution)/shard_map/ppermute | solution.py:378
  381.3 6.8 fusion.125
  393.4 16.7 %fusion.132 = f32[1024,4096]{1,0:T(8,128)} fusion(bf16[1024,1024]{1,0:T(8,128)(2,1)} %bitcast.374, bf16[1024,4096]{1,0:T(8,128)(2,1)} %all-gather.9.cloned.1.call-done), kind=kOutput, calls=%fused_computation.385 | convolution fusion | flops 8589934592 | bytes 27262976 | tf_op jit(solution)/shard_map/dot_general | solution.py:35
  410.1 18.6 %fusion.107 = f32[4096,1024]{1,0:T(8,128)} fusion(bf16[1024,1024]{1,0:T(8,128)(2,1)S(1)} %bitcast.372, f32[1024,4096]{1,0:T(8,128)} %fusion.132), kind=kOutput, calls=%fused_computation.370 | convolution fusion | flops 8627683328 | bytes 35651584 | tf_op jit(solution)/shard_map/dot_general | solution.py:39
  428.7 22.9 %fusion.6 = bf16[1024,4096]{1,0:T(8,128)(2,1)} fusion(f32[1024,4096]{1,0:T(8,128)} %fusion.132, bf16[1024,1024]{1,0:T(8,128)(2,1)S(1)} %bitcast.373, bf16[4096,1024]{1,0:T(8,128)(2,1)} %all-gather.11.cloned.1.call-done), kind=kOutput, calls=%fused_computation.8 | convolution fusion | flops 8673820672 | bytes 35651584 | tf_op jit(solution)/shard_map/dot_general | solution.py:39
  451.6 16.3 %fusion.136 = f32[1024,4096]{1,0:T(8,128)} fusion(bf16[1024,1024]{1,0:T(8,128)(2,1)} %bitcast.375, bf16[1024,4096]{1,0:T(8,128)(2,1)} %fusion.6), kind=kOutput, calls=%fused_computation.389 | convolution fusion | flops 8589934592 | bytes 27262976 | tf_op jit(solution)/shard_map/dot_general | solution.py:39
  467.9 11.6 %fusion.133 = f32[1024,1024]{1,0:T(8,128)S(1)} fusion(bf16[1024,4096]{1,0:T(8,128)(2,1)S(1)} %copy-done.103, bf16[1024,4096]{1,0:T(8,128)(2,1)} %all-gather.9.cloned.1.call-done), kind=kOutput, calls=%fused_computation.386 | convolution fusion | flops 8589934592 | bytes 20971520 | tf_op jit(solution)/shard_map/dot_general | solution.py:39
  481.3 16.1 %fusion.108 = f32[1024,1024]{1,0:T(8,128)S(1)} fusion(bf16[4096,1024]{1,0:T(8,128)(2,1)} %all-gather.11.cloned.1.call-done, f32[1024,4096]{1,0:T(8,128)} %fusion.132), kind=kOutput, calls=%fused_computation.371 | convolution fusion | flops 8627683328 | bytes 29360128 | tf_op jit(solution)/shard_map/dot_general | solution.py:35
  518.7 9.6 fusion.126
  528.2 13.0 %fusion.127 = (f32[1024,2048]{1,0:T(8,128)}, f32[1024,2048]{1,0:T(8,128)S(1)}) fusion(f32[1024,4096]{1,0:T(8,128)} %fusion.136), kind=kLoop, calls=%fused_computation.380 | loop fusion | bytes 33554432 | tf_op jit(solution)/shard_map/slice | solution.py:529
  541.2 7.0 fusion.16
  574.1 16.5 %collective-permute-done.39 = bf16[2,2,2,32,512]{4,3,0,1,2:T(8,128)(2,1)S(1)} collective-permute-done((bf16[2,2,2,32,512]{4,3,0,1,2:T(8,128)(2,1)S(1)}, bf16[2,2,2,32,512]{4,3,0,1,2:T(8,128)(2,1)S(1)}, u32[]{:S(2)}, u32[]{:S(2)}) %collective-permute-start.39) | collective-permute-done | bytes 262176 | tf_op jit(solution)/shard_map/ppermute | solution.py:378
  591.0 7.5 collective-permute-done.44
  625.2 168.4 %attend_back.1 = (bf16[3,256,1024]{2,1,0:T(8,128)(2,1)}, bf16[3,256,1024]{2,1,0:T(8,128)(2,1)}, bf16[3,256,1024]{2,1,0:T(8,128)(2,1)}, bf16[3,256,1024]{2,1,0:T(8,128)(2,1)}) custom-call(bf16[3,256,1024]{2,1,0:T(8,128)(2,1)} %copy-done.4, bf16[3,256,1024]{2,1,0:T(8,128)(2,1)} %collective-permute-done.13.refs_1_, ...), custom_call_target="tpu_custom_call" | custom-call | flops 171798691840 | bytes 16777216 | tf_op jit(solution)/shard_map/attend_back/pallas_call | solution.py:310
  805.3 6.6 concatenate.88
  851.2 30.9 %collective-permute-done.26 = bf16[3,256,1024]{2,1,0:T(8,128)(2,1)S(1)} collective-permute-done((bf16[3,256,1024]{2,1,0:T(8,128)(2,1)S(1)}, bf16[3,256,1024]{2,1,0:T(8,128)(2,1)S(1)}, u32[]{:S(2)}, u32[]{:S(2)}) %collective-permute-start.26) | collective-permute-done | bytes 1572896 | tf_op jit(solution)/shard_map/ppermute | solution.py:378
  883.4 8.9 copy.122
  892.2 11.1 multiply_reduce_fusion.2
  921.2 12.5 %fusion.134 = f32[1024,3072]{1,0:T(8,128)} fusion(bf16[1024,1024]{1,0:T(8,128)(2,1)S(1)} %bitcast.371, bf16[3072,1024]{1,0:T(8,128)(2,1)} %bitcast.58), kind=kOutput, calls=%fused_computation.387 | convolution fusion | flops 6442450944 | bytes 20971520 | tf_op jit(solution)/shard_map/dot_general | solution.py:39
  934.8 10.6 fusion.128
  974.8 38.4 %collective-permute-done.27 = bf16[512,1024]{1,0:T(8,128)(2,1)S(1)} collective-permute-done((bf16[512,1024]{1,0:T(8,128)(2,1)S(1)}, bf16[512,1024]{1,0:T(8,128)(2,1)S(1)}, u32[]{:S(2)}, u32[]{:S(2)}) %collective-permute-start.27) | collective-permute-done | bytes 1048608 | tf_op jit(solution)/shard_map/ppermute | solution.py:378
  1018.9 7.3 collective-permute-done.50
  1048.3 8.5 collective-permute-done.52
  1057.0 6.9 collective-permute-done.57
  1069.8 6.5 collective-permute-done.30
  1078.8 6.4 collective-permute-done.31
  (623 shorter events, 384.6 us)
Async XLA Ops:
  7.2 115.9 %all-gather.5.cloned.1.call-start = ((), (), s32[]{:S(2)}) async-start(), calls=%async_computation | async-start | bytes 6488064 | tf_op jit(solution)/shard_map/all_gather | solution.py:389
  9.0 372.3 %all-gather.7.cloned.1.call-start = ((), (), s32[]{:S(2)}) async-start(), calls=%async_computation.1 | async-start | bytes 2162688 | tf_op jit(solution)/shard_map/all_gather | solution.py:389
  10.6 382.7 %all-gather.9.cloned.1.call-start = ((), (), s32[]{:S(2)}) async-start(), calls=%async_computation.2 | async-start | bytes 8650752 | tf_op jit(solution)/shard_map/all_gather | solution.py:389
  12.5 416.2 %all-gather.11.cloned.1.call-start = ((), (), s32[]{:S(2)}) async-start(), calls=%async_computation.3 | async-start | bytes 8650752 | tf_op jit(solution)/shard_map/all_gather | solution.py:389
  24.2 65.5 %collective-permute-start = (bf16[512,1024]{1,0:T(8,128)(2,1)}, bf16[512,1024]{1,0:T(8,128)(2,1)S(1)}, u32[]{:S(2)}, u32[]{:S(2)}) collective-permute-start(bf16[512,1024]{1,0:T(8,128)(2,1)} %get-tuple-element.115), channel_id=1, source_target_pairs={{0,4},{1,5},{2,6},{3,7},{4,0},{5,1},{6,2},{7,3},{8,12},{9,13},{10,... | collective-permute-start | bytes 3145736 | tf_op jit(solution)/shard_map/ppermute | solution.py:378
  129.7 92.5 %collective-permute-start.14 = (bf16[3,256,1024]{2,1,0:T(8,128)(2,1)}, bf16[3,256,1024]{2,1,0:T(8,128)(2,1)}, u32[]{:S(2)}, u32[]{:S(2)}) collective-permute-start(bf16[3,256,1024]{2,1,0:T(8,128)(2,1)} %project.6), channel_id=1, source_target_pairs={{0,2},{1,3},{2,0},{3,1},{4,6},{5,7},{6,4},{7,5},{8,10},{9,11},{10,... | collective-permute-start | bytes 4718600 | tf_op jit(solution)/shard_map/ppermute | solution.py:378
  138.0 98.7 %collective-permute-start.15 = (bf16[3,256,1024]{2,1,0:T(8,128)(2,1)}, bf16[3,256,1024]{2,1,0:T(8,128)(2,1)}, u32[]{:S(2)}, u32[]{:S(2)}) collective-permute-start(bf16[3,256,1024]{2,1,0:T(8,128)(2,1)} %project.7), channel_id=1, source_target_pairs={{0,3},{1,2},{2,1},{3,0},{4,7},{5,6},{6,5},{7,4},{8,11},{9,10},{10,... | collective-permute-start | bytes 4718600 | tf_op jit(solution)/shard_map/ppermute | solution.py:378
  142.8 94.0 %collective-permute-start.13 = (bf16[3,256,1024]{2,1,0:T(8,128)(2,1)}, bf16[3,256,1024]{2,1,0:T(8,128)(2,1)}, u32[]{:S(2)}, u32[]{:S(2)}) collective-permute-start(bf16[3,256,1024]{2,1,0:T(8,128)(2,1)} %project.5), channel_id=1, source_target_pairs={{0,1},{1,0},{2,3},{3,2},{4,5},{5,4},{6,7},{7,6},{8,9},{9,8},{10,11... | collective-permute-start | bytes 4718600 | tf_op jit(solution)/shard_map/ppermute | solution.py:378
  144.9 69.0 %collective-permute-start.7 = (f32[4,4096]{1,0:T(4,128)}, f32[4,4096]{1,0:T(4,128)}, u32[]{:S(2)}, u32[]{:S(2)}) collective-permute-start(f32[4,4096]{1,0:T(4,128)} %slice.208), channel_id=1, source_target_pairs={{0,4},{1,5},{2,6},{3,7},{4,0},{5,1},{6,2},{7,3},{8,12},{9,13},{10,... | collective-permute-start | bytes 196616 | tf_op jit(solution)/shard_map/ppermute | solution.py:378
  149.1 186.6 %collective-permute-start.20 = (bf16[512,1024]{1,0:T(8,128)(2,1)}, bf16[512,1024]{1,0:T(8,128)(2,1)}, u32[]{:S(2)}, u32[]{:S(2)}) collective-permute-start(bf16[512,1024]{1,0:T(8,128)(2,1)} %get-tuple-element.111), channel_id=1, source_target_pairs={{0,4},{1,5},{2,6},{3,7},{4,0},{5,1},{6,2},{7,3},{8,12},{9,13},{10,... | collective-permute-start | bytes 3145736 | tf_op jit(solution)/shard_map/ppermute | solution.py:378
  338.9 37.6 %collective-permute-start.18 = (bf16[256,1024]{1,0:T(8,128)(2,1)S(1)}, bf16[256,1024]{1,0:T(8,128)(2,1)S(1)}, u32[]{:S(2)}, u32[]{:S(2)}) collective-permute-start(bf16[256,1024]{1,0:T(8,128)(2,1)S(1)} %get-tuple-element.46), channel_id=1, source_target_pairs={{0,3},{1,2},{2,1},{3,0},{4,7},{5,6},{6,5},{7,4},{8,11},{9,10},{10,... | collective-permute-start | bytes 1572872 | tf_op jit(solution)/shard_map/ppermute | solution.py:378
  513.4 108.4 %collective-permute-start.21 = (bf16[256,1024]{1,0:T(8,128)(2,1)}, bf16[256,1024]{1,0:T(8,128)(2,1)}, u32[]{:S(2)}, u32[]{:S(2)}) collective-permute-start(bf16[256,1024]{1,0:T(8,128)(2,1)} %get-tuple-element.108), channel_id=1, source_target_pairs={{0,1},{1,0},{2,3},{3,2},{4,5},{5,4},{6,7},{7,6},{8,9},{9,8},{10,11... | collective-permute-start | bytes 1572872 | tf_op jit(solution)/shard_map/ppermute | solution.py:378
  515.0 107.2 %collective-permute-start.22 = (bf16[256,1024]{1,0:T(8,128)(2,1)}, bf16[256,1024]{1,0:T(8,128)(2,1)}, u32[]{:S(2)}, u32[]{:S(2)}) collective-permute-start(bf16[256,1024]{1,0:T(8,128)(2,1)} %get-tuple-element.107), channel_id=1, source_target_pairs={{0,2},{1,3},{2,0},{3,1},{4,6},{5,7},{6,4},{7,5},{8,10},{9,11},{10,... | collective-permute-start | bytes 1572872 | tf_op jit(solution)/shard_map/ppermute | solution.py:378
  515.0 109.3 %collective-permute-start.23 = (bf16[256,1024]{1,0:T(8,128)(2,1)}, bf16[256,1024]{1,0:T(8,128)(2,1)}, u32[]{:S(2)}, u32[]{:S(2)}) collective-permute-start(bf16[256,1024]{1,0:T(8,128)(2,1)} %get-tuple-element.106), channel_id=1, source_target_pairs={{0,3},{1,2},{2,1},{3,0},{4,7},{5,6},{6,5},{7,4},{8,11},{9,10},{10,... | collective-permute-start | bytes 1572872 | tf_op jit(solution)/shard_map/ppermute | solution.py:378
  517.1 39.0 %collective-permute-start.73 = (f32[4,4096]{1,0:T(4,128)S(1)}, f32[4,4096]{1,0:T(4,128)S(1)}, u32[]{:S(2)}, u32[]{:S(2)}) collective-permute-start(f32[4,4096]{1,0:T(4,128)S(1)} %constant_dynamic-update-slice_fusion.2), channel_id=1, source_target_pairs={{0,4},{1,5},{2,6},{3,7},{4,0},{5,1},{6,2},{7,3},{8,12},{9,13},{10,... | collective-permute-start | bytes 196616 | tf_op jit(solution)/shard_map/ppermute | solution.py:378
  570.6 48.0 %collective-permute-start.76 = (f32[32,4096]{1,0:T(8,128)S(1)}, f32[32,4096]{1,0:T(8,128)S(1)}, u32[]{:S(2)}, u32[]{:S(2)}) collective-permute-start(f32[32,4096]{1,0:T(8,128)S(1)} %pad_maximum_fusion.6), channel_id=1, source_target_pairs={{0,16},{1,17},{2,18},{3,19},{4,20},{5,21},{6,22},{7,23},{8,24},{9,... | collective-permute-start | bytes 1572872 | tf_op jit(solution)/shard_map/ppermute | solution.py:378
  618.6 193.3 %collective-permute-start.58 = (bf16[2,2,2,2,128,512]{5,4,1,2,3,0:T(8,128)(2,1)}, bf16[2,2,2,2,128,512]{5,4,1,2,3,0:T(8,128)(2,1)}, u32[]{:S(2)}, u32[]{:S(2)}) collective-permute-start(bf16[2,2,2,2,128,512]{5,4,1,2,3,0:T(8,128)(2,1)} %fusion.18), channel_id=1, source_target_pairs={{0,8},{1,9},{2,10},{3,11},{4,12},{5,13},{6,14},{7,15},{8,0},{9,1},... | collective-permute-start | bytes 6291464 | tf_op jit(solution)/shard_map/ppermute | solution.py:378
  621.8 195.6 %collective-permute-start.48 = (bf16[2,2,2,2,32,2048]{5,4,1,2,3,0:T(8,128)(2,1)}, bf16[2,2,2,2,32,2048]{5,4,1,2,3,0:T(8,128)(2,1)}, u32[]{:S(2)}, u32[]{:S(2)}) collective-permute-start(bf16[2,2,2,2,32,2048]{5,4,1,2,3,0:T(8,128)(2,1)} %fusion.16), channel_id=1, source_target_pairs={{0,8},{1,9},{2,10},{3,11},{4,12},{5,13},{6,14},{7,15},{8,0},{9,1},... | collective-permute-start | bytes 6291464 | tf_op jit(solution)/shard_map/ppermute | solution.py:378
  622.2 177.9 %collective-permute-start.19 = (bf16[512,1024]{1,0:T(8,128)(2,1)}, bf16[512,1024]{1,0:T(8,128)(2,1)}, u32[]{:S(2)}, u32[]{:S(2)}) collective-permute-start(bf16[512,1024]{1,0:T(8,128)(2,1)} %bitcast.35), channel_id=1, source_target_pairs={{0,4},{1,5},{2,6},{3,7},{4,0},{5,1},{6,2},{7,3},{8,12},{9,13},{10,... | collective-permute-start | bytes 3145736 | tf_op jit(solution)/shard_map/ppermute | solution.py:378
  624.3 179.4 %collective-permute-start.77 = (f32[64,4096]{1,0:T(8,128)}, f32[64,4096]{1,0:T(8,128)}, u32[]{:S(2)}, u32[]{:S(2)}) collective-permute-start(f32[64,4096]{1,0:T(8,128)} %concatenate.87), channel_id=1, source_target_pairs={{0,8},{1,9},{2,10},{3,11},{4,12},{5,13},{6,14},{7,15},{8,0},{9,1},... | collective-permute-start | bytes 3145736 | tf_op jit(solution)/shard_map/ppermute | solution.py:378
  624.3 169.4 %collective-permute-start.47 = (bf16[32,512]{1,0:T(8,128)(2,1)}, bf16[32,512]{1,0:T(8,128)(2,1)}, u32[]{:S(2)}, u32[]{:S(2)}) collective-permute-start(bf16[32,512]{1,0:T(8,128)(2,1)} %fusion.78), channel_id=1, source_target_pairs={{0,4},{1,5},{2,6},{3,7},{4,0},{5,1},{6,2},{7,3},{8,12},{9,13},{10,... | collective-permute-start | bytes 98312 | tf_op jit(solution)/shard_map/ppermute | solution.py:378
  803.7 37.6 %collective-permute-start.24 = (bf16[3,256,1024]{2,1,0:T(8,128)(2,1)}, bf16[3,256,1024]{2,1,0:T(8,128)(2,1)}, u32[]{:S(2)}, u32[]{:S(2)}) collective-permute-start(bf16[3,256,1024]{2,1,0:T(8,128)(2,1)} %get-tuple-element.50), channel_id=1, source_target_pairs={{0,1},{1,0},{2,3},{3,2},{4,5},{5,4},{6,7},{7,6},{8,9},{9,8},{10,11... | collective-permute-start | bytes 4718600 | tf_op jit(solution)/shard_map/ppermute | solution.py:378
  818.8 63.2 %collective-permute-start.26 = (bf16[3,256,1024]{2,1,0:T(8,128)(2,1)S(1)}, bf16[3,256,1024]{2,1,0:T(8,128)(2,1)S(1)}, u32[]{:S(2)}, u32[]{:S(2)}) collective-permute-start(bf16[3,256,1024]{2,1,0:T(8,128)(2,1)S(1)} %copy-done.102), channel_id=1, source_target_pairs={{0,3},{1,2},{2,1},{3,0},{4,7},{5,6},{6,5},{7,4},{8,11},{9,10},{10,... | collective-permute-start | bytes 4718600 | tf_op jit(solution)/shard_map/ppermute | solution.py:378
  823.9 138.7 %collective-permute-start.59 = (bf16[2,2,2,128,512]{4,3,0,1,2:T(8,128)(2,1)}, bf16[2,2,2,128,512]{4,3,0,1,2:T(8,128)(2,1)}, u32[]{:S(2)}, u32[]{:S(2)}) collective-permute-start(bf16[2,2,2,128,512]{4,3,0,1,2:T(8,128)(2,1)} %fusion.27), channel_id=1, source_target_pairs={{0,16},{1,17},{2,18},{3,19},{4,20},{5,21},{6,22},{7,23},{8,24},{9,... | collective-permute-start | bytes 3145736 | tf_op jit(solution)/shard_map/ppermute | solution.py:378
  831.6 133.0 %collective-permute-start.64 = (bf16[2,2,2,128,512]{4,3,1,2,0:T(8,128)(2,1)}, bf16[2,2,2,128,512]{4,3,1,2,0:T(8,128)(2,1)}, u32[]{:S(2)}, u32[]{:S(2)}) collective-permute-start(bf16[2,2,2,128,512]{4,3,1,2,0:T(8,128)(2,1)} %fusion.28), channel_id=1, source_target_pairs={{0,1},{1,0},{2,3},{3,2},{4,5},{5,4},{6,7},{7,6},{8,9},{9,8},{10,11... | collective-permute-start | bytes 3145736 | tf_op jit(solution)/shard_map/ppermute | solution.py:378
  841.2 127.6 %collective-permute-start.49 = (bf16[2,2,2,32,2048]{4,3,0,1,2:T(8,128)(2,1)}, bf16[2,2,2,32,2048]{4,3,0,1,2:T(8,128)(2,1)}, u32[]{:S(2)}, u32[]{:S(2)}) collective-permute-start(bf16[2,2,2,32,2048]{4,3,0,1,2:T(8,128)(2,1)} %fusion.25), channel_id=1, source_target_pairs={{0,16},{1,17},{2,18},{3,19},{4,20},{5,21},{6,22},{7,23},{8,24},{9,... | collective-permute-start | bytes 3145736 | tf_op jit(solution)/shard_map/ppermute | solution.py:378
  849.5 122.8 %collective-permute-start.54 = (bf16[2,2,2,32,2048]{4,3,1,2,0:T(8,128)(2,1)}, bf16[2,2,2,32,2048]{4,3,1,2,0:T(8,128)(2,1)}, u32[]{:S(2)}, u32[]{:S(2)}) collective-permute-start(bf16[2,2,2,32,2048]{4,3,1,2,0:T(8,128)(2,1)} %fusion.26), channel_id=1, source_target_pairs={{0,1},{1,0},{2,3},{3,2},{4,5},{5,4},{6,7},{7,6},{8,9},{9,8},{10,11... | collective-permute-start | bytes 3145736 | tf_op jit(solution)/shard_map/ppermute | solution.py:378
  956.3 74.2 %collective-permute-start.28 = (bf16[2,2,2,2,32,1536]{5,4,1,2,3,0:T(8,128)(2,1)}, bf16[2,2,2,2,32,1536]{5,4,1,2,3,0:T(8,128)(2,1)}, u32[]{:S(2)}, u32[]{:S(2)}) collective-permute-start(bf16[2,2,2,2,32,1536]{5,4,1,2,3,0:T(8,128)(2,1)} %fusion.23), channel_id=1, source_target_pairs={{0,8},{1,9},{2,10},{3,11},{4,12},{5,13},{6,14},{7,15},{8,0},{9,1},... | collective-permute-start | bytes 4718600 | tf_op jit(solution)/shard_map/ppermute | solution.py:378
  962.5 72.1 %collective-permute-start.33 = (bf16[2,2,2,2,32,1536]{5,4,1,2,0,3:T(8,128)(2,1)S(1)}, bf16[2,2,2,2,32,1536]{5,4,1,2,0,3:T(8,128)(2,1)S(1)}, u32[]{:S(2)}, u32[]{:S(2)}) collective-permute-start(bf16[2,2,2,2,32,1536]{5,4,1,2,0,3:T(8,128)(2,1)S(1)} %copy-done.53), channel_id=1, source_target_pairs={{0,8},{1,9},{2,10},{3,11},{4,12},{5,13},{6,14},{7,15},{8,0},{9,1},... | collective-permute-start | bytes 4718600 | tf_op jit(solution)/shard_map/ppermute | solution.py:378
  964.7 48.5 %collective-permute-start.27 = (bf16[512,1024]{1,0:T(8,128)(2,1)S(1)}, bf16[512,1024]{1,0:T(8,128)(2,1)S(1)}, u32[]{:S(2)}, u32[]{:S(2)}) collective-permute-start(bf16[512,1024]{1,0:T(8,128)(2,1)S(1)} %bitcast.380), channel_id=1, source_target_pairs={{0,4},{1,5},{2,6},{3,7},{4,0},{5,1},{6,2},{7,3},{8,12},{9,13},{10,... | collective-permute-start | bytes 3145736 | tf_op jit(solution)/shard_map/ppermute | solution.py:378
  968.8 48.6 %collective-permute-start.60 = (bf16[2,2,128,512]{3,2,0,1:T(8,128)(2,1)S(1)}, bf16[2,2,128,512]{3,2,0,1:T(8,128)(2,1)S(1)}, u32[]{:S(2)}, u32[]{:S(2)}) collective-permute-start(bf16[2,2,128,512]{3,2,0,1:T(8,128)(2,1)S(1)} %fusion.36), channel_id=1, source_target_pairs={{0,1},{1,0},{2,3},{3,2},{4,5},{5,4},{6,7},{7,6},{8,9},{9,8},{10,11... | collective-permute-start | bytes 1572872 | tf_op jit(solution)/shard_map/ppermute | solution.py:378
  972.3 46.3 %collective-permute-start.65 = (bf16[2,2,128,512]{3,2,0,1:T(8,128)(2,1)S(1)}, bf16[2,2,128,512]{3,2,0,1:T(8,128)(2,1)S(1)}, u32[]{:S(2)}, u32[]{:S(2)}) collective-permute-start(bf16[2,2,128,512]{3,2,0,1:T(8,128)(2,1)S(1)} %fusion.37), channel_id=1, source_target_pairs={{0,16},{1,17},{2,18},{3,19},{4,20},{5,21},{6,22},{7,23},{8,24},{9,... | collective-permute-start | bytes 1572872 | tf_op jit(solution)/shard_map/ppermute | solution.py:378
  (172 other events, 3537.1 us)
Sparse Core Ops, SparseCore 0:
  11.5 111.5 all-gather.4
  126.7 114.7 all-gather.6
  245.0 77.6 all-gather.8
  326.1 84.5 all-gather.10

commit v2 on v1

v2 whole, which is shorter than its diff:
```python
from functools import partial
import math

import jax
import jax.numpy as jnp
from jax import lax
from jax.experimental import pallas as pl
from jax.experimental.pallas import tpu as pltpu
from jax.sharding import PartitionSpec as P

D = 1024
HEADS = 16
HEAD = 64
FF = 4096
FRAMES = 16
GRID_W = 16
STEP = 10
PATCHES = 256
LENGTH = 4096

norm_epsilon = 1e-06
adam_epsilon = 1e-08
first_decay = 0.5
second_decay = 0.5
weight_decay = 0.1
clip_limit = 1.0
highest = lax.Precision.HIGHEST
AXES = ("clip", "seq")
LOW = jnp.bfloat16
WIDE = jnp.float32
SOFT = math.log2(math.e) * HEAD ** (-0.5)


def dot(left, right):
    return jnp.dot(left, right, preferred_element_type=WIDE)


def contract(left, right, left_dim, right_dim):
    return lax.dot_general(
        left, right, (((left_dim,), (right_dim,)), ((), ())), preferred_element_type=WIDE
    )


def normalize(operand):
    centered = operand - jnp.mean(operand, axis=-1, keepdims=True)
    variance = jnp.mean(centered * centered, axis=-1, keepdims=True)
    return centered * lax.rsqrt(variance + norm_epsilon)


def modulate(operand, shift_by, scale_by):
    return normalize(operand) * (1.0 + scale_by) + shift_by


def adam_update(gradient, master, moment_one, moment_two, step_rate):
    moment_one = first_decay * moment_one + (1.0 - first_decay) * gradient
    moment_two = second_decay * moment_two + (1.0 - second_decay) * gradient * gradient
    corrected_one = moment_one / (1.0 - first_decay**STEP)
    corrected_two = moment_two / (1.0 - second_decay**STEP)
    master = master - step_rate * (
        corrected_one / (jnp.sqrt(corrected_two) + adam_epsilon) + weight_decay * master
    )
    return (moment_one, moment_two, master)


def rotary_tables(times, places):
    frame_ids = places // PATCHES
    patch_row = (places % PATCHES // GRID_W).astype(WIDE)
    column = (places % GRID_W).astype(WIDE)
    matches = frame_ids[None, :] == jnp.arange(FRAMES, dtype=jnp.int32)[:, None]
    moment = jnp.sum(jnp.where(matches, times[:, None], 0), axis=0).astype(WIDE)
    time_pairs = HEAD // 8
    grid_pairs = 3 * HEAD // 16
    pair_ids = jnp.arange(HEAD // 2, dtype=jnp.int32)
    second = time_pairs + grid_pairs
    offset = jnp.where(pair_ids < time_pairs, 0, jnp.where(pair_ids < second, time_pairs, second))
    length = jnp.where(pair_ids < time_pairs, time_pairs, grid_pairs)
    frequency = jnp.exp(
        -math.log(10000.0) * (pair_ids - offset).astype(WIDE) / length.astype(WIDE)
    )
    ids = pair_ids[:, None]
    coordinate = jnp.where(
        ids < time_pairs, moment[None], jnp.where(ids < second, patch_row[None], column[None])
    )
    angles = coordinate * frequency[:, None]
    return jnp.cos(angles), jnp.sin(angles)


anywhere = pl.BlockSpec(memory_space=pl.ANY)


def whole(shape):
    return pl.BlockSpec(shape, lambda *ids: (0,) * len(shape))


def call(
    kernel,
    name,
    ids,
    grid,
    ins,
    in_specs,
    outs,
    out_specs,
    scratch=(),
    after=(),
    room=56,
    aliases=None,
    time=2,
):
    count, extra = 1 + len(ins), len(after)

    def body(*refs):
        kernel(*refs[:count], *refs[count + extra :])

    body.__name__ = name
    return pl.pallas_call(
        body,
        grid_spec=pltpu.PrefetchScalarGridSpec(
            num_scalar_prefetch=1,
            grid=grid,
            in_specs=list(in_specs) + [anywhere] * extra,
            out_specs=out_specs,
            scratch_shapes=list(scratch),
        ),
        out_shape=outs,
        input_output_aliases=aliases or {},
        compiler_params=pltpu.CompilerParams(vmem_limit_bytes=room << 20),
        cost_estimate=pl.CostEstimate(
            flops=int(time * 1.15e9), bytes_accessed=int(time * 3e6), transcendentals=0
        ),
        name=name,
    )(ids, *ins, *after)


def low_array(*shape):
    return jax.ShapeDtypeStruct(shape, LOW)


def wide_array(*shape):
    return jax.ShapeDtypeStruct(shape, WIDE)


def bit_of(rank, mask):
    return rank // mask % 2


def chunk_spec(rows, frames):
    return pl.BlockSpec((1, rows // frames, D), lambda r, f, ids: (r, f, 0))


def pair_specs(rows, frames):
    size = rows // frames
    return [
        pl.BlockSpec((1, size, D), lambda r, f, ids: (ids[1], f, 0)),
        pl.BlockSpec((size, D), lambda r, f, ids: (f, 0)),
    ]


def row_spec(rows, frames):
    return pl.BlockSpec((rows // frames, D), lambda r, f, ids: (r * frames + f, 0))


def read_pair(ids_ref, own_ref, other_ref):
    own = pl.program_id(0) == ids_ref[1]
    return jnp.where(own, own_ref[0].astype(WIDE), other_ref[...].astype(WIDE))


def piece(ref, number, frames):
    row = pl.program_id(0) * frames + pl.program_id(1)
    return ref[pl.ds(row, 1), number * D : (number + 1) * D]


def put_piece(ref, number, frames, value):
    row = pl.program_id(0) * frames + pl.program_id(1)
    ref[pl.ds(row, 1), number * D : (number + 1) * D] = value


def norm_parts(operand):
    centered = operand - jnp.mean(operand, axis=-1, keepdims=True)
    variance = jnp.mean(centered * centered, axis=-1, keepdims=True)
    inverse = lax.rsqrt(variance + norm_epsilon)
    return centered * inverse, inverse


def norm_back(gradient, normed, inverse, scale):
    shift_grad = jnp.sum(gradient, axis=0, keepdims=True)
    scale_grad = jnp.sum(gradient * normed, axis=0, keepdims=True)
    inner = gradient * (1.0 + scale)
    mean = jnp.mean(inner, axis=-1, keepdims=True)
    along = jnp.mean(inner * normed, axis=-1, keepdims=True)
    return (inner - mean - normed * along) * inverse, shift_grad, scale_grad


def norm_one(ids, tokens, early, frames, after=()):
    rows = tokens.shape[1]

    def kernel(ids_ref, tokens_ref, early_ref, out_ref):
        normed, _ = norm_parts(tokens_ref[0].astype(WIDE))
        shift, scale = piece(early_ref, 0, frames), piece(early_ref, 1, frames)
        out_ref[...] = (normed * (1.0 + scale) + shift).astype(LOW)

    return call(
        kernel,
        "norm_one",
        ids,
        (2, frames),
        [tokens, early],
        [chunk_spec(rows, frames), whole(early.shape)],
        low_array(2 * rows, D),
        row_spec(rows, frames),
        after=after,
        time=5,
    )


def project(ids, rows, weight, cosines, sines, members, first, after=()):
    tokens, width = rows.shape
    columns = members * HEAD
    half = HEAD // 2

    def kernel(ids_ref, rows_ref, weight_ref, cos_ref, sin_ref, out_ref):
        across = dot(rows_ref[...], weight_ref[...]).T
        kind = pl.program_id(0)

        @pl.when(kind == 2)
        def _():
            for member in range(members):
                out_ref[member, 0] = across[member * HEAD : (member + 1) * HEAD].astype(LOW)

        @pl.when(kind < 2)
        def _():
            cosines, sines = cos_ref[...], sin_ref[...]
            for member in range(members):
                one = across[member * HEAD : member * HEAD + half]
                two = across[member * HEAD + half : (member + 1) * HEAD]
                out_ref[member, 0, :half] = (one * cosines - two * sines).astype(LOW)
                out_ref[member, 0, half:] = (two * cosines + one * sines).astype(LOW)

    table = pl.BlockSpec((half, tokens), lambda t, ids: (0, ids[0]))
    return call(
        kernel,
        "project",
        ids,
        (3,),
        [rows, weight, cosines, sines],
        [
            whole((tokens, width)),
            pl.BlockSpec((width, columns), lambda t, ids: (0, first * 3 + t)),
            table,
            table,
        ],
        low_array(members, 3, HEAD, tokens),
        pl.BlockSpec((members, 1, HEAD, tokens), lambda t, ids: (0, t, 0, 0)),
        after=after,
        time=6,
    )


def attend(ids, parts, into, head, heads, after=()):
    members, _, _, tokens = parts.shape
    size, block = min(1024, tokens), min(512, tokens)
    length = members * tokens
    per, count, inside = tokens // size, length // block, tokens // block
    before = [] if into is None else [into]

    def kernel(ids_ref, part_ref, *refs):
        low_ref, wide_ref, total_ref, key_rows = refs[len(before) :]
        step = pl.program_id(0)

        @pl.when(step == 0)
        def _():
            for member in range(members):
                key_rows[member * tokens : (member + 1) * tokens, :] = part_ref[member, 1].T

        member = step // per
        start = 0 if per == 1 else pl.multiple_of(step % per * size, size)
        queries = part_ref[member, 0, :, pl.ds(start, size)]
        gathered = jnp.zeros((HEAD, size), WIDE)
        top = jnp.full((1, size), -1e30, WIDE)
        total = jnp.zeros((1, size), WIDE)
        following = dot(key_rows[0:block, :], queries)
        for number in range(count):
            scores = following
            if number + 1 < count:
                following = dot(key_rows[(number + 1) * block : (number + 2) * block, :], queries)
            raised = jnp.maximum(top, jnp.max(scores, axis=0, keepdims=True))
            shrink = jnp.exp2((top - raised) * SOFT)
            probs = jnp.exp2(scores * SOFT - raised * SOFT)
            total = total * shrink + jnp.sum(probs, axis=0, keepdims=True)
            at = number % inside * block
            values = part_ref[number // inside, 2, :, at : at + block]
            gathered = gathered * shrink + dot(values, probs.astype(LOW))
            top = raised
        attended = gathered / total
        wide_ref[...] = attended
        total_ref[...] = top * SOFT + jnp.log2(total)
        low_ref[member, :, pl.ds(start, size)] = attended.astype(LOW)

    return call(
        kernel,
        "attend",
        ids,
        (length // size,),
        [parts, *before],
        [whole(parts.shape)] + [anywhere] * len(before),
        [
            low_array(members, heads * HEAD, tokens),
            wide_array(HEAD, length),
            wide_array(1, length),
        ],
        [
            pl.BlockSpec((members, HEAD, tokens), lambda i, ids: (0, head, 0)),
            pl.BlockSpec((HEAD, size), lambda i, ids: (0, i)),
            pl.BlockSpec((1, size), lambda i, ids: (0, i)),
        ],
        [pltpu.VMEM((length, HEAD), LOW)],
        after,
        aliases={2: 0} if before else {},
        time=26,
    )


def middle_part(ids, parts, members, weight, tokens, upstream, late, frames, after=()):
    rows = tokens.shape[1]
    size = rows // frames
    group = D // members

    def kernel(ids_ref, *refs):
        part_refs = refs[: len(parts)]
        weight_ref, tokens_ref, g_own, g_other, late_ref = refs[len(parts) : len(parts) + 5]
        low_ref, projected_ref, middle_ref, normed_ref, grad_ref, across = refs[len(parts) + 5 :]
        for member in range(members):
            at = member * group
            for ref in part_refs:
                across[at : at + ref.shape[1], :] = ref[member]
                at += ref.shape[1]
        low = across[...].T
        low_ref[...] = low
        projected = dot(low, weight_ref[...].reshape(D, D))
        projected_ref[...] = projected
        middle = tokens_ref[0].astype(WIDE) + piece(late_ref, 0, frames) * projected
        middle_ref[...] = middle
        normed, _ = norm_parts(middle)
        shift, scale = piece(late_ref, 1, frames), piece(late_ref, 2, frames)
        normed_ref[...] = (normed * (1.0 + scale) + shift).astype(LOW)
        upstream = read_pair(ids_ref, g_own, g_other)
        grad_ref[...] = (piece(late_ref, 3, frames) * upstream).astype(LOW)

    part_specs = [
        pl.BlockSpec(part.shape[:2] + (size,), lambda r, f, ids: (0, 0, r * frames + f))
        for part in parts
    ]
    return call(
        kernel,
        "middle_part",
        ids,
        (2, frames),
        [*parts, weight[0], tokens, *upstream, late],
        part_specs
        + [weight[1], chunk_spec(rows, frames)]
        + pair_specs(rows, frames)
        + [whole(late.shape)],
        [
            low_array(2 * rows, D),
            wide_array(2 * rows, D),
            wide_array(2 * rows, D),
            low_array(2 * rows, D),
            low_array(2 * rows, D),
        ],
        [row_spec(rows, frames)] * 5,
        [pltpu.VMEM((D, size), LOW)],
        after,
        time=12,
    )


def quarter_at(step, ids, core_mask, pairs):
    core = bit_of(ids[2], core_mask)
    return step % pairs * 2 + jnp.where(step < pairs, 1 - core, core)


def feed(ids, rows, grads, up, down, hidden, devices, core_mask, pairs, after=()):
    tokens, width = rows.shape
    chunk = 512
    own_up, own_down = width // devices, hidden // devices
    aside = width // chunk
    quarter = width // (2 * pairs)
    owners = devices // 2
    spans = hidden // (2 * pairs) // chunk
    steps = hidden // chunk
    kind = LOW if own_up % 16 == 0 else WIDE

    def chunk_at(step, ids):
        return quarter_at(step // spans, ids, core_mask, pairs) * spans + step % spans

    def kernel(
        ids_ref,
        rows_ref,
        grad_ref,
        up_ref,
        down_ref,
        branch_ref,
        back_ref,
        down_sent,
        down_kept,
        up_sent,
        up_kept,
        across,
    ):
        step = pl.program_id(0)

        @pl.when(step == 0)
        def _():
            across[...] = rows_ref[...].T
            branch_ref[...] = jnp.zeros_like(branch_ref)
            back_ref[...] = jnp.zeros_like(back_ref)

        grads = grad_ref[...]
        up, down = up_ref[...].reshape(width, chunk), down_ref[...].reshape(chunk, width)
        upper = dot(rows_ref[...], up)
        hidden_grad = dot(grads, down.T)
        root = math.sqrt(2 / math.pi)
        square = upper * upper
        curve = jnp.tanh(upper * (root + root * 0.044715 * square))
        share = 0.5 + 0.5 * curve
        low = (upper * share).astype(LOW)
        slope = share + 0.5 * upper * (1.0 - curve * curve) * (root + 3 * root * 0.044715 * square)
        upper_grad = (hidden_grad * slope).astype(LOW)
        branch_ref[...] += dot(low, down)
        back_ref[...] += dot(upper_grad, up.T)
        down_grad = dot(low.T, grads)

        @pl.when(step < steps // 2)
        def _():
            down_sent[...] = down_grad.astype(LOW).reshape(down_sent.shape)

        @pl.when(step >= steps // 2)
        def _():
            down_kept[...] = down_grad.astype(kind).reshape(down_kept.shape)

        core = bit_of(ids_ref[2], core_mask)
        taken = owners // pairs
        for out, bit in ((up_sent, 1 - core), (up_kept, core)):
            for number in range(pairs):
                start = pl.multiple_of((2 * number + bit) * quarter, quarter)
                value = dot(across[pl.ds(start, quarter), :], upper_grad).astype(out.dtype)
                out[number * taken : (number + 1) * taken] = value.reshape(
                    (taken,) + out.shape[1:]
                )

    def sent_at(step, ids):
        return (jnp.minimum(step, steps // 2 - 1), 0, 0)

    def kept_at(step, ids):
        return (jnp.maximum(step - steps // 2, 0), 0, 0)

    def up_at(step, ids):
        at = chunk_at(step, ids)
        return (0, at // aside, 0, at % aside)

    down_block = (chunk // own_down, own_down, width)
    up_block = (owners, 1, own_up, chunk)
    up_shape = (owners, hidden // width, own_up, width)
    return call(
        kernel,
        "feed",
        ids,
        (steps,),
        [rows, grads, up[0], down[0]],
        [
            whole((tokens, width)),
            whole((tokens, width)),
            pl.BlockSpec(up[1], lambda step, ids: up[2](chunk_at(step, ids))),
            pl.BlockSpec(down[1], lambda step, ids: down[2](chunk_at(step, ids))),
        ],
        [
            wide_array(tokens, width),
            wide_array(tokens, width),
            low_array(owners, own_down, width),
            jax.ShapeDtypeStruct((owners, own_down, width), kind),
            low_array(*up_shape) if kind == LOW else wide_array(*up_shape),
            jax.ShapeDtypeStruct(up_shape, kind),
        ],
        [
            whole((tokens, width)),
            whole((tokens, width)),
            pl.BlockSpec(down_block, sent_at),
            pl.BlockSpec(down_block, kept_at),
            pl.BlockSpec(up_block, up_at),
            pl.BlockSpec(up_block, up_at),
        ],
        [pltpu.VMEM((width, tokens), LOW)],
        after,
        room=62,
        time=66,
    )


def middle_back(ids, middle, branch, back, projected, upstream, late, frames, after=()):
    rows = upstream[1].shape[0]

    def kernel(
        ids_ref,
        middle_ref,
        branch_ref,
        back_ref,
        projected_ref,
        g_own,
        g_other,
        late_ref,
        result_ref,
        middle_grad_ref,
        projected_grad_ref,
        pieces_ref,
    ):
        middle, branch = middle_ref[...], branch_ref[...]
        upstream = read_pair(ids_ref, g_own, g_other)
        result_ref[0] = (middle + piece(late_ref, 3, frames) * branch).astype(LOW)
        normed, inverse = norm_parts(middle)
        grad, shift_grad, scale_grad = norm_back(
            back_ref[...], normed, inverse, piece(late_ref, 2, frames)
        )
        grad = grad + upstream
        middle_grad_ref[...] = grad
        projected_grad_ref[...] = (piece(late_ref, 0, frames) * grad).astype(LOW)
        gate_grad = jnp.sum(grad * projected_ref[...], axis=0, keepdims=True)
        put_piece(pieces_ref, 0, frames, gate_grad)
        put_piece(pieces_ref, 1, frames, shift_grad)
        put_piece(pieces_ref, 2, frames, scale_grad)
        put_piece(pieces_ref, 3, frames, jnp.sum(upstream * branch, axis=0, keepdims=True))

    block = row_spec(rows, frames)
    return call(
        kernel,
        "middle_back",
        ids,
        (2, frames),
        [middle, branch, back, projected, *upstream, late],
        [block] * 4 + pair_specs(rows, frames) + [whole(late.shape)],
        [
            low_array(2, rows, D),
            wide_array(2 * rows, D),
            low_array(2 * rows, D),
            wide_array(2 * frames, 4 * D),
        ],
        [chunk_spec(rows, frames)] + [block] * 2 + [whole((2 * frames, 4 * D))],
        after=after,
        time=12,
    )


def put_half(step, pairs, value, sent_ref, kept_ref):
    @pl.when(step < pairs)
    def _():
        sent_ref[0] = value.astype(LOW)

    @pl.when(step >= pairs)
    def _():
        kept_ref[0] = value


def half_specs(pairs, rows, width):
    return [
        pl.BlockSpec((1, rows, width), lambda i, ids: (jnp.minimum(i, pairs - 1), 0, 0)),
        pl.BlockSpec((1, rows, width), lambda i, ids: (jnp.maximum(i - pairs, 0), 0, 0)),
    ]


def hand_out(ids, weight, gradient, attended, members, head_count, core_mask, pairs, after=()):
    tokens, width = gradient.shape
    quarter = width // (2 * pairs)
    groups = members // (2 * pairs)
    group = width // members
    front = group - HEAD

    def kernel(ids_ref, weight_ref, grad_ref, attended_ref, *refs):
        *out_refs, sent_ref, kept_ref = refs
        step = pl.program_id(0)
        grads = grad_ref[...]
        if weight_ref.shape[0] == 1:
            taken = weight_ref[0, pl.ds(pl.multiple_of(step * quarter, quarter), quarter), :]
        else:
            blocks = quarter // weight_ref.shape[1]
            taken = weight_ref[pl.ds(step * blocks, blocks)].reshape(quarter, width)
        block = contract(taken, grads, 1, 1).astype(LOW)
        for number in range(groups):
            at = number * group
            out_refs[0][number] = block[at + front : at + group]
            if front:
                out_refs[1][number] = block[at : at + front]
        put_half(step, pairs, dot(attended_ref[...].T, grads), sent_ref, kept_ref)

    shapes = [(members, HEAD, tokens)] + [(members, front, tokens)] * (front > 0)
    halves = (pairs, quarter, width)
    return call(
        kernel,
        "hand_out",
        ids,
        (2 * pairs,),
        [weight[0], gradient, attended],
        [
            weight[1],
            whole(gradient.shape),
            pl.BlockSpec(
                (tokens, quarter), lambda i, ids: (0, quarter_at(i, ids, core_mask, pairs))
            ),
        ],
        [low_array(*shape) for shape in shapes] + [low_array(*halves), wide_array(*halves)],
        [
            pl.BlockSpec((groups,) + shape[1:], lambda i, ids: (i, 0, 0))
            for shape in shapes
        ]
        + half_specs(pairs, quarter, width),
        after=after,
        time=10,
    )


def turn_back(operand, cosines, sines):
    half = HEAD // 2
    one, two = operand[:half], operand[half:]
    return jnp.concatenate([one * cosines + two * sines, two * cosines - one * sines], axis=0)


def attend_back(ids, parts, grads, head, wide, total, cosines, sines, after=()):
    members, _, _, tokens = parts.shape
    size, block = min(1024, tokens), min(512, tokens)
    length = members * tokens
    per, count, inside = tokens // size, length // block, tokens // block
    back = HEAD ** (-0.5)

    def kernel(
        ids_ref,
        part_ref,
        grad_ref,
        wide_ref,
        total_ref,
        cos_ref,
        sin_ref,
        out_ref,
        key_rows,
        key_sum,
        value_sum,
    ):
        step = pl.program_id(0)

        @pl.when(step == 0)
        def _():
            for member in range(members):
                key_rows[member * tokens : (member + 1) * tokens, :] = part_ref[member, 1].T
            key_sum[...] = jnp.zeros_like(key_sum)
            value_sum[...] = jnp.zeros_like(value_sum)

        member = step // per
        start = 0 if per == 1 else pl.multiple_of(step % per * size, size)
        queries_across = part_ref[member, 0, :, pl.ds(start, size)]
        grads_across = grad_ref[member, :, pl.ds(start, size)]
        queries = queries_across.T
        out_grads = grads_across.T
        delta = jnp.sum(grads_across.astype(WIDE) * wide_ref[...], axis=0, keepdims=True).T
        totals = total_ref[...].T
        query_grad = jnp.zeros((size, HEAD), WIDE)

        def pair(number):
            source, at = number // inside, number % inside * block
            return (
                dot(queries, part_ref[source, 1, :, at : at + block]),
                dot(out_grads, part_ref[source, 2, :, at : at + block]),
            )

        following = pair(0)
        for number in range(count):
            scores, prob_grad = following
            if number + 1 < count:
                following = pair(number + 1)
            here = slice(number * block, (number + 1) * block)
            probs = jnp.exp2(scores * SOFT - totals)
            score_grad = (probs * (prob_grad - delta)).astype(LOW)
            value_sum[:, here] += dot(grads_across, probs.astype(LOW))
            key_sum[:, here] += dot(queries_across, score_grad)
            query_grad += dot(score_grad, key_rows[here, :])

        where = pl.multiple_of(step * size, size)
        out_ref[member, 0, :, pl.ds(start, size)] = turn_back(
            query_grad.T * back, cos_ref[:, pl.ds(where, size)], sin_ref[:, pl.ds(where, size)]
        ).astype(LOW)

        @pl.when(step == length // size - 1)
        def _():
            for source in range(members):
                span = slice(source * tokens, (source + 1) * tokens)
                out_ref[source, 1] = turn_back(
                    key_sum[:, span] * back, cos_ref[:, span], sin_ref[:, span]
                ).astype(LOW)
                out_ref[source, 2] = value_sum[:, span].astype(LOW)

    return call(
        kernel,
        "attend_back",
        ids,
        (length // size,),
        [parts, grads, wide, total, cosines, sines],
        [
            whole(parts.shape),
            pl.BlockSpec((members, HEAD, tokens), lambda i, ids: (0, head, 0)),
            pl.BlockSpec((HEAD, size), lambda i, ids: (0, i)),
            pl.BlockSpec((1, size), lambda i, ids: (0, i)),
            whole(cosines.shape),
            whole(sines.shape),
        ],
        low_array(members, 3, HEAD, tokens),
        whole((members, 3, HEAD, tokens)),
        [
            pltpu.VMEM((length, HEAD), LOW),
            pltpu.VMEM((HEAD, length), WIDE),
            pltpu.VMEM((HEAD, length), WIDE),
        ],
        after,
        time=44,
    )


def joint_back(ids, parts, normed, weight, column, total, core_mask, pairs, after=()):
    members, _, _, tokens = parts.shape
    group = members * HEAD
    width = 3 * group
    quarter = D // (2 * pairs)
    halves = (pairs, quarter, width)
    before = [] if total is None else [total]

    def kernel(ids_ref, part_ref, normed_ref, weight_ref, *refs):
        *total_refs, sent_ref, kept_ref, total_ref, across, lined = refs
        step = pl.program_id(0)

        @pl.when(step == 0)
        def _():
            for member in range(members):
                for kind in range(3):
                    at = kind * group + member * HEAD
                    across[at : at + HEAD, :] = part_ref[member, kind]
            lined[...] = across[...].T

        rows = lined[...]
        put_half(step, pairs, dot(normed_ref[...].T, rows), sent_ref, kept_ref)
        added = contract(rows, weight_ref[...], 1, 1)
        total_ref[...] = total_refs[0][...] + added if total_refs else added

    def at(i, ids):
        return quarter_at(i, ids, core_mask, pairs)

    strip = pl.BlockSpec((tokens, quarter), lambda i, ids: (0, at(i, ids)))
    return call(
        kernel,
        "joint_back",
        ids,
        (2 * pairs,),
        [parts, normed, weight, *before],
        [
            whole(parts.shape),
            strip,
            pl.BlockSpec((quarter, width), lambda i, ids: (at(i, ids), column)),
        ]
        + [strip] * len(before),
        [low_array(*halves), wide_array(*halves), wide_array(tokens, D)],
        half_specs(pairs, quarter, width) + [strip],
        [pltpu.VMEM((width, tokens), LOW), pltpu.VMEM((tokens, width), LOW)],
        after,
        time=10,
    )


def tokens_back(ids, gradient, tokens, middle_grad, early, frames, after=()):
    rows = tokens.shape[1]
    size = rows // frames

    def kernel(
        ids_ref, grad_ref, tokens_ref, middle_ref, early_ref, own_ref, other_ref, pieces_ref
    ):
        normed, inverse = norm_parts(tokens_ref[0].astype(WIDE))
        grad, shift_grad, scale_grad = norm_back(
            grad_ref[...], normed, inverse, piece(early_ref, 1, frames)
        )
        grad = grad + middle_ref[...]
        put_piece(pieces_ref, 0, frames, shift_grad)
        put_piece(pieces_ref, 1, frames, scale_grad)

        @pl.when(pl.program_id(0) == ids_ref[1])
        def _():
            own_ref[...] = grad

        @pl.when(pl.program_id(0) != ids_ref[1])
        def _():
            other_ref[...] = grad.astype(LOW)

    def chunk_at(number):
        def index(r, f, ids):
            mine = ids[1] if number == 0 else 1 - ids[1]
            return (jnp.where(r == mine, f, jnp.where(r < mine, 0, frames - 1)), 0)

        return index

    block = row_spec(rows, frames)
    return call(
        kernel,
        "tokens_back",
        ids,
        (2, frames),
        [gradient, tokens, middle_grad, early],
        [block, chunk_spec(rows, frames), block, whole(early.shape)],
        [wide_array(rows, D), low_array(rows, D), wide_array(2 * frames, 2 * D)],
        [
            pl.BlockSpec((size, D), chunk_at(0)),
            pl.BlockSpec((size, D), chunk_at(1)),
            whole((2 * frames, 2 * D)),
        ],
        after=after,
        time=9,
    )


def two_clips(ids, own, others, kind, frames, after=()):
    rows = others.shape[0]
    size = rows // frames
    if own.ndim == 3:
        own_spec = pl.BlockSpec((1, size, D), lambda r, f, ids: (ids[1], f, 0))
    else:
        own_spec = pl.BlockSpec((size, D), lambda r, f, ids: (f, 0))

    def kernel(ids_ref, own_ref, other_ref, out_ref):
        mine = pl.program_id(0) == ids_ref[1]

        @pl.when(mine)
        def _():
            out_ref[0] = own_ref[...].reshape(size, D).astype(kind)

        @pl.when(jnp.logical_not(mine))
        def _():
            out_ref[0] = other_ref[...].astype(kind)

    return call(
        kernel,
        "two_clips",
        ids,
        (2, frames),
        [own, others],
        [own_spec, pl.BlockSpec((size, D), lambda r, f, ids: (f, 0))],
        jax.ShapeDtypeStruct((2, rows, D), kind),
        chunk_spec(rows, frames),
        after=after,
        time=3,
    )


def modulation_back(ids, condition, pieces, after=()):
    count, width = pieces.shape
    own = condition.shape[1]
    size = 1024

    def kernel(ids_ref, condition_ref, pieces_ref, out_ref, sum_ref):
        pieces = pieces_ref[...]
        out_ref[...] = lax.dot_general(
            condition_ref[...].astype(WIDE).T,
            pieces,
            (((1,), (0,)), ((), ())),
            precision=highest,
            preferred_element_type=WIDE,
        )
        sum_ref[...] = jnp.sum(pieces, axis=0, keepdims=True)

    return call(
        kernel,
        "modulation_back",
        ids,
        (width // size,),
        [condition, pieces],
        [whole(condition.shape), pl.BlockSpec((count, size), lambda i, ids: (0, i))],
        [wide_array(own, width), wide_array(1, width)],
        [
            pl.BlockSpec((own, size), lambda i, ids: (0, i)),
            pl.BlockSpec((1, size), lambda i, ids: (0, i)),
        ],
        after=after,
        time=4,
    )


def join_and_add(ids, joins, adds, after=()):
    ins, outs = [], []
    for own, arrived, _ in joins:
        ins += [own, arrived]
        pre, post, width = own.shape
        outs.append(jax.ShapeDtypeStruct((pre, 2, post, width), own.dtype))
    for kept, arrived, final in adds:
        ins += [kept, arrived]
        rows, width = kept.shape
        outs += [wide_array(rows, width)] if final else [wide_array(rows // 2, width)] * 2

    def kernel(ids_ref, *refs):
        in_refs, out_refs = list(refs[: len(ins)]), list(refs[len(ins) :])
        for _, _, mask in joins:
            own, arrived, out = in_refs.pop(0), in_refs.pop(0), out_refs.pop(0)
            bit = bit_of(ids_ref[2], mask)
            for row in range(own.shape[0]):
                out[row, pl.ds(bit, 1)] = own[row][None]
                out[row, pl.ds(1 - bit, 1)] = arrived[row][None]
        for _, _, final in adds:
            kept, arrived = in_refs.pop(0), in_refs.pop(0)
            rows = kept.shape[0]
            if final:
                out_refs.pop(0)[...] = kept[...] + arrived[...]
            else:
                for start in (0, rows // 2):
                    span = slice(start, start + rows // 2)
                    out_refs.pop(0)[...] = kept[span] + arrived[span]

    return call(
        kernel,
        "join_and_add",
        ids,
        (1,),
        ins,
        [whole(value.shape) for value in ins],
        outs,
        [whole(out.shape) for out in outs],
        after=after,
        time=3,
    )


def stack_rows(ids, first, second, after=()):
    count, width = first.shape

    def kernel(ids_ref, first_ref, second_ref, out_ref):
        out_ref[:count] = first_ref[...]
        out_ref[count:] = second_ref[...]

    return call(
        kernel,
        "stack_rows",
        ids,
        (1,),
        [first, second],
        [whole(first.shape)] * 2,
        wide_array(2 * count, width),
        whole((2 * count, width)),
        after=after,
    )


def pack(ids, down, up, output, after=()):
    count = down.shape[0] + up.shape[0] * (up.shape[1] // D) + output.shape[0]

    def kernel(ids_ref, down_ref, up_ref, output_ref, out_ref):
        at = 0
        pieces = [down_ref[...]]
        pieces += [up_ref[:, i * D : (i + 1) * D] for i in range(up.shape[1] // D)]
        for value in pieces + [output_ref[...]]:
            out_ref[at : at + value.shape[0]] = value.astype(LOW)
            at += value.shape[0]

    return call(
        kernel,
        "pack",
        ids,
        (1,),
        [down, up, output],
        [whole(down.shape), whole(up.shape), whole(output.shape)],
        low_array(count, D),
        whole((count, D)),
        after=after,
        time=3,
    )


def other_clip(ids, tokens, frames, after=()):
    rows = tokens.shape[1]
    size = rows // frames

    def kernel(ids_ref, in_ref, out_ref):
        out_ref[...] = in_ref[0]

    return call(
        kernel,
        "other_clip",
        ids,
        (frames,),
        [tokens],
        [pl.BlockSpec((1, size, D), lambda f, ids: (1 - ids[1], f, 0))],
        low_array(rows, D),
        pl.BlockSpec((size, D), lambda f, ids: (f, 0)),
        after=after,
    )


def copy_of(ids, value, after=()):
    def kernel(ids_ref, in_ref, out_ref):
        out_ref[...] = in_ref[...]

    return call(
        kernel,
        "copy_of",
        ids,
        (1,),
        [value],
        [whole(value.shape)],
        jax.ShapeDtypeStruct(value.shape, value.dtype),
        whole(value.shape),
        after=after,
    )


def halve(ids, jobs, after=()):
    ins, in_specs, outs, out_specs = [], [], [], []
    count = jobs[0][1].shape[0]
    together = min([post or 1 for _, _, post, _ in jobs] + [4])
    steps = max(1, count // 2) // together
    for kept, arrived, post, mask in jobs:
        block = (together,) + arrived.shape[1:]

        def source(i, ids, side, post=post // together, mask=mask):
            if not post:
                return (i, 0, 0)
            bit = bit_of(ids[2], mask)
            return (i // post * 2 * post + (bit if side else 1 - bit) * post + i % post, 0, 0)

        for side in (0, 1) if post else (1,):
            ins += [kept, arrived]
            spec = pl.BlockSpec(
                block, lambda i, ids, side=side, source=source: source(i, ids, side)
            )
            in_specs += [spec, spec]
            kind = LOW if side == 0 else WIDE
            outs.append(jax.ShapeDtypeStruct((max(1, count // 2),) + arrived.shape[1:], kind))
            out_specs.append(pl.BlockSpec(block, lambda i, ids: (i, 0, 0)))

    def kernel(ids_ref, *refs):
        for number, out in enumerate(refs[len(ins) :]):
            value = refs[2 * number][...].astype(WIDE) + refs[2 * number + 1][...].astype(WIDE)
            out[...] = value.astype(out.dtype)

    return call(kernel, "halve", ids, (steps,), ins, in_specs, outs, out_specs, after=after, time=5)


def halve_plain(rank, jobs):
    outs = []
    for kept, arrived, post, mask in jobs:
        value = kept.astype(WIDE) + arrived.astype(WIDE)
        if not post:
            outs.append(value)
            continue
        split = value.reshape((-1, 2, post) + value.shape[1:])
        for side in (1 - bit_of(rank, mask), bit_of(rank, mask)):
            taken = lax.dynamic_index_in_dim(split, side, 1, keepdims=False)
            outs.append(taken.reshape((-1,) + value.shape[1:]))
        outs[-2] = outs[-2].astype(LOW)
    return outs


def per_device(
    clip_size,
    seq_size,
    frames_in,
    noise_level,
    frame_time,
    cotangent,
    joint_weight,
    output_weight,
    up_weight,
    down_weight,
    modulation,
    modulation_bias,
    first_joint,
    first_output,
    first_up,
    first_down,
    first_modulation,
    first_bias,
    second_joint,
    second_output,
    second_up,
    second_down,
    second_modulation,
    second_bias,
):
    devices = clip_size * seq_size
    masters = (joint_weight, output_weight, up_weight, down_weight, modulation, modulation_bias)
    firsts = (first_joint, first_output, first_up, first_down, first_modulation, first_bias)
    seconds = (second_joint, second_output, second_up, second_down, second_modulation, second_bias)
    clip_id, seq_id = lax.axis_index("clip"), lax.axis_index("seq")
    rank = clip_id * seq_size + seq_id
    half = seq_size // 2
    side = seq_id // half
    members = half
    ids = jnp.stack([seq_id % half, side, rank]).astype(jnp.int32)
    head_count = HEADS // members
    group_ids = [[i * half + j for j in range(half)] for i in range(2)]
    last = []

    def swap_with(value, mask):
        return lax.ppermute(value, AXES, [(i, i ^ mask) for i in range(devices)])

    def pick(value, index):
        return lax.dynamic_index_in_dim(value, index, 0, keepdims=False)

    def run(kernel, *args, **options):
        result = kernel(ids, *args, after=tuple(last), **options)
        last[:] = jax.tree.leaves(result)[:1]
        return result

    clip_masks = [seq_size << bit for bit in range(clip_size.bit_length() - 1)]
    seq_masks = [1 << bit for bit in range(seq_size.bit_length() - 1)]
    order = clip_masks + seq_masks
    core_mask = clip_masks[0]
    pairs = clip_size // 2

    local_rows = frames_in.shape[1]
    frames = max(1, local_rows // PATCHES)
    tokens_here = 2 * local_rows
    pair_ids = [[j, j + half] for j in range(half)]
    tokens = lax.all_to_all(frames_in, "seq", 0, 0, axis_index_groups=pair_ids)

    levels = noise_level.astype(WIDE)[None]
    for mask in clip_masks:
        levels = jnp.concatenate([levels, swap_with(levels, mask)], axis=0)
    all_levels = levels.reshape(-1)
    masks = [0]
    for mask in reversed(order):
        masks = masks + [other ^ mask for other in masks]
    own_width = modulation.shape[0]
    columns = rank * own_width + jnp.arange(own_width, dtype=jnp.int32)
    half_width = D // 2
    frequency = jnp.exp(-math.log(10000.0) * (columns % half_width).astype(WIDE) / half_width)

    def condition_of(targets):
        seq_of = targets % seq_size
        chunk = jnp.stack([seq_of % half, seq_of % half + half], axis=1)
        frame_of = chunk[:, :, None] * local_rows // PATCHES + jnp.arange(frames, dtype=jnp.int32)
        clip_of = (targets // seq_size ^ clip_id) * 2 + seq_of // half
        level_ids = (clip_of[:, None, None] * FRAMES + frame_of).reshape(-1)
        every = jnp.arange(all_levels.shape[0], dtype=jnp.int32)
        level_of = jnp.sum(jnp.where(level_ids[:, None] == every, all_levels, 0.0), axis=1)
        angles = level_of[:, None] * frequency
        wave = jnp.where(columns < half_width, jnp.cos(angles), jnp.sin(angles))
        return jax.nn.silu(wave).astype(LOW)

    condition = condition_of(rank ^ jnp.array(masks, jnp.int32))

    bias_width = modulation_bias.shape[0]
    bias_row = lax.dynamic_update_slice_in_dim(
        jnp.zeros((6 * D,), WIDE), modulation_bias.astype(LOW).astype(WIDE), rank * bias_width, 0
    )
    modulation_low = modulation.astype(LOW)

    class Terms:
        def __init__(self, condition, first, stop):
            terms = dot(condition, modulation_low[:, first:stop]) + bias_row[first:stop]
            middle = terms.shape[0] // 2
            self.kept, self.sent = terms[:middle], terms[middle:]
            self.masks = order[:]
            self.send()

        def send(self):
            self.arrived = swap_with(self.sent, self.masks.pop(0))

        def job(self):
            return (self.kept, self.arrived, not self.masks)

        def take(self, outs):
            self.kept = outs.pop(0)
            if self.masks:
                self.sent = outs.pop(0)
                self.send()

    rows = joint_weight.shape[0]
    joint_low = joint_weight.astype(LOW).reshape(rows, 3, members, head_count, HEAD)
    joint_low = jnp.transpose(joint_low, (0, 3, 1, 2, 4)).reshape(1, rows, 3 * D)
    far = seq_masks[:0:-1]
    routes = [
        far + [seq_masks[0]] + clip_masks[::-1],
        far + clip_masks[:0:-1] + [seq_masks[0], clip_masks[0]],
    ]
    joined = [joint_low]
    early_terms = None
    for stage in range(len(order) + 1):
        joins = []
        if stage < len(order):
            if stage == len(far):
                middle_column = joint_low.shape[2] // 2
                joined = [joined[0][..., :middle_column], joined[0][..., middle_column:]]
            for value, route in zip(joined, routes):
                mask, done = route[stage], route[:stage]
                pre = 2 ** sum(1 for other in done if other > mask)
                width = value.shape[-1]
                own = value.reshape(pre, -1, width)
                arrived = swap_with(value, mask).reshape(pre, -1, width)
                joins.append((own, arrived, mask))
        if stage == 1:
            early_terms = Terms(condition, 0, 2 * D)
        adds = [early_terms.job()] if stage else []
        if stage == 3:
            last.append(tokens)
        outs = list(run(join_and_add, joins, adds))
        if stage < len(order):
            joined = [outs.pop(0) for _ in joins]
            joined = [value.reshape(1, -1, value.shape[-1]) for value in joined]
        if stage:
            early_terms.take(outs)
    early = early_terms.kept
    joint_sides = [value[0] for value in joined]
    if head_count % 2:
        joint_sides = [jnp.concatenate(joint_sides, axis=1)]
    heads_aside = head_count // len(joint_sides)

    up_blocks = FF // D
    own_up = up_weight.shape[0]
    own_down = down_weight.shape[0]
    tiled = own_up % 16 == 0
    packed = run(pack, down_weight, up_weight, output_weight)
    packed = lax.all_gather(packed, AXES, axis=0, tiled=False)
    chunk_rows = 512
    up_first = own_down // own_up
    if tiled:
        chunks_aside = D // chunk_rows
        up_source = (
            packed,
            (devices, own_up, chunk_rows),
            lambda at: (0, up_first + at // chunks_aside, at % chunks_aside),
        )
        output_source = (
            packed,
            pl.BlockSpec((devices, own_up, D), lambda *at: (0, up_first + up_blocks, 0)),
        )
    else:
        upward = packed[:, own_down : own_down + own_up * up_blocks]
        upward = jnp.transpose(
            upward.reshape(devices, up_blocks, own_up, D), (0, 2, 1, 3)
        ).reshape(1, D, FF)
        up_source = (upward, (1, D, chunk_rows), lambda at: (0, 0, at))
        output_full = packed[:, own_down + own_up * up_blocks :].reshape(1, D, D)
        output_source = (output_full, whole((1, D, D)))
    down_source = (packed, (chunk_rows // own_down, own_down, D), lambda at: (at, 0, 0))

    member_seq = side * half + jnp.arange(members, dtype=jnp.int32)
    starts = jnp.stack([member_seq % half, member_seq % half + half], axis=1) * local_rows
    places = (starts[:, :, None] + jnp.arange(local_rows, dtype=jnp.int32)).reshape(-1)
    cosines, sines = rotary_tables(pick(frame_time, side), places)

    normed_one_low = run(norm_one, tokens, early, frames)

    def exchange(value):
        return lax.all_to_all(value, "seq", 0, 0, axis_index_groups=group_ids)

    late_terms = Terms(run(copy_of, condition), 2 * D, 6 * D)

    def late_step():
        if late_terms.masks or late_terms.arrived is not None:
            final = not late_terms.masks
            outs = list(run(join_and_add, [], [late_terms.job()]))
            late_terms.take(outs)
            if final:
                late_terms.arrived = None

    def project_head(head):
        weight, offset = joint_sides[head // heads_aside], head % heads_aside
        return exchange(
            run(project, normed_one_low, weight, cosines, sines, members, offset)
        )

    parts = {0: project_head(0)}
    late_step()
    upstream = (cotangent, swap_with(run(other_clip, cotangent, frames), half))
    wide, totals = {}, {}
    front = None
    front_heads = head_count - 1
    for head in range(head_count):
        if head + 1 < head_count:
            parts[head + 1] = project_head(head + 1)
            late_step()
        else:
            last.append(upstream[1])
        if head < front_heads:
            front, wide[head], totals[head] = run(attend, parts[head], front, head, front_heads)
            if head + 1 == front_heads:
                front = exchange(front)
        else:
            back, wide[head], totals[head] = run(attend, parts[head], None, 0, 1)
        late_step()
    while late_terms.arrived is not None:
        late_step()
    late = late_terms.kept
    back = exchange(back)

    attended_low, projected, middle, normed_two_low, branch_grad = run(
        middle_part,
        [back] if front is None else [front, back],
        members,
        output_source,
        tokens,
        upstream,
        late,
        frames,
    )
    branch, normed_two_grad, down_sent, down_kept, up_sent, up_kept = run(
        feed,
        normed_two_low,
        branch_grad,
        up_source,
        down_source,
        FF,
        devices,
        core_mask,
        pairs,
    )

    class Chain:
        def __init__(self, sent, kept, masks):
            self.kept, self.masks = kept, list(masks)
            self.remaining = sorted(self.masks)
            self.arrived = swap_with(sent.astype(LOW), core_mask)

        def job(self):
            if not self.masks:
                return (self.kept, self.arrived, 0, 1)
            post = 2 ** self.remaining.index(self.masks[0])
            return (self.kept, self.arrived, post, self.masks[0])

        def take(self, outs):
            if self.masks:
                mask = self.masks.pop(0)
                self.remaining.remove(mask)
                self.arrived, self.kept = swap_with(outs.pop(0), mask), outs.pop(0)
            else:
                self.arrived, self.kept = None, outs.pop(0)

    def step(*chains):
        chains = [chain for chain in chains if chain.arrived is not None]
        if not chains:
            return
        jobs = [chain.job() for chain in chains]
        outs = list(run(halve, jobs)) if tiled else halve_plain(rank, jobs)
        for chain in chains:
            chain.take(outs)

    def owners(value):
        return value.reshape(devices // 2, -1, value.shape[2])

    one_way = clip_masks[1:] + seq_masks
    other_way = seq_masks[:1] + clip_masks[1:] + seq_masks[1:]
    up_shape = (devices // 2, up_blocks * own_up, D)
    down_chain = Chain(down_sent, down_kept, one_way)
    up_chain = Chain(up_sent.reshape(up_shape), up_kept.reshape(up_shape), other_way)

    result, middle_grad, projected_grad, late_rows = run(
        middle_back, middle, branch, normed_two_grad, projected, upstream, late, frames
    )
    *outer, output_sent, output_kept = run(
        hand_out,
        output_source,
        projected_grad,
        attended_low,
        members,
        head_count,
        core_mask,
        pairs,
    )
    outer_back = exchange(outer[0])
    output_chain = Chain(owners(output_sent), owners(output_kept), one_way)
    step(down_chain, up_chain)
    last.append(outer_back)
    late_pieces = lax.all_gather(late_rows, AXES, axis=0, tiled=True)

    class Frames:
        def __init__(self, rows):
            self.rows, self.masks = rows, order[::-1]
            self.send()

        def send(self):
            self.arrived = swap_with(self.rows, self.masks.pop(0)) if self.masks else None

        def step(self):
            if self.arrived is not None:
                self.rows = run(stack_rows, self.rows, self.arrived)
                self.send()

    def head_back(head):
        grads, at = (outer_front, head) if head < front_heads else (outer_back, 0)
        return run(
            attend_back, parts[head], grads, at, wide[head], totals[head], cosines, sines
        )

    def head_joint(head, total):
        weight, offset = joint_sides[head // heads_aside], head % heads_aside
        sent, kept, total = run(
            joint_back,
            joint_parts[head],
            normed_one_low,
            weight,
            offset,
            total,
            core_mask,
            pairs,
        )
        return owners(sent), owners(kept), total

    joint_parts, head_chains = {}, {}
    total = None
    outer_front = exchange(outer[1]) if front_heads else None
    heads = list(reversed(range(head_count)))
    ready = []
    for number, head in enumerate(heads):
        raw = head_back(head)
        joint_parts[head] = exchange(raw)
        if number == 0:
            other_rows = pick(result, 1 - side)
            if head_count > 1:
                other_rows = run(copy_of, other_rows)
            others = swap_with(other_rows, half)
        if number == min(2, head_count - 1):
            mixed = run(two_clips, result, others, LOW, frames)
        step(down_chain, up_chain)
        step(output_chain)
        if number == 2:
            for other in heads[:2]:
                sent, kept, total = head_joint(other, total)
                head_chains[other] = Chain(sent, kept, other_way if other % 2 else one_way)
            mod_late, sum_late = run(
                modulation_back, condition_of(jnp.arange(devices, dtype=jnp.int32)), late_pieces
            )
            step(*head_chains.values())
    early_chains = list(head_chains.values())
    late_chains = []
    waiting = [head for head in heads if head not in head_chains]
    for head in waiting:
        sent, kept, total = head_joint(head, total)
        head_chains[head] = Chain(sent, kept, other_way if head % 2 else one_way)
        late_chains.append(head_chains[head])
        step(*early_chains)
    own_rows, other_rows, early_rows = run(
        tokens_back, total, tokens, middle_grad, early, frames
    )
    early_frames = Frames(early_rows)
    others = swap_with(other_rows, half)
    chains = late_chains + early_chains + [up_chain, output_chain, down_chain]
    while any(chain.arrived is not None for chain in chains) or early_frames.arrived is not None:
        step(*late_chains)
        early_frames.step()
        step(*early_chains)
        step(down_chain, up_chain)
        step(output_chain)
    if head_count < 3:
        mod_late, sum_late = run(
            modulation_back, condition_of(jnp.arange(devices, dtype=jnp.int32)), late_pieces
        )
    mod_early, sum_early = run(modulation_back, condition, early_frames.rows)
    input_grad = run(two_clips, own_rows, others, WIDE, frames)

    output_sum = output_chain.kept[0]
    down_sum = down_chain.kept[0]
    up_sum = up_chain.kept[0].reshape(up_blocks, own_up, D)
    up_sum = jnp.transpose(up_sum, (1, 0, 2)).reshape(own_up, FF)
    joint_sum = jnp.stack([head_chains[head].kept[0] for head in range(head_count)], axis=1)
    joint_sum = joint_sum.reshape(rows, head_count, 3, members, HEAD)
    joint_sum = jnp.transpose(joint_sum, (0, 2, 3, 1, 4)).reshape(rows, 3 * D)
    mod_sum = jnp.concatenate([mod_early, mod_late], axis=1)
    bias_sum = lax.dynamic_slice_in_dim(
        jnp.concatenate([sum_early[0], sum_late[0]]), rank * bias_width, bias_width, 0
    )

    summed = (joint_sum, output_sum, up_sum, down_sum, mod_sum, bias_sum)
    squares = sum(jnp.sum(shard * shard) for shard in summed).reshape(1, 1)
    for mask in order:
        squares = squares + swap_with(squares, mask)
    grad_norm = jnp.sqrt(squares[0, 0])
    factor = jnp.minimum(1.0, clip_limit / (grad_norm + 1e-06))
    step_rates = (
        D ** (-0.5),
        max(1, 2 * D // LENGTH) ** (-0.5),
        D ** (-0.5),
        FF ** (-0.5),
        D ** (-0.5),
        0.5,
    )
    clipped = [shard * factor for shard in summed]
    updates = [
        adam_update(clipped[slot], masters[slot], firsts[slot], seconds[slot], step_rates[slot])
        for slot in range(6)
    ]
    return (
        mixed,
        input_grad,
        *clipped,
        grad_norm,
        *(update[0] for update in updates),
        *(update[1] for update in updates),
        *(update[2] for update in updates),
        *(update[2].astype(LOW) for update in updates),
    )


def solution(mesh):
    tokens = P("clip", "seq", None)
    rows = P(AXES, None)
    weights = (rows, rows, rows, rows, rows, P(AXES))
    in_specs = (tokens, P("clip", None), P("clip", None), tokens) + weights * 3
    out_specs = (tokens, tokens) + weights + (P(),) + weights * 4
    return jax.shard_map(
        partial(per_device, mesh.shape["clip"], mesh.shape["seq"]),
        mesh=mesh,
        in_specs=in_specs,
        out_specs=out_specs,
        check_vma=False,
    )
```

time: 1160 us -> 1030 us (0.89)
  Pallas kernels: 281 us -> 632 us
  waiting for transfers between devices: 360 us -> 127 us
  matrix products: 144 us -> 1.76 us
  local copies, waits for them, and re-layouts: 131 us -> 41.6 us
  other arithmetic: 96.1 us -> 23.6 us
  starting transfers between devices: 109 us -> 143 us
  blocking collectives: 0 us -> 29 us
    pallas_call x6 -> x66, Pallas kernels: 281 us -> 632 us  [call(): pl.pallas_call(body, grid_spec=pltpu.PrefetchScalarGridSpec(num_scalar_pr...]
    ppermute x88 -> x68, waiting for transfers between devices: 356 us -> 107 us  [swap_with(): return lax.ppermute(value, AXES, [(i, i ^ mask) for i in range(devices)])]
    dot_general x9 -> x0, matrix products: 105 us -> none  [the longest x8 102 us: contract(): lax.dot_general(left, right, (((left_dim,), (right_dim,)), ((), ())), pre...]
    all_to_all x0 -> x11, starting transfers between devices: none -> 47.9 us  [the longest x10 43.2 us: exchange(): return lax.all_to_all(value, 'seq', 0, 0, axis_index_groups=group_ids)]
    slice x21 -> x5, local copies, waits for them, and re-layouts: 42.3 us -> 3.19 us  [the longest x2 2.02 us: __init__(): self.kept, self.sent = (terms[:middle], terms[middle:])]
    dot_general x5 -> x2, matrix products: 38.9 us -> 1.76 us  [dot(): return jnp.dot(left, right, preferred_element_type=WIDE)]
    add x51 -> x2, other arithmetic: 29.9 us -> 0.26 us  [condition_of(): level_ids = (clip_of[:, None, None] * FRAMES + frame_of).reshape(-1)]
    all_to_all x0 -> x2, blocking collectives: none -> 29 us  [exchange(): return lax.all_to_all(value, 'seq', 0, 0, axis_index_groups=group_ids)]
  transfers between devices with their start and end apart: 92 -> 81, of which waited for: 40 -> 19; matrix products, arithmetic and copies ran while one was open for 23% -> 3% of each run, Pallas kernels for 24% -> 53%
where the time goes in v2:
time: 1030 us; the launch traced here: 1020 us
  Pallas kernels  632 us (61%)
  starting transfers between devices  143 us (14%)
  waiting for transfers between devices  127 us (12%)
  local copies, waits for them, and re-layouts  41.6 us (4%)
  blocking collectives  29 us (3%)
  between operations  23.7 us (2%)
  other arithmetic  23.6 us (2%)
    pallas_call x66, Pallas kernels, call(): pl.pallas_call(body, grid_spec=pltpu.PrefetchScalarGridSpec(num_scalar_pr...  632 us
    ppermute x68, waiting for transfers between devices, swap_with(): return lax.ppermute(value, AXES, [(i, i ^ mask) for i in range(devices)])  107 us
    ppermute x68, starting transfers between devices, swap_with(): return lax.ppermute(value, AXES, [(i, i ^ mask) for i in range(devices)])  94.8 us
    all_to_all x10, starting transfers between devices, exchange(): return lax.all_to_all(value, 'seq', 0, 0, axis_index_groups=group_ids)  43.2 us
    unnamed x194, local copies, waits for them, and re-layouts  30.8 us
    all_to_all x2, blocking collectives, exchange(): return lax.all_to_all(value, 'seq', 0, 0, axis_index_groups=group_ids)  29 us
  transfers between devices with their start and end apart: 81, of which 19 were waited for; matrix products, arithmetic and copies ran while one was open for 3% of the time, Pallas kernels for 53%

profile of v2, /device:TPU:0, one launch (start us, length us, event | category | flops | bytes accessed | tf_op | source)
XLA Modules:
  0.0 1021.7 jit_solution(10795387443130423907)
XLA Ops:
  32.2 10.2 %collective-permute-done.1 = bf16[1,64,3072]{2,1,0:T(8,128)(2,1)S(1)} collective-permute-done((bf16[1,64,3072]{2,1,0:T(8,128)(2,1)}, bf16[1,64,3072]{2,1,0:T(8,128)(2,1)S(1)}, u32[]{:S(2)}, u32[]{:S(2)}) %collective-permute-start.1) | collective-permute-done | bytes 393248 | tf_op jit(solution)/shard_map/ppermute | solution.py:1100
  51.0 12.3 %collective-permute-done.7.refs_6_ = f32[32,2048]{1,0:T(8,128)S(1)} collective-permute-done((f32[32,2048]{1,0:T(8,128)}, f32[32,2048]{1,0:T(8,128)S(1)}, u32[]{:S(2)}, u32[]{:S(2)}) %collective-permute-start.7) | collective-permute-done | bytes 262176 | tf_op jit(solution)/shard_map/ppermute | solution.py:1100
  70.9 17.5 %collective-permute-done.10.refs_6_ = f32[16,2048]{1,0:T(8,128)S(1)} collective-permute-done((f32[16,2048]{1,0:T(8,128)}, f32[16,2048]{1,0:T(8,128)S(1)}, u32[]{:S(2)}, u32[]{:S(2)}) %collective-permute-start.10) | collective-permute-done | bytes 131104 | tf_op jit(solution)/shard_map/ppermute | solution.py:1100
  160.8 8.9 collective-permute-done.16.refs_2_
  175.3 19.6 %all-to-all-done.1.refs_1_ = bf16[4,3,64,1024]{3,2,1,0:T(8,128)(2,1)S(1)} async-done(((bf16[4,3,64,1024]{3,2,1,0:T(8,128)(2,1)}), bf16[4,3,64,1024]{3,2,1,0:T(8,128)(2,1)S(1)}, u32[]{:S(2)}, u32[]{:S(2)}) %all-to-all-start.1) | async-done | bytes 1572896 | tf_op jit(solution)/shard_map/all_to_all | solution.py:1251
  198.7 26.6 %attend.4 = (bf16[4,192,1024]{2,1,0:T(8,128)(2,1)}, f32[64,4096]{1,0:T(8,128)}, f32[1,4096]{1,0:T(1,128)}) custom-call(s32[3]{0:T(128)} %pad_add_fusion.refs_0_, bf16[4,3,64,1024]{3,2,1,0:T(8,128)(2,1)} %copy-done.9, f32[16,4096]{1,0:T(8,128)} %get-tuple-element.185.refs_2_.refs_1_), custom_call_target="tpu_custom_call" | custom-call | flops 29899999232 | bytes 78000000 | tf_op jit(solution)/shard_map/attend/pallas_call | solution.py:116
  236.7 21.4 %collective-permute-done.18.refs_2_ = f32[8,4096]{1,0:T(8,128)S(1)} collective-permute-done((f32[8,4096]{1,0:T(8,128)}, f32[8,4096]{1,0:T(8,128)S(1)}, u32[]{:S(2)}, u32[]{:S(2)}) %collective-permute-start.18) | collective-permute-done | bytes 131104 | tf_op jit(solution)/shard_map/ppermute | solution.py:1100
  267.8 26.6 %attend.5 = (bf16[4,192,1024]{2,1,0:T(8,128)(2,1)}, f32[64,4096]{1,0:T(8,128)}, f32[1,4096]{1,0:T(1,128)}) custom-call(s32[3]{0:T(128)} %pad_add_fusion.refs_0_, bf16[4,3,64,1024]{3,2,1,0:T(8,128)(2,1)} %copy-done.10, bf16[4,192,1024]{2,1,0:T(8,128)(2,1)} %get-tuple-element.187.refs_3_.refs_2_, ...), custom_call_target="tpu_custom_call", output_to_operand_aliasing={{0}: (2, {})} | custom-call | flops 29899999232 | bytes 78000000 | tf_op jit(solution)/shard_map/attend/pallas_call | solution.py:116
  308.3 26.7 %attend.6 = (bf16[4,192,1024]{2,1,0:T(8,128)(2,1)}, f32[64,4096]{1,0:T(8,128)}, f32[1,4096]{1,0:T(1,128)}) custom-call(s32[3]{0:T(128)} %pad_add_fusion.refs_0_, bf16[4,3,64,1024]{3,2,1,0:T(8,128)(2,1)} %copy-done.11, bf16[4,192,1024]{2,1,0:T(8,128)(2,1)} %get-tuple-element.191.refs_3_.refs_2_, ...), custom_call_target="tpu_custom_call", output_to_operand_aliasing={{0}: (2, {})} | custom-call | flops 29899999232 | bytes 78000000 | tf_op jit(solution)/shard_map/attend/pallas_call | solution.py:116
  336.2 26.7 %attend.7 = (bf16[4,64,1024]{2,1,0:T(8,128)(2,1)}, f32[64,4096]{1,0:T(8,128)}, f32[1,4096]{1,0:T(1,128)}) custom-call(s32[3]{0:T(128)} %pad_add_fusion.refs_0_, bf16[4,3,64,1024]{3,2,1,0:T(8,128)(2,1)} %copy-done.12, bf16[4,192,1024]{2,1,0:T(8,128)(2,1)} %get-tuple-element.193.refs_2_, bf16[512,1024]{1,0:T(8,128)(2,1)} %collective-permute-done.20.refs_3_.refs_6_), custom_call_target="tpu_custom_call" | custom-call | flops 29899999232 | bytes 78000000 | tf_op jit(solution)/shard_map/attend/pallas_call | solution.py:116
  362.9 11.4 %all_to_all.65.refs_2_ = bf16[4,64,1024]{2,1,0:T(8,128)(2,1)} all-to-all(bf16[4,64,1024]{2,1,0:T(8,128)(2,1)} %get-tuple-element.194.refs_8_), channel_id=1, replica_groups={{0,1,2,3},{4,5,6,7},{8,9,10,11},{12,13,14,15},{16,17,18,19},{20,21,22,2..., dimensions={0} | all-to-all | bytes 1048576 | tf_op jit(solution)/shard_map/all_to_all | solution.py:1251
  374.3 17.6 %all_to_all.66.refs_1_ = bf16[4,192,1024]{2,1,0:T(8,128)(2,1)} all-to-all(bf16[4,192,1024]{2,1,0:T(8,128)(2,1)S(1)} %copy-done.16), channel_id=1, replica_groups={{0,1,2,3},{4,5,6,7},{8,9,10,11},{12,13,14,15},{16,17,18,19},{20,21,22,2..., dimensions={0} | all-to-all | bytes 3145728 | tf_op jit(solution)/shard_map/all_to_all | solution.py:1251
  392.0 11.4 %middle_part.1 = (bf16[1024,1024]{1,0:T(8,128)(2,1)}, f32[1024,1024]{1,0:T(8,128)}, f32[1024,1024]{1,0:T(8,128)}, bf16[1024,1024]{1,0:T(8,128)(2,1)}, bf16[1024,1024]{1,0:T(8,128)(2,1)}) custom-call(s32[3]{0:T(128)} %pad_add_fusion.refs_0_, bf16[4,192,1024]{2,1,0:T(8,128)(2,1)} %all_to_all.66.refs_1_, bf16[4,64,1024]{2,1,0:T(8,128)(2,1)} %all_to_all.65.refs_2_, ...), custom_call_target="tpu_custom_call" | custom-call | flops 13799999488 | bytes 36000000 | tf_op jit(solution)/shard_map/middle_part/pallas_call | solution.py:116
  403.4 68.7 %feed.1 = (f32[1024,1024]{1,0:T(8,128)}, f32[1024,1024]{1,0:T(8,128)}, bf16[16,128,1024]{2,1,0:T(8,128)(2,1)}, bf16[16,128,1024]{2,1,0:T(8,128)(2,1)}, bf16[16,4...) custom-call(s32[3]{0:T(128)} %pad_add_fusion.refs_0_, bf16[1024,1024]{1,0:T(8,128)(2,1)} %get-tuple-element.196.refs_1_, ...), custom_call_target="tpu_custom_call" | custom-call | flops 75900002304 | bytes 198000000 | tf_op jit(solution)/shard_map/feed/pallas_call | solution.py:116
  472.7 13.1 %middle_back.1 = (bf16[2,512,1024]{2,1,0:T(8,128)(2,1)}, f32[1024,1024]{1,0:T(8,128)}, bf16[1024,1024]{1,0:T(8,128)(2,1)}, f32[4,4096]{1,0:T(4,128)}) custom-call(s32[3]{0:T(128)} %pad_add_fusion.refs_0_, f32[1024,1024]{1,0:T(8,128)} %get-tuple-element.195.refs_1_, f32[1024,1024]{1,0:T(8,128)} %get-tuple-element.199.refs_2_.refs_8_, ...), custom_call_target="tpu_custom_call" | custom-call | flops 13799999488 | bytes 36000000 | tf_op jit(solution)/shard_map/middle_back/pallas_call | solution.py:116
  485.8 10.4 %hand_out.1 = (bf16[4,64,1024]{2,1,0:T(8,128)(2,1)}, bf16[4,192,1024]{2,1,0:T(8,128)(2,1)}, bf16[2,256,1024]{2,1,0:T(8,128)(2,1)}, f32[2,256,1024]{2,1,0:T(8,128)}) custom-call(s32[3]{0:T(128)} %pad_add_fusion.refs_0_, bf16[32,288,1024]{2,1,0:T(8,128)(2,1)} %bitcast.84, bf16[1024,1024]{1,0:T(8,128)(2,1)} %get-tuple-element.203.refs_2_, ...), custom_call_target="tpu_custom_call" | custom-call | flops 11500000256 | bytes 30000000 | tf_op jit(solution)/shard_map/hand_out/pallas_call | solution.py:116
  501.5 12.7 %halve.20 = (bf16[8,128,1024]{2,1,0:T(8,128)(2,1)}, f32[8,128,1024]{2,1,0:T(8,128)}, bf16[8,128,1024]{2,1,0:T(8,128)(2,1)}, f32[8,128,1024]{2,1,0:T(8,128)}) custom-call(s32[3]{0:T(128)} %pad_add_fusion.refs_0_, bf16[16,128,1024]{2,1,0:T(8,128)(2,1)} %get-tuple-element.207.refs_1_.refs_3_, bf16[16,128,1024]{2,1,0:T(8,128)(2,1)} %collective-permute-done.21.refs_2_.refs_4_, ...), custom_call_target="tpu_custom_call" | custom-call | flops 5750000128 | bytes 15000000 | tf_op jit(solution)/shard_map/halve/pallas_call | solution.py:116
  516.3 7.7 collective-permute-start.25
  528.6 44.4 %attend_back.4.refs_2_ = bf16[4,3,64,1024]{3,2,1,0:T(8,128)(2,1)} custom-call(s32[3]{0:T(128)} %pad_add_fusion.refs_0_, bf16[4,3,64,1024]{3,2,1,0:T(8,128)(2,1)} %copy-done.12, bf16[4,64,1024]{2,1,0:T(8,128)(2,1)} %copy-done.27, f32[64,4096]{1,0:T(8,128)} %get-tuple-element.205.refs_3_, f32[1,4096]{1,0:T(1,128)} %get-tuple-element.206.refs_4_, ...), custom_call_target="tpu_custom_call" | custom-call | flops 50600001536 | bytes 132000000 | tf_op jit(solution)/shard_map/attend_back/pallas_call | solution.py:116
  577.9 8.0 halve.21
  591.3 7.2 collective-permute-start.27
  602.7 44.5 %attend_back.5.refs_9_ = bf16[4,3,64,1024]{3,2,1,0:T(8,128)(2,1)} custom-call(s32[3]{0:T(128)} %pad_add_fusion.refs_0_, bf16[4,3,64,1024]{3,2,1,0:T(8,128)(2,1)} %copy-done.11, bf16[4,192,1024]{2,1,0:T(8,128)(2,1)} %all-to-all-done.8.refs_2_, f32[64,4096]{1,0:T(8,128)} %get-tuple-element.226.refs_3_, f32[1,4096]{1,0:T(1,128)} %get-tuple-element.227.refs_4_, ...), custom_call_target="tpu_custom_call" | custom-call | flops 50600001536 | bytes 132000000 | tf_op jit(solution)/shard_map/attend_back/pallas_call | solution.py:116
  662.0 44.6 %attend_back.6.refs_3_ = bf16[4,3,64,1024]{3,2,1,0:T(8,128)(2,1)} custom-call(s32[3]{0:T(128)} %pad_add_fusion.refs_0_, bf16[4,3,64,1024]{3,2,1,0:T(8,128)(2,1)} %copy-done.10, bf16[4,192,1024]{2,1,0:T(8,128)(2,1)} %all-to-all-done.8.refs_2_, f32[64,4096]{1,0:T(8,128)} %get-tuple-element.213.refs_3_, f32[1,4096]{1,0:T(1,128)} %get-tuple-element.214.refs_4_, ...), custom_call_target="tpu_custom_call" | custom-call | flops 50600001536 | bytes 132000000 | tf_op jit(solution)/shard_map/attend_back/pallas_call | solution.py:116
  722.1 10.1 joint_back.4
  733.4 10.9 %joint_back.5 = (bf16[2,256,768]{2,1,0:T(8,128)(2,1)}, f32[2,256,768]{2,1,0:T(8,128)}, f32[1024,1024]{1,0:T(8,128)}) custom-call(s32[3]{0:T(128)} %pad_add_fusion.refs_0_, bf16[4,3,64,1024]{3,2,1,0:T(8,128)(2,1)} %copy-done.15, bf16[1024,1024]{1,0:T(8,128)(2,1)} %norm_one.1.refs_2_.refs_1_, bf16[1024,1536]{1,0:T(8,128)(2,1)} %bitcast.113, ...), custom_call_target="tpu_custom_call" | custom-call | flops 11500000256 | bytes 30000000 | tf_op jit(solution)/shard_map/joint_back/pallas_call | solution.py:116
  763.4 7.0 halve.27
  771.9 44.4 %attend_back.7.refs_5_ = bf16[4,3,64,1024]{3,2,1,0:T(8,128)(2,1)} custom-call(s32[3]{0:T(128)} %pad_add_fusion.refs_0_, bf16[4,3,64,1024]{3,2,1,0:T(8,128)(2,1)} %copy-done.9, bf16[4,192,1024]{2,1,0:T(8,128)(2,1)} %all-to-all-done.8.refs_2_, f32[64,4096]{1,0:T(8,128)} %get-tuple-element.230.refs_3_, f32[1,4096]{1,0:T(1,128)} %get-tuple-element.231.refs_4_, ...), custom_call_target="tpu_custom_call" | custom-call | flops 50600001536 | bytes 132000000 | tf_op jit(solution)/shard_map/attend_back/pallas_call | solution.py:116
  831.0 10.9 %joint_back.6 = (bf16[2,256,768]{2,1,0:T(8,128)(2,1)}, f32[2,256,768]{2,1,0:T(8,128)}, f32[1024,1024]{1,0:T(8,128)}) custom-call(s32[3]{0:T(128)} %pad_add_fusion.refs_0_, bf16[4,3,64,1024]{3,2,1,0:T(8,128)(2,1)} %copy-done.13, bf16[1024,1024]{1,0:T(8,128)(2,1)} %norm_one.1.refs_2_.refs_1_, bf16[1024,1536]{1,0:T(8,128)(2,1)} %bitcast.108, ...), custom_call_target="tpu_custom_call" | custom-call | flops 11500000256 | bytes 30000000 | tf_op jit(solution)/shard_map/joint_back/pallas_call | solution.py:116
  849.3 11.0 %joint_back.7 = (bf16[2,256,768]{2,1,0:T(8,128)(2,1)}, f32[2,256,768]{2,1,0:T(8,128)}, f32[1024,1024]{1,0:T(8,128)}) custom-call(s32[3]{0:T(128)} %pad_add_fusion.refs_0_, bf16[4,3,64,1024]{3,2,1,0:T(8,128)(2,1)} %all-to-all-done.11.refs_1_, bf16[1024,1024]{1,0:T(8,128)(2,1)} %norm_one.1.refs_2_.refs_1_, bf16[1024,1536]{1,0:T(8,128)(2,1)} %bitcast.109, ...), custom_call_target="tpu_custom_call" | custom-call | flops 11500000256 | bytes 30000000 | tf_op jit(solution)/shard_map/joint_back/pallas_call | solution.py:116
  865.5 8.5 tokens_back.1
  878.2 7.0 halve.32
  917.3 12.8 %collective-permute-done.56.refs_4_ = bf16[1,32,768]{2,1,0:T(8,128)(2,1)S(1)} collective-permute-done((bf16[1,32,768]{2,1,0:T(8,128)(2,1)S(1)}, bf16[1,32,768]{2,1,0:T(8,128)(2,1)S(1)}, u32[]{:S(2)}, u32[]{:S(2)}) %collective-permute-start.56) | collective-permute-done | bytes 49184 | tf_op jit(solution)/shard_map/ppermute | solution.py:1100
  (461 shorter events, 376.7 us)
Async XLA Ops:
  27.6 61.8 %all-to-all-start = ((bf16[2,512,1024]{2,1,0:T(8,128)(2,1)}), bf16[2,512,1024]{2,1,0:T(8,128)(2,1)S(1)}, u32[]{:S(2)}, u32[]{:S(2)}) async-start(bf16[2,512,1024]{2,1,0:T(8,128)(2,1)} %param.23), calls=%async_computation | async-start | bytes 4194304 | tf_op jit(solution)/shard_map/all_to_all | solution.py:1120
  32.2 359.8 %all-gather.5.cloned.1.call-start = ((), (), s32[]{:S(2)}) async-start(), calls=%async_computation.13 | async-start | bytes 19464192 | tf_op jit(solution)/shard_map/all_gather | solution.py:1219
  139.5 55.4 %all-to-all-start.1 = ((bf16[4,3,64,1024]{3,2,1,0:T(8,128)(2,1)}), bf16[4,3,64,1024]{3,2,1,0:T(8,128)(2,1)S(1)}, u32[]{:S(2)}, u32[]{:S(2)}) async-start(bf16[4,3,64,1024]{3,2,1,0:T(8,128)(2,1)} %project.4.refs_3_), calls=%async_computation.1 | async-start | bytes 3145728 | tf_op jit(solution)/shard_map/all_to_all | solution.py:1251
  151.6 183.4 %collective-permute-start.20 = (bf16[512,1024]{1,0:T(8,128)(2,1)}, bf16[512,1024]{1,0:T(8,128)(2,1)}, u32[]{:S(2)}, u32[]{:S(2)}) collective-permute-start(bf16[512,1024]{1,0:T(8,128)(2,1)} %other_clip.1.refs_5_), channel_id=1, source_target_pairs={{0,4},{1,5},{2,6},{3,7},{4,0},{5,1},{6,2},{7,3},{8,12},{9,13},{10,... | collective-permute-start | bytes 3145736 | tf_op jit(solution)/shard_map/ppermute | solution.py:1100
  173.2 52.1 %collective-permute-start.17 = (f32[16,4096]{1,0:T(8,128)}, f32[16,4096]{1,0:T(8,128)S(1)}, u32[]{:S(2)}, u32[]{:S(2)}) collective-permute-start(f32[16,4096]{1,0:T(8,128)} %get-tuple-element.186), channel_id=1, source_target_pairs={{0,1},{1,0},{2,3},{3,2},{4,5},{5,4},{6,7},{7,6},{8,9},{9,8},{10,11... | collective-permute-start | bytes 786440 | tf_op jit(solution)/shard_map/ppermute | solution.py:1100
  194.9 67.6 %all-to-all-start.3 = ((bf16[4,3,64,1024]{3,2,1,0:T(8,128)(2,1)}), bf16[4,3,64,1024]{3,2,1,0:T(8,128)(2,1)S(1)}, u32[]{:S(2)}, u32[]{:S(2)}) async-start(bf16[4,3,64,1024]{3,2,1,0:T(8,128)(2,1)} %project.5.refs_3_), calls=%async_computation.3 | async-start | bytes 3145728 | tf_op jit(solution)/shard_map/all_to_all | solution.py:1251
  261.1 33.4 %collective-permute-start.19 = (f32[4,4096]{1,0:T(4,128)}, f32[4,4096]{1,0:T(4,128)S(1)}, u32[]{:S(2)}, u32[]{:S(2)}) collective-permute-start(f32[4,4096]{1,0:T(4,128)} %get-tuple-element.192), channel_id=1, source_target_pairs={{0,4},{1,5},{2,6},{3,7},{4,0},{5,1},{6,2},{7,3},{8,12},{9,13},{10,... | collective-permute-start | bytes 196616 | tf_op jit(solution)/shard_map/ppermute | solution.py:1100
  262.5 41.1 %all-to-all-start.2 = ((bf16[4,3,64,1024]{3,2,1,0:T(8,128)(2,1)}), bf16[4,3,64,1024]{3,2,1,0:T(8,128)(2,1)S(1)}, u32[]{:S(2)}, u32[]{:S(2)}) async-start(bf16[4,3,64,1024]{3,2,1,0:T(8,128)(2,1)} %project.6.refs_3_), calls=%async_computation.2 | async-start | bytes 3145728 | tf_op jit(solution)/shard_map/all_to_all | solution.py:1251
  303.6 31.3 %all-to-all-start.5 = ((bf16[4,3,64,1024]{3,2,1,0:T(8,128)(2,1)}), bf16[4,3,64,1024]{3,2,1,0:T(8,128)(2,1)S(1)}, u32[]{:S(2)}, u32[]{:S(2)}) async-start(bf16[4,3,64,1024]{3,2,1,0:T(8,128)(2,1)} %project.7.refs_3_), calls=%async_computation.5 | async-start | bytes 3145728 | tf_op jit(solution)/shard_map/all_to_all | solution.py:1251
  499.6 245.3 %all-gather.7.cloned.1.call-start = ((), (), s32[]{:S(2)}) async-start(), calls=%async_computation.14 | async-start | bytes 2162688 | tf_op jit(solution)/shard_map/all_gather | solution.py:1370
  500.3 87.5 %collective-permute-start.24 = (bf16[16,32,1024]{2,1,0:T(8,128)(2,1)}, bf16[16,32,1024]{2,1,0:T(8,128)(2,1)}, u32[]{:S(2)}, u32[]{:S(2)}) collective-permute-start(bf16[16,32,1024]{2,1,0:T(8,128)(2,1)} %bitcast.92), channel_id=1, source_target_pairs={{0,8},{1,9},{2,10},{3,11},{4,12},{5,13},{6,14},{7,15},{8,0},{9,1},... | collective-permute-start | bytes 3145736 | tf_op jit(solution)/shard_map/ppermute | solution.py:1100
  514.3 62.3 %collective-permute-start.26 = (bf16[8,128,1024]{2,1,0:T(8,128)(2,1)}, bf16[8,128,1024]{2,1,0:T(8,128)(2,1)S(1)}, u32[]{:S(2)}, u32[]{:S(2)}) collective-permute-start(bf16[8,128,1024]{2,1,0:T(8,128)(2,1)} %get-tuple-element.219), channel_id=1, source_target_pairs={{0,1},{1,0},{2,3},{3,2},{4,5},{5,4},{6,7},{7,6},{8,9},{9,8},{10,11... | collective-permute-start | bytes 6291464 | tf_op jit(solution)/shard_map/ppermute | solution.py:1100
  516.3 60.3 %collective-permute-start.25 = (bf16[8,128,1024]{2,1,0:T(8,128)(2,1)}, bf16[8,128,1024]{2,1,0:T(8,128)(2,1)}, u32[]{:S(2)}, u32[]{:S(2)}) collective-permute-start(bf16[8,128,1024]{2,1,0:T(8,128)(2,1)} %get-tuple-element.211.refs_7_), channel_id=1, source_target_pairs={{0,16},{1,17},{2,18},{3,19},{4,20},{5,21},{6,22},{7,23},{8,24},{9,... | collective-permute-start | bytes 6291464 | tf_op jit(solution)/shard_map/ppermute | solution.py:1100
  524.0 74.7 %all-to-all-start.8 = ((bf16[4,192,1024]{2,1,0:T(8,128)(2,1)}), bf16[4,192,1024]{2,1,0:T(8,128)(2,1)}, u32[]{:S(2)}, u32[]{:S(2)}) async-start(bf16[4,192,1024]{2,1,0:T(8,128)(2,1)} %get-tuple-element.212), calls=%async_computation.8 | async-start | bytes 3145728 | tf_op jit(solution)/shard_map/all_to_all | solution.py:1251
  575.9 134.3 %collective-permute-start.23 = (bf16[512,1024]{1,0:T(8,128)(2,1)}, bf16[512,1024]{1,0:T(8,128)(2,1)}, u32[]{:S(2)}, u32[]{:S(2)}) collective-permute-start(bf16[512,1024]{1,0:T(8,128)(2,1)} %copy_of.3.refs_9_), channel_id=1, source_target_pairs={{0,4},{1,5},{2,6},{3,7},{4,0},{5,1},{6,2},{7,3},{8,12},{9,13},{10,... | collective-permute-start | bytes 3145736 | tf_op jit(solution)/shard_map/ppermute | solution.py:1100
  585.9 61.3 %collective-permute-start.28 = (bf16[4,128,1024]{2,1,0:T(8,128)(2,1)}, bf16[4,128,1024]{2,1,0:T(8,128)(2,1)S(1)}, u32[]{:S(2)}, u32[]{:S(2)}) collective-permute-start(bf16[4,128,1024]{2,1,0:T(8,128)(2,1)} %get-tuple-element.220.refs_5_), channel_id=1, source_target_pairs={{0,1},{1,0},{2,3},{3,2},{4,5},{5,4},{6,7},{7,6},{8,9},{9,8},{10,11... | collective-permute-start | bytes 3145736 | tf_op jit(solution)/shard_map/ppermute | solution.py:1100
  591.3 63.7 %collective-permute-start.27 = (bf16[8,32,1024]{2,1,0:T(8,128)(2,1)}, bf16[8,32,1024]{2,1,0:T(8,128)(2,1)S(1)}, u32[]{:S(2)}, u32[]{:S(2)}) collective-permute-start(bf16[8,32,1024]{2,1,0:T(8,128)(2,1)} %get-tuple-element.222.refs_7_), channel_id=1, source_target_pairs={{0,16},{1,17},{2,18},{3,19},{4,20},{5,21},{6,22},{7,23},{8,24},{9,... | collective-permute-start | bytes 1572872 | tf_op jit(solution)/shard_map/ppermute | solution.py:1100
  598.6 48.6 %collective-permute-start.29 = (bf16[4,128,1024]{2,1,0:T(8,128)(2,1)}, bf16[4,128,1024]{2,1,0:T(8,128)(2,1)}, u32[]{:S(2)}, u32[]{:S(2)}) collective-permute-start(bf16[4,128,1024]{2,1,0:T(8,128)(2,1)} %get-tuple-element.225), channel_id=1, source_target_pairs={{0,16},{1,17},{2,18},{3,19},{4,20},{5,21},{6,22},{7,23},{8,24},{9,... | collective-permute-start | bytes 3145736 | tf_op jit(solution)/shard_map/ppermute | solution.py:1100
  598.6 108.0 %all-to-all-start.9 = ((bf16[4,3,64,1024]{3,2,1,0:T(8,128)(2,1)}), bf16[4,3,64,1024]{3,2,1,0:T(8,128)(2,1)S(1)}, u32[]{:S(2)}, u32[]{:S(2)}) async-start(bf16[4,3,64,1024]{3,2,1,0:T(8,128)(2,1)} %attend_back.4.refs_2_), calls=%async_computation.9 | async-start | bytes 3145728 | tf_op jit(solution)/shard_map/all_to_all | solution.py:1251
  653.0 62.0 %collective-permute-start.31 = (bf16[2,128,1024]{2,1,0:T(8,128)(2,1)}, bf16[2,128,1024]{2,1,0:T(8,128)(2,1)}, u32[]{:S(2)}, u32[]{:S(2)}) collective-permute-start(bf16[2,128,1024]{2,1,0:T(8,128)(2,1)} %get-tuple-element.228.refs_5_), channel_id=1, source_target_pairs={{0,2},{1,3},{2,0},{3,1},{4,6},{5,7},{6,4},{7,5},{8,10},{9,11},{10,... | collective-permute-start | bytes 1572872 | tf_op jit(solution)/shard_map/ppermute | solution.py:1100
  660.0 58.8 %collective-permute-start.30 = (bf16[4,32,1024]{2,1,0:T(8,128)(2,1)}, bf16[4,32,1024]{2,1,0:T(8,128)(2,1)S(1)}, u32[]{:S(2)}, u32[]{:S(2)}) collective-permute-start(bf16[4,32,1024]{2,1,0:T(8,128)(2,1)} %get-tuple-element.229.refs_7_), channel_id=1, source_target_pairs={{0,1},{1,0},{2,3},{3,2},{4,5},{5,4},{6,7},{7,6},{8,9},{9,8},{10,11... | collective-permute-start | bytes 786440 | tf_op jit(solution)/shard_map/ppermute | solution.py:1100
  661.4 53.6 %collective-permute-start.32 = (bf16[2,128,1024]{2,1,0:T(8,128)(2,1)}, bf16[2,128,1024]{2,1,0:T(8,128)(2,1)}, u32[]{:S(2)}, u32[]{:S(2)}) collective-permute-start(bf16[2,128,1024]{2,1,0:T(8,128)(2,1)} %get-tuple-element.235), channel_id=1, source_target_pairs={{0,2},{1,3},{2,0},{3,1},{4,6},{5,7},{6,4},{7,5},{8,10},{9,11},{10,... | collective-permute-start | bytes 1572872 | tf_op jit(solution)/shard_map/ppermute | solution.py:1100
  732.2 30.0 %collective-permute-start.33 = (bf16[16,32,768]{2,1,0:T(8,128)(2,1)}, bf16[16,32,768]{2,1,0:T(8,128)(2,1)S(1)}, u32[]{:S(2)}, u32[]{:S(2)}) collective-permute-start(bf16[16,32,768]{2,1,0:T(8,128)(2,1)} %bitcast.95), channel_id=1, source_target_pairs={{0,8},{1,9},{2,10},{3,11},{4,12},{5,13},{6,14},{7,15},{8,0},{9,1},... | collective-permute-start | bytes 2359304 | tf_op jit(solution)/shard_map/ppermute | solution.py:1100
  747.8 72.4 %all-to-all-start.12 = ((bf16[4,3,64,1024]{3,2,1,0:T(8,128)(2,1)}), bf16[4,3,64,1024]{3,2,1,0:T(8,128)(2,1)S(1)}, u32[]{:S(2)}, u32[]{:S(2)}) async-start(bf16[4,3,64,1024]{3,2,1,0:T(8,128)(2,1)} %attend_back.6.refs_3_), calls=%async_computation.12 | async-start | bytes 3145728 | tf_op jit(solution)/shard_map/all_to_all | solution.py:1251
  752.3 72.6 %collective-permute-start.35 = (bf16[2,32,1024]{2,1,0:T(8,128)(2,1)S(1)}, bf16[2,32,1024]{2,1,0:T(8,128)(2,1)}, u32[]{:S(2)}, u32[]{:S(2)}) collective-permute-start(bf16[2,32,1024]{2,1,0:T(8,128)(2,1)S(1)} %copy-done.74), channel_id=1, source_target_pairs={{0,2},{1,3},{2,0},{3,1},{4,6},{5,7},{6,4},{7,5},{8,10},{9,11},{10,... | collective-permute-start | bytes 393224 | tf_op jit(solution)/shard_map/ppermute | solution.py:1100
  754.4 62.0 %collective-permute-start.36 = (bf16[1,128,1024]{2,1,0:T(8,128)(2,1)S(1)}, bf16[1,128,1024]{2,1,0:T(8,128)(2,1)S(1)}, u32[]{:S(2)}, u32[]{:S(2)}) collective-permute-start(bf16[1,128,1024]{2,1,0:T(8,128)(2,1)S(1)} %copy-done.61), channel_id=1, source_target_pairs={{0,4},{1,5},{2,6},{3,7},{4,0},{5,1},{6,2},{7,3},{8,12},{9,13},{10,... | collective-permute-start | bytes 786440 | tf_op jit(solution)/shard_map/ppermute | solution.py:1100
  754.4 62.0 %collective-permute-start.37 = (bf16[1,128,1024]{2,1,0:T(8,128)(2,1)}, bf16[1,128,1024]{2,1,0:T(8,128)(2,1)S(1)}, u32[]{:S(2)}, u32[]{:S(2)}) collective-permute-start(bf16[1,128,1024]{2,1,0:T(8,128)(2,1)} %get-tuple-element.250), channel_id=1, source_target_pairs={{0,4},{1,5},{2,6},{3,7},{4,0},{5,1},{6,2},{7,3},{8,12},{9,13},{10,... | collective-permute-start | bytes 786440 | tf_op jit(solution)/shard_map/ppermute | solution.py:1100
  770.4 71.5 %collective-permute-start.38 = (bf16[8,32,768]{2,1,0:T(8,128)(2,1)}, bf16[8,32,768]{2,1,0:T(8,128)(2,1)S(1)}, u32[]{:S(2)}, u32[]{:S(2)}) collective-permute-start(bf16[8,32,768]{2,1,0:T(8,128)(2,1)} %get-tuple-element.245.refs_7_), channel_id=1, source_target_pairs={{0,1},{1,0},{2,3},{3,2},{4,5},{5,4},{6,7},{7,6},{8,9},{9,8},{10,11... | collective-permute-start | bytes 1179656 | tf_op jit(solution)/shard_map/ppermute | solution.py:1100
  827.5 67.3 %collective-permute-start.49 = (bf16[1,32,1024]{2,1,0:T(8,128)(2,1)}, bf16[1,32,1024]{2,1,0:T(8,128)(2,1)S(1)}, u32[]{:S(2)}, u32[]{:S(2)}) collective-permute-start(bf16[1,32,1024]{2,1,0:T(8,128)(2,1)} %get-tuple-element.252.refs_5_), channel_id=1, source_target_pairs={{0,4},{1,5},{2,6},{3,7},{4,0},{5,1},{6,2},{7,3},{8,12},{9,13},{10,... | collective-permute-start | bytes 196616 | tf_op jit(solution)/shard_map/ppermute | solution.py:1100
  841.9 34.8 %collective-permute-start.44 = (bf16[16,32,768]{2,1,0:T(8,128)(2,1)}, bf16[16,32,768]{2,1,0:T(8,128)(2,1)S(1)}, u32[]{:S(2)}, u32[]{:S(2)}) collective-permute-start(bf16[16,32,768]{2,1,0:T(8,128)(2,1)} %bitcast.93), channel_id=1, source_target_pairs={{0,8},{1,9},{2,10},{3,11},{4,12},{5,13},{6,14},{7,15},{8,0},{9,1},... | collective-permute-start | bytes 2359304 | tf_op jit(solution)/shard_map/ppermute | solution.py:1100
  877.3 99.8 %collective-permute-start.42 = (bf16[512,1024]{1,0:T(8,128)(2,1)}, bf16[512,1024]{1,0:T(8,128)(2,1)}, u32[]{:S(2)}, u32[]{:S(2)}) collective-permute-start(bf16[512,1024]{1,0:T(8,128)(2,1)} %get-tuple-element.267), channel_id=1, source_target_pairs={{0,4},{1,5},{2,6},{3,7},{4,0},{5,1},{6,2},{7,3},{8,12},{9,13},{10,... | collective-permute-start | bytes 3145736 | tf_op jit(solution)/shard_map/ppermute | solution.py:1100
  892.7 37.8 %collective-permute-start.55 = (bf16[1,32,768]{2,1,0:T(8,128)(2,1)}, bf16[1,32,768]{2,1,0:T(8,128)(2,1)S(1)}, u32[]{:S(2)}, u32[]{:S(2)}) collective-permute-start(bf16[1,32,768]{2,1,0:T(8,128)(2,1)} %get-tuple-element.279.refs_3_), channel_id=1, source_target_pairs={{0,4},{1,5},{2,6},{3,7},{4,0},{5,1},{6,2},{7,3},{8,12},{9,13},{10,... | collective-permute-start | bytes 147464 | tf_op jit(solution)/shard_map/ppermute | solution.py:1100
  (143 other events, 1138.5 us)
Sparse Core Ops, SparseCore 0:
  119.3 178.8 all-gather.4
  504.0 66.5 all-gather.6

commit v3 on v2

--- a/solution.py
+++ b/solution.py
@@ -160,6 +160,10 @@
     return pl.BlockSpec((rows // frames, D), lambda r, f, ids: (r * frames + f, 0))
 
 
+def column_spec(rows, frames):
+    return pl.BlockSpec((D, rows // frames), lambda r, f, ids: (0, r * frames + f))
+
+
 def read_pair(ids_ref, own_ref, other_ref):
     own = pl.program_id(0) == ids_ref[1]
     return jnp.where(own, own_ref[0].astype(WIDE), other_ref[...].astype(WIDE))
@@ -197,7 +201,7 @@
     def kernel(ids_ref, tokens_ref, early_ref, out_ref):
         normed, _ = norm_parts(tokens_ref[0].astype(WIDE))
         shift, scale = piece(early_ref, 0, frames), piece(early_ref, 1, frames)
-        out_ref[...] = (normed * (1.0 + scale) + shift).astype(LOW)
+        out_ref[...] = (normed * (1.0 + scale) + shift).astype(LOW).T
 
     return call(
         kernel,
@@ -206,20 +210,20 @@
         (2, frames),
         [tokens, early],
         [chunk_spec(rows, frames), whole(early.shape)],
-        low_array(2 * rows, D),
-        row_spec(rows, frames),
+        low_array(D, 2 * rows),
+        column_spec(rows, frames),
         after=after,
         time=5,
     )
 
 
 def project(ids, rows, weight, cosines, sines, members, first, after=()):
-    tokens, width = rows.shape
+    width, tokens = rows.shape
     columns = members * HEAD
     half = HEAD // 2
 
     def kernel(ids_ref, rows_ref, weight_ref, cos_ref, sin_ref, out_ref):
-        across = dot(rows_ref[...], weight_ref[...]).T
+        across = dot(weight_ref[...].T, rows_ref[...])
         kind = pl.program_id(0)
 
         @pl.when(kind == 2)
@@ -244,7 +248,7 @@
         (3,),
         [rows, weight, cosines, sines],
         [
-            whole((tokens, width)),
+            whole((width, tokens)),
             pl.BlockSpec((width, columns), lambda t, ids: (0, first * 3 + t)),
             table,
             table,
@@ -256,7 +260,12 @@
     )
 
 
-def attend(ids, parts, into, head, heads, after=()):
+def two_lows(value):
+    high = value.astype(LOW)
+    return high, (value - high.astype(WIDE)).astype(LOW)
+
+
+def attend(ids, parts, into, head, heads, relative, after=()):
     members, _, _, tokens = parts.shape
     size, block = min(1024, tokens), min(512, tokens)
     length = members * tokens
@@ -264,37 +273,74 @@
     before = [] if into is None else [into]
 
     def kernel(ids_ref, part_ref, *refs):
-        low_ref, wide_ref, total_ref, key_rows = refs[len(before) :]
+        low_ref, wide_ref, total_ref, key_rows, key_top = refs[len(before) :]
         step = pl.program_id(0)
 
         @pl.when(step == 0)
         def _():
+            top = jnp.zeros((1, 1), WIDE)
             for member in range(members):
-                key_rows[member * tokens : (member + 1) * tokens, :] = part_ref[member, 1].T
+                keys = part_ref[member, 1].astype(WIDE) * SOFT
+                top = jnp.maximum(top, jnp.max(jnp.sum(keys * keys, axis=0, keepdims=True)))
+                high, low = two_lows(keys)
+                key_rows[member * tokens : (member + 1) * tokens, :] = jnp.concatenate(
+                    [high, low], axis=0
+                ).T
+            key_top[...] = top
 
         member = step // per
         start = 0 if per == 1 else pl.multiple_of(step % per * size, size)
         queries = part_ref[member, 0, :, pl.ds(start, size)]
-        gathered = jnp.zeros((HEAD, size), WIDE)
-        top = jnp.full((1, size), -1e30, WIDE)
-        total = jnp.zeros((1, size), WIDE)
-        following = dot(key_rows[0:block, :], queries)
-        for number in range(count):
-            scores = following
-            if number + 1 < count:
-                following = dot(key_rows[(number + 1) * block : (number + 2) * block, :], queries)
-            raised = jnp.maximum(top, jnp.max(scores, axis=0, keepdims=True))
-            shrink = jnp.exp2((top - raised) * SOFT)
-            probs = jnp.exp2(scores * SOFT - raised * SOFT)
-            total = total * shrink + jnp.sum(probs, axis=0, keepdims=True)
+        doubled = jnp.concatenate([queries, queries], axis=0)
+        wide_queries = queries.astype(WIDE)
+        query_top = jnp.max(jnp.sum(wide_queries * wide_queries, axis=0, keepdims=True))
+        bounded = query_top * jnp.max(key_top[...]) <= 60.0**2
+
+        def scores_of(number):
+            return dot(key_rows[number * block : (number + 1) * block, :], doubled)
+
+        def values_of(number):
             at = number % inside * block
-            values = part_ref[number // inside, 2, :, at : at + block]
-            gathered = gathered * shrink + dot(values, probs.astype(LOW))
-            top = raised
-        attended = gathered / total
-        wide_ref[...] = attended
-        total_ref[...] = top * SOFT + jnp.log2(total)
-        low_ref[member, :, pl.ds(start, size)] = attended.astype(LOW)
+            return part_ref[number // inside, 2, :, at : at + block]
+
+        def finish(gathered, total, top):
+            attended = gathered / total
+            wide_ref[...] = attended
+            total_ref[...] = top + jnp.log2(total)
+            target = member ^ ids_ref[0] if relative else member
+            low_ref[target, :, pl.ds(start, size)] = attended.astype(LOW)
+
+        @pl.when(bounded)
+        def _():
+            gathered = jnp.zeros((HEAD, size), WIDE)
+            total = jnp.zeros((1, size), WIDE)
+            following = scores_of(0)
+            for number in range(count):
+                scores = following
+                if number + 1 < count:
+                    following = scores_of(number + 1)
+                probs = jnp.exp2(scores)
+                total = total + jnp.sum(probs, axis=0, keepdims=True)
+                gathered = gathered + dot(values_of(number), probs.astype(LOW))
+            finish(gathered, total, 0.0)
+
+        @pl.when(jnp.logical_not(bounded))
+        def _():
+            gathered = jnp.zeros((HEAD, size), WIDE)
+            top = jnp.full((1, size), -1e30, WIDE)
+            total = jnp.zeros((1, size), WIDE)
+            following = scores_of(0)
+            for number in range(count):
+                scores = following
+                if number + 1 < count:
+                    following = scores_of(number + 1)
+                raised = jnp.maximum(top, jnp.max(scores, axis=0, keepdims=True))
+                shrink = jnp.exp2(top - raised)
+                probs = jnp.exp2(scores - raised)
+                total = total * shrink + jnp.sum(probs, axis=0, keepdims=True)
+                gathered = gathered * shrink + dot(values_of(number), probs.astype(LOW))
+                top = raised
+            finish(gathered, total, top)
 
     return call(
         kernel,
@@ -313,30 +359,33 @@
             pl.BlockSpec((HEAD, size), lambda i, ids: (0, i)),
             pl.BlockSpec((1, size), lambda i, ids: (0, i)),
         ],
-        [pltpu.VMEM((length, HEAD), LOW)],
+        [pltpu.VMEM((length, 2 * HEAD), LOW), pltpu.VMEM((1, 1), WIDE)],
         after,
         aliases={2: 0} if before else {},
-        time=26,
-    )
-
-
-def middle_part(ids, parts, members, weight, tokens, upstream, late, frames, after=()):
+        time=18,
+    )
+
+
+def middle_part(ids, front, backs, members, weight, tokens, upstream, late, frames, after=()):
     rows = tokens.shape[1]
     size = rows // frames
     group = D // members
+    parts = [front] * (front is not None) + list(backs)
 
     def kernel(ids_ref, *refs):
-        part_refs = refs[: len(parts)]
+        part_refs = list(refs[: len(parts)])
         weight_ref, tokens_ref, g_own, g_other, late_ref = refs[len(parts) : len(parts) + 5]
         low_ref, projected_ref, middle_ref, normed_ref, grad_ref, across = refs[len(parts) + 5 :]
-        for member in range(members):
-            at = member * group
-            for ref in part_refs:
-                across[at : at + ref.shape[1], :] = ref[member]
-                at += ref.shape[1]
-        low = across[...].T
+        if front is not None:
+            front_ref = part_refs.pop(0)
+            for member in range(members):
+                across[member * group : member * group + group - HEAD, :] = front_ref[member]
+        for member, ref in enumerate(part_refs):
+            at = pl.multiple_of((ids_ref[0] ^ member) * group + group - HEAD, HEAD)
+            across[pl.ds(at, HEAD), :] = ref[...]
+        low = across[...]
         low_ref[...] = low
-        projected = dot(low, weight_ref[...].reshape(D, D))
+        projected = dot(low.T, weight_ref[...].reshape(D, D))
         projected_ref[...] = projected
         middle = tokens_ref[0].astype(WIDE) + piece(late_ref, 0, frames) * projected
         middle_ref[...] = middle
@@ -347,7 +396,10 @@
         grad_ref[...] = (piece(late_ref, 3, frames) * upstream).astype(LOW)
 
     part_specs = [
-        pl.BlockSpec(part.shape[:2] + (size,), lambda r, f, ids: (0, 0, r * frames + f))
+        pl.BlockSpec(
+            part.shape[:-1] + (size,),
+            lambda r, f, ids, lead=part.ndim - 1: (0,) * lead + (r * frames + f,),
+        )
         for part in parts
     ]
     return call(
@@ -361,13 +413,13 @@
         + pair_specs(rows, frames)
         + [whole(late.shape)],
         [
-            low_array(2 * rows, D),
+            low_array(D, 2 * rows),
             wide_array(2 * rows, D),
             wide_array(2 * rows, D),
             low_array(2 * rows, D),
             low_array(2 * rows, D),
         ],
-        [row_spec(rows, frames)] * 5,
+        [column_spec(rows, frames)] + [row_spec(rows, frames)] * 4,
         [pltpu.VMEM((D, size), LOW)],
         after,
         time=12,
@@ -379,19 +431,13 @@
     return step % pairs * 2 + jnp.where(step < pairs, 1 - core, core)
 
 
-def feed(ids, rows, grads, up, down, hidden, devices, core_mask, pairs, after=()):
+def feed(ids, rows, grads, up, down, hidden, devices, kind, after=()):
     tokens, width = rows.shape
     chunk = 512
     own_up, own_down = width // devices, hidden // devices
-    aside = width // chunk
-    quarter = width // (2 * pairs)
-    owners = devices // 2
-    spans = hidden // (2 * pairs) // chunk
+    aside, down_blocks = width // chunk, chunk // own_down
     steps = hidden // chunk
-    kind = LOW if own_up % 16 == 0 else WIDE
-
-    def chunk_at(step, ids):
-        return quarter_at(step // spans, ids, core_mask, pairs) * spans + step % spans
+    own_rows = own_down + own_up * (hidden // width) + own_up
 
     def kernel(
         ids_ref,
@@ -401,19 +447,44 @@
         down_ref,
         branch_ref,
         back_ref,
-        down_sent,
-        down_kept,
-        up_sent,
-        up_kept,
+        out_ref,
         across,
+        down_rows,
+        up_rows,
+        sems,
     ):
         step = pl.program_id(0)
+        slot = step % 2
+
+        def copies(step, slot):
+            first = own_down + step // aside * own_up
+            return (
+                pltpu.make_async_copy(
+                    down_rows.at[slot],
+                    out_ref.at[pl.ds(step * down_blocks, down_blocks), pl.ds(0, own_down)],
+                    sems.at[0, slot],
+                ),
+                pltpu.make_async_copy(
+                    up_rows.at[slot],
+                    out_ref.at[
+                        :,
+                        pl.ds(pl.multiple_of(first, own_up), own_up),
+                        pl.ds(pl.multiple_of(step % aside * chunk, chunk), chunk),
+                    ],
+                    sems.at[1, slot],
+                ),
+            )
 
         @pl.when(step == 0)
         def _():
             across[...] = rows_ref[...].T
             branch_ref[...] = jnp.zeros_like(branch_ref)
             back_ref[...] = jnp.zeros_like(back_ref)
+
+        @pl.when(step >= 2)
+        def _():
+            for copy in copies(step - 2, slot):
+                copy.wait()
 
         grads = grad_ref[...]
         up, down = up_ref[...].reshape(width, chunk), down_ref[...].reshape(chunk, width)
@@ -428,39 +499,18 @@
         upper_grad = (hidden_grad * slope).astype(LOW)
         branch_ref[...] += dot(low, down)
         back_ref[...] += dot(upper_grad, up.T)
-        down_grad = dot(low.T, grads)
-
-        @pl.when(step < steps // 2)
+        down_grad = dot(low.T, grads).astype(kind)
+        up_grad = dot(across[...], upper_grad).astype(kind)
+        down_rows[slot] = down_grad.reshape(down_rows.shape[1:])
+        up_rows[slot] = up_grad.reshape(up_rows.shape[1:])
+        for copy in copies(step, slot):
+            copy.start()
+
+        @pl.when(step == steps - 1)
         def _():
-            down_sent[...] = down_grad.astype(LOW).reshape(down_sent.shape)
-
-        @pl.when(step >= steps // 2)
-        def _():
-            down_kept[...] = down_grad.astype(kind).reshape(down_kept.shape)
-
-        core = bit_of(ids_ref[2], core_mask)
-        taken = owners // pairs
-        for out, bit in ((up_sent, 1 - core), (up_kept, core)):
-            for number in range(pairs):
-                start = pl.multiple_of((2 * number + bit) * quarter, quarter)
-                value = dot(across[pl.ds(start, quarter), :], upper_grad).astype(out.dtype)
-                out[number * taken : (number + 1) * taken] = value.reshape(
-                    (taken,) + out.shape[1:]
-                )
-
-    def sent_at(step, ids):
-        return (jnp.minimum(step, steps // 2 - 1), 0, 0)
-
-    def kept_at(step, ids):
-        return (jnp.maximum(step - steps // 2, 0), 0, 0)
-
-    def up_at(step, ids):
-        at = chunk_at(step, ids)
-        return (0, at // aside, 0, at % aside)
-
-    down_block = (chunk // own_down, own_down, width)
-    up_block = (owners, 1, own_up, chunk)
-    up_shape = (owners, hidden // width, own_up, width)
+            for copy in copies(step - 1, 1 - slot) + copies(step, slot):
+                copy.wait()
+
     return call(
         kernel,
         "feed",
@@ -470,29 +520,24 @@
         [
             whole((tokens, width)),
             whole((tokens, width)),
-            pl.BlockSpec(up[1], lambda step, ids: up[2](chunk_at(step, ids))),
-            pl.BlockSpec(down[1], lambda step, ids: down[2](chunk_at(step, ids))),
+            pl.BlockSpec(up[1], lambda step, ids: up[2](step)),
+            pl.BlockSpec(down[1], lambda step, ids: down[2](step)),
         ],
         [
             wide_array(tokens, width),
             wide_array(tokens, width),
-            low_array(owners, own_down, width),
-            jax.ShapeDtypeStruct((owners, own_down, width), kind),
-            low_array(*up_shape) if kind == LOW else wide_array(*up_shape),
-            jax.ShapeDtypeStruct(up_shape, kind),
+            jax.ShapeDtypeStruct((devices, own_rows, width), kind),
         ],
+        [whole((tokens, width)), whole((tokens, width)), anywhere],
         [
-            whole((tokens, width)),
-            whole((tokens, width)),
-            pl.BlockSpec(down_block, sent_at),
-            pl.BlockSpec(down_block, kept_at),
-            pl.BlockSpec(up_block, up_at),
-            pl.BlockSpec(up_block, up_at),
+            pltpu.VMEM((width, tokens), LOW),
+            pltpu.VMEM((2, down_blocks, own_down, width), kind),
+            pltpu.VMEM((2, devices, own_up, chunk), kind),
+            pltpu.SemaphoreType.DMA((2, 2)),
         ],
-        [pltpu.VMEM((width, tokens), LOW)],
         after,
         room=62,
-        time=66,
+        time=64,
     )
 
 
@@ -559,22 +604,24 @@
         kept_ref[0] = value
 
 
-def half_specs(pairs, rows, width):
+def half_specs(pairs, rows, width, slot):
     return [
-        pl.BlockSpec((1, rows, width), lambda i, ids: (jnp.minimum(i, pairs - 1), 0, 0)),
-        pl.BlockSpec((1, rows, width), lambda i, ids: (jnp.maximum(i - pairs, 0), 0, 0)),
+        pl.BlockSpec((1, rows, width), lambda i, ids: (jnp.minimum(i, pairs - 1), 0, slot)),
+        pl.BlockSpec((1, rows, width), lambda i, ids: (jnp.maximum(i - pairs, 0), 0, slot)),
     ]
 
 
-def hand_out(ids, weight, gradient, attended, members, head_count, core_mask, pairs, after=()):
+def hand_out(ids, weight, gradient, attended, into, members, steps, after=()):
     tokens, width = gradient.shape
-    quarter = width // (2 * pairs)
-    groups = members // (2 * pairs)
+    quarter = width // steps
+    groups = members // steps
     group = width // members
     front = group - HEAD
-
-    def kernel(ids_ref, weight_ref, grad_ref, attended_ref, *refs):
-        *out_refs, sent_ref, kept_ref = refs
+    devices, own_rows, _ = into.shape
+    own = width // devices
+
+    def kernel(ids_ref, weight_ref, grad_ref, attended_ref, into_ref, *refs):
+        gradient_ref, *out_refs = refs
         step = pl.program_id(0)
         grads = grad_ref[...]
         if weight_ref.shape[0] == 1:
@@ -588,31 +635,29 @@
             out_refs[0][number] = block[at + front : at + group]
             if front:
                 out_refs[1][number] = block[at : at + front]
-        put_half(step, pairs, dot(attended_ref[...].T, grads), sent_ref, kept_ref)
+        value = dot(attended_ref[...], grads).astype(into.dtype)
+        gradient_ref[...] = value.reshape(gradient_ref.shape)
 
     shapes = [(members, HEAD, tokens)] + [(members, front, tokens)] * (front > 0)
-    halves = (pairs, quarter, width)
     return call(
         kernel,
         "hand_out",
         ids,
-        (2 * pairs,),
-        [weight[0], gradient, attended],
+        (steps,),
+        [weight[0], gradient, attended, into],
         [
             weight[1],
             whole(gradient.shape),
-            pl.BlockSpec(
-                (tokens, quarter), lambda i, ids: (0, quarter_at(i, ids, core_mask, pairs))
-            ),
+            pl.BlockSpec((quarter, tokens), lambda i, ids: (i, 0)),
+            anywhere,
         ],
-        [low_array(*shape) for shape in shapes] + [low_array(*halves), wide_array(*halves)],
-        [
-            pl.BlockSpec((groups,) + shape[1:], lambda i, ids: (i, 0, 0))
-            for shape in shapes
-        ]
-        + half_specs(pairs, quarter, width),
+        [jax.ShapeDtypeStruct(into.shape, into.dtype)]
+        + [low_array(*shape) for shape in shapes],
+        [pl.BlockSpec((quarter // own, own, width), lambda i, ids: (i, own_rows // own - 1, 0))]
+        + [pl.BlockSpec((groups,) + shape[1:], lambda i, ids: (i, 0, 0)) for shape in shapes],
         after=after,
-        time=10,
+        aliases={4: 0},
+        time=9,
     )
 
 
@@ -626,7 +671,7 @@
     members, _, _, tokens = parts.shape
     size, block = min(1024, tokens), min(512, tokens)
     length = members * tokens
-    per, count, inside = tokens // size, length // block, tokens // block
+    per, count = tokens // size, length // block
     back = HEAD ** (-0.5)
 
     def kernel(
@@ -639,6 +684,8 @@
         sin_ref,
         out_ref,
         key_rows,
+        key_more,
+        value_more,
         key_sum,
         value_sum,
     ):
@@ -647,7 +694,12 @@
         @pl.when(step == 0)
         def _():
             for member in range(members):
-                key_rows[member * tokens : (member + 1) * tokens, :] = part_ref[member, 1].T
+                span = slice(member * tokens, (member + 1) * tokens)
+                key_rows[span, :] = part_ref[member, 1].T
+                key_more[:HEAD, span] = part_ref[member, 1]
+                value_more[:HEAD, span] = part_ref[member, 2]
+            key_more[HEAD:, :] = jnp.full((16, length), -1.0, LOW)
+            value_more[HEAD:, :] = jnp.full((16, length), -1.0, LOW)
             key_sum[...] = jnp.zeros_like(key_sum)
             value_sum[...] = jnp.zeros_like(value_sum)
 
@@ -655,18 +707,21 @@
         start = 0 if per == 1 else pl.multiple_of(step % per * size, size)
         queries_across = part_ref[member, 0, :, pl.ds(start, size)]
         grads_across = grad_ref[member, :, pl.ds(start, size)]
-        queries = queries_across.T
-        out_grads = grads_across.T
-        delta = jnp.sum(grads_across.astype(WIDE) * wide_ref[...], axis=0, keepdims=True).T
-        totals = total_ref[...].T
+        delta = jnp.sum(grads_across.astype(WIDE) * wide_ref[...], axis=0, keepdims=True)
+
+        def less(rows, amount):
+            high = amount.astype(LOW)
+            middle, low = two_lows(amount - high.astype(WIDE))
+            spare = jnp.zeros((13, size), LOW)
+            return jnp.concatenate([rows, high, middle, low, spare], axis=0).T
+
+        queries = less(queries_across, total_ref[...] * (1 / SOFT))
+        out_grads = less(grads_across, delta)
         query_grad = jnp.zeros((size, HEAD), WIDE)
 
         def pair(number):
-            source, at = number // inside, number % inside * block
-            return (
-                dot(queries, part_ref[source, 1, :, at : at + block]),
-                dot(out_grads, part_ref[source, 2, :, at : at + block]),
-            )
+            here = slice(number * block, (number + 1) * block)
+            return dot(queries, key_more[:, here]), dot(out_grads, value_more[:, here])
 
         following = pair(0)
         for number in range(count):
@@ -674,8 +729,8 @@
             if number + 1 < count:
                 following = pair(number + 1)
             here = slice(number * block, (number + 1) * block)
-            probs = jnp.exp2(scores * SOFT - totals)
-            score_grad = (probs * (prob_grad - delta)).astype(LOW)
+            probs = jnp.exp2(scores * SOFT)
+            score_grad = (probs * prob_grad).astype(LOW)
             value_sum[:, here] += dot(grads_across, probs.astype(LOW))
             key_sum[:, here] += dot(queries_across, score_grad)
             query_grad += dot(score_grad, key_rows[here, :])
@@ -712,24 +767,31 @@
         whole((members, 3, HEAD, tokens)),
         [
             pltpu.VMEM((length, HEAD), LOW),
+            pltpu.VMEM((HEAD + 16, length), LOW),
+            pltpu.VMEM((HEAD + 16, length), LOW),
             pltpu.VMEM((HEAD, length), WIDE),
             pltpu.VMEM((HEAD, length), WIDE),
         ],
         after,
-        time=44,
-    )
-
-
-def joint_back(ids, parts, normed, weight, column, total, core_mask, pairs, after=()):
+        time=26,
+    )
+
+
+def joint_back(
+    ids, parts, normed, weight, column, total, core_mask, pairs, into, slot, slots, after=()
+):
     members, _, _, tokens = parts.shape
     group = members * HEAD
     width = 3 * group
     quarter = D // (2 * pairs)
-    halves = (pairs, quarter, width)
+    halves = (pairs, quarter, slots * width)
     before = [] if total is None else [total]
+    held = [] if into is None else list(into)
 
     def kernel(ids_ref, part_ref, normed_ref, weight_ref, *refs):
-        *total_refs, sent_ref, kept_ref, total_ref, across, lined = refs
+        refs = list(refs)
+        total_refs = [refs.pop(0) for _ in before]
+        sent_ref, kept_ref, total_ref, across, lined = refs[len(held) :]
         step = pl.program_id(0)
 
         @pl.when(step == 0)
@@ -741,7 +803,7 @@
             lined[...] = across[...].T
 
         rows = lined[...]
-        put_half(step, pairs, dot(normed_ref[...].T, rows), sent_ref, kept_ref)
+        put_half(step, pairs, dot(normed_ref[...], rows), sent_ref, kept_ref)
         added = contract(rows, weight_ref[...], 1, 1)
         total_ref[...] = total_refs[0][...] + added if total_refs else added
 
@@ -749,23 +811,26 @@
         return quarter_at(i, ids, core_mask, pairs)
 
     strip = pl.BlockSpec((tokens, quarter), lambda i, ids: (0, at(i, ids)))
+    first = 4 + len(before)
     return call(
         kernel,
         "joint_back",
         ids,
         (2 * pairs,),
-        [parts, normed, weight, *before],
+        [parts, normed, weight, *before, *held],
         [
             whole(parts.shape),
-            strip,
+            pl.BlockSpec((quarter, tokens), lambda i, ids: (at(i, ids), 0)),
             pl.BlockSpec((quarter, width), lambda i, ids: (at(i, ids), column)),
         ]
-        + [strip] * len(before),
+        + [strip] * len(before)
+        + [anywhere] * len(held),
         [low_array(*halves), wide_array(*halves), wide_array(tokens, D)],
-        half_specs(pairs, quarter, width) + [strip],
+        half_specs(pairs, quarter, width, slot) + [strip],
         [pltpu.VMEM((width, tokens), LOW), pltpu.VMEM((tokens, width), LOW)],
         after,
-        time=10,
+        aliases={first: 0, first + 1: 1} if held else {},
+        time=9,
     )
 
 
@@ -847,7 +912,7 @@
         jax.ShapeDtypeStruct((2, rows, D), kind),
         chunk_spec(rows, frames),
         after=after,
-        time=3,
+        time=4,
     )
 
 
@@ -927,23 +992,24 @@
     )
 
 
-def stack_rows(ids, first, second, after=()):
-    count, width = first.shape
-
-    def kernel(ids_ref, first_ref, second_ref, out_ref):
-        out_ref[:count] = first_ref[...]
-        out_ref[count:] = second_ref[...]
+def stack_rows(ids, values, after=()):
+    count, width = values[0].shape
+
+    def kernel(ids_ref, *refs):
+        for number, ref in enumerate(refs[:-1]):
+            refs[-1][number * count : (number + 1) * count] = ref[...]
 
     return call(
         kernel,
         "stack_rows",
         ids,
         (1,),
-        [first, second],
-        [whole(first.shape)] * 2,
-        wide_array(2 * count, width),
-        whole((2 * count, width)),
+        values,
+        [whole(values[0].shape)] * len(values),
+        wide_array(len(values) * count, width),
+        whole((len(values) * count, width)),
         after=after,
+        time=1,
     )
 
 
@@ -992,6 +1058,30 @@
     )
 
 
+def settle(ids, rows, own_down, blocks, after=()):
+    own = (rows.shape[0] - own_down) // (blocks + 1)
+
+    def kernel(ids_ref, rows_ref, down_out, up_out, output_out):
+        down_out[...] = rows_ref[:own_down].astype(WIDE)
+        for number in range(blocks):
+            at = own_down + number * own
+            up_out[:, number * D : (number + 1) * D] = rows_ref[at : at + own].astype(WIDE)
+        output_out[...] = rows_ref[own_down + blocks * own :].astype(WIDE)
+
+    shapes = [(own_down, D), (own, blocks * D), (own, D)]
+    return call(
+        kernel,
+        "settle",
+        ids,
+        (1,),
+        [rows],
+        [whole(rows.shape)],
+        [wide_array(*shape) for shape in shapes],
+        [whole(shape) for shape in shapes],
+        after=after,
+    )
+
+
 def copy_of(ids, value, after=()):
     def kernel(ids_ref, in_ref, out_ref):
         out_ref[...] = in_ref[...]
@@ -1009,36 +1099,56 @@
     )
 
 
-def halve(ids, jobs, after=()):
-    ins, in_specs, outs, out_specs = [], [], [], []
-    count = jobs[0][1].shape[0]
-    together = min([post or 1 for _, _, post, _ in jobs] + [4])
-    steps = max(1, count // 2) // together
-    for kept, arrived, post, mask in jobs:
-        block = (together,) + arrived.shape[1:]
-
-        def source(i, ids, side, post=post // together, mask=mask):
-            if not post:
-                return (i, 0, 0)
-            bit = bit_of(ids[2], mask)
-            return (i // post * 2 * post + (bit if side else 1 - bit) * post + i % post, 0, 0)
-
-        for side in (0, 1) if post else (1,):
-            ins += [kept, arrived]
-            spec = pl.BlockSpec(
-                block, lambda i, ids, side=side, source=source: source(i, ids, side)
-            )
-            in_specs += [spec, spec]
-            kind = LOW if side == 0 else WIDE
-            outs.append(jax.ShapeDtypeStruct((max(1, count // 2),) + arrived.shape[1:], kind))
-            out_specs.append(pl.BlockSpec(block, lambda i, ids: (i, 0, 0)))
+def split_four(ids, kept, arrived, blocks_of, masks, after=()):
+    rows = kept.shape[1:]
+    ins = [kept, *arrived]
+    if not masks:
+
+        def add(ids_ref, *refs):
+            *in_refs, out_ref = refs
+            out_ref[...] = sum(ref[...].astype(WIDE) for ref in in_refs)
+
+        return call(
+            add,
+            "split_four",
+            ids,
+            (1,),
+            ins,
+            [whole(kept.shape)] * len(ins),
+            wide_array(*kept.shape),
+            whole(kept.shape),
+            after=after,
+        )
+    pre, mid, post = blocks_of
+    high, low = masks
 
     def kernel(ids_ref, *refs):
-        for number, out in enumerate(refs[len(ins) :]):
-            value = refs[2 * number][...].astype(WIDE) + refs[2 * number + 1][...].astype(WIDE)
-            out[...] = value.astype(out.dtype)
-
-    return call(kernel, "halve", ids, (steps,), ins, in_specs, outs, out_specs, after=after, time=5)
+        in_refs, out_refs = refs[: len(ins)], refs[len(ins) :]
+        bits = bit_of(ids_ref[2], high), bit_of(ids_ref[2], low)
+        for out, (across, aside) in zip(out_refs, ((0, 0), (1, 0), (0, 1), (1, 1))):
+            first = 1 - bits[0] if across else bits[0]
+            second = 1 - bits[1] if aside else bits[1]
+            for one in range(pre):
+                for two in range(post):
+                    value = sum(ref[one, first, 0, second, two].astype(WIDE) for ref in in_refs)
+                    out[one, 0, two] = value.astype(out.dtype)
+
+    shape = (pre, 2, mid, 2, post) + rows
+    lead = (pre, 2, 1, 2, post) + rows
+    out_shape = (pre, mid, post) + rows
+    zeros = (0,) * len(rows)
+    return call(
+        kernel,
+        "split_four",
+        ids,
+        (mid,),
+        [value.reshape(shape) for value in ins],
+        [pl.BlockSpec(lead, lambda i, ids: (0, 0, i, 0, 0) + zeros)] * len(ins),
+        [wide_array(*out_shape)] + [low_array(*out_shape)] * 3,
+        [pl.BlockSpec((pre, 1, post) + rows, lambda i, ids: (0, i, 0) + zeros)] * 4,
+        after=after,
+        time=3,
+    )
 
 
 def halve_plain(rank, jobs):
@@ -1104,7 +1214,7 @@
 
     def run(kernel, *args, **options):
         result = kernel(ids, *args, after=tuple(last), **options)
-        last[:] = jax.tree.leaves(result)[:1]
+        last[:] = jax.tree.leaves(result)[-1:]
         return result
 
     clip_masks = [seq_size << bit for bit in range(clip_size.bit_length() - 1)]
@@ -1181,6 +1291,8 @@
     ]
     joined = [joint_low]
     early_terms = None
+    packed = run(pack, down_weight, up_weight, output_weight)
+    packed = lax.all_gather(packed, AXES, axis=0, tiled=False)
     for stage in range(len(order) + 1):
         joins = []
         if stage < len(order):
@@ -1215,8 +1327,6 @@
     own_up = up_weight.shape[0]
     own_down = down_weight.shape[0]
     tiled = own_up % 16 == 0
-    packed = run(pack, down_weight, up_weight, output_weight)
-    packed = lax.all_gather(packed, AXES, axis=0, tiled=False)
     chunk_rows = 512
     up_first = own_down // own_up
     if tiled:
@@ -1245,7 +1355,7 @@
     places = (starts[:, :, None] + jnp.arange(local_rows, dtype=jnp.int32)).reshape(-1)
     cosines, sines = rotary_tables(pick(frame_time, side), places)
 
-    normed_one_low = run(norm_one, tokens, early, frames)
+    normed_across = run(norm_one, tokens, early, frames)
 
     def exchange(value):
         return lax.all_to_all(value, "seq", 0, 0, axis_index_groups=group_ids)
@@ -1253,7 +1363,7 @@
     late_terms = Terms(run(copy_of, condition), 2 * D, 6 * D)
 
     def late_step():
-        if late_terms.masks or late_terms.arrived is not None:
+        if late_terms.arrived is not None:
             final = not late_terms.masks
             outs = list(run(join_and_add, [], [late_terms.job()]))
             late_terms.take(outs)
@@ -1263,44 +1373,41 @@
     def project_head(head):
         weight, offset = joint_sides[head // heads_aside], head % heads_aside
         return exchange(
-            run(project, normed_one_low, weight, cosines, sines, members, offset)
+            run(project, normed_across, weight, cosines, sines, members, offset)
         )
 
     parts = {0: project_head(0)}
     late_step()
-    upstream = (cotangent, swap_with(run(other_clip, cotangent, frames), half))
     wide, totals = {}, {}
     front = None
     front_heads = head_count - 1
     for head in range(head_count):
         if head + 1 < head_count:
             parts[head + 1] = project_head(head + 1)
+        else:
+            last.append(upstream[1] if head else tokens)
+        late_step()
+        if head == 0:
             late_step()
-        else:
-            last.append(upstream[1])
         if head < front_heads:
-            front, wide[head], totals[head] = run(attend, parts[head], front, head, front_heads)
+            front, wide[head], totals[head] = run(
+                attend, parts[head], front, head, front_heads, False
+            )
             if head + 1 == front_heads:
                 front = exchange(front)
         else:
-            back, wide[head], totals[head] = run(attend, parts[head], None, 0, 1)
-        late_step()
+            back, wide[head], totals[head] = run(attend, parts[head], None, 0, 1, True)
+        if head == 0:
+            upstream = (cotangent, swap_with(run(other_clip, cotangent, frames), half))
     while late_terms.arrived is not None:
         late_step()
     late = late_terms.kept
-    back = exchange(back)
-
-    attended_low, projected, middle, normed_two_low, branch_grad = run(
-        middle_part,
-        [back] if front is None else [front, back],
-        members,
-        output_source,
-        tokens,
-        upstream,
-        late,
-        frames,
-    )
-    branch, normed_two_grad, down_sent, down_kept, up_sent, up_kept = run(
+    backs = [swap_with(back[i], i) if i else back[i] for i in range(members)]
+
+    attended_across, projected, middle, normed_two_low, branch_grad = run(
+        middle_part, front, backs, members, output_source, tokens, upstream, late, frames
+    )
+    branch, normed_two_grad, weight_grads = run(
         feed,
         normed_two_low,
         branch_grad,
@@ -1308,79 +1415,81 @@
         down_source,
         FF,
         devices,
-        core_mask,
-        pairs,
+        LOW if tiled else WIDE,
     )
 
     class Chain:
-        def __init__(self, sent, kept, masks):
-            self.kept, self.masks = kept, list(masks)
-            self.remaining = sorted(self.masks)
-            self.arrived = swap_with(sent.astype(LOW), core_mask)
-
-        def job(self):
+        def __init__(self, sent, kept):
+            self.kept = kept
+            self.masks = [clip_masks[1], *seq_masks]
+            self.arrived = [swap_with(sent.astype(LOW), core_mask)]
+
+        def step(self):
+            if self.arrived is None:
+                return
+            if not tiled:
+                mask = self.masks.pop(0) if self.masks else None
+                post = 2 ** sum(1 for other in self.masks if other < mask) if mask else 0
+                outs = halve_plain(rank, [(self.kept, self.arrived[0], post, mask)])
+                self.arrived = [swap_with(outs[0], mask)] if mask else None
+                self.kept = outs[-1]
+                return
+            rows = self.kept.shape[1:]
             if not self.masks:
-                return (self.kept, self.arrived, 0, 1)
-            post = 2 ** self.remaining.index(self.masks[0])
-            return (self.kept, self.arrived, post, self.masks[0])
-
-        def take(self, outs):
-            if self.masks:
-                mask = self.masks.pop(0)
-                self.remaining.remove(mask)
-                self.arrived, self.kept = swap_with(outs.pop(0), mask), outs.pop(0)
-            else:
-                self.arrived, self.kept = None, outs.pop(0)
-
-    def step(*chains):
-        chains = [chain for chain in chains if chain.arrived is not None]
-        if not chains:
-            return
-        jobs = [chain.job() for chain in chains]
-        outs = list(run(halve, jobs)) if tiled else halve_plain(rank, jobs)
-        for chain in chains:
-            chain.take(outs)
+                self.kept = run(split_four, self.kept, self.arrived, None, None)
+                self.arrived = None
+                return
+            pair = sorted((self.masks.pop(0), self.masks.pop(0)), reverse=True)
+            pre = 2 ** sum(1 for other in self.masks if other > pair[0])
+            post = 2 ** sum(1 for other in self.masks if other < pair[1])
+            mid = 2 ** len(self.masks) // pre // post
+            kept, *sent = run(split_four, self.kept, self.arrived, (pre, mid, post), pair)
+            self.kept = kept.reshape((-1,) + rows)
+            ways = (*pair, pair[0] ^ pair[1])
+            self.arrived = [
+                swap_with(value.reshape((-1,) + rows), mask) for value, mask in zip(sent, ways)
+            ]
 
     def owners(value):
         return value.reshape(devices // 2, -1, value.shape[2])
 
-    one_way = clip_masks[1:] + seq_masks
-    other_way = seq_masks[:1] + clip_masks[1:] + seq_masks[1:]
-    up_shape = (devices // 2, up_blocks * own_up, D)
-    down_chain = Chain(down_sent, down_kept, one_way)
-    up_chain = Chain(up_sent.reshape(up_shape), up_kept.reshape(up_shape), other_way)
-
     result, middle_grad, projected_grad, late_rows = run(
         middle_back, middle, branch, normed_two_grad, projected, upstream, late, frames
     )
-    *outer, output_sent, output_kept = run(
-        hand_out,
-        output_source,
-        projected_grad,
-        attended_low,
-        members,
-        head_count,
-        core_mask,
-        pairs,
-    )
+    weight_grads, *outer = run(
+        hand_out, output_source, projected_grad, attended_across, weight_grads, members, 2 * pairs
+    )
+    weight_sums = lax.psum_scatter(
+        weight_grads.astype(LOW), AXES, scatter_dimension=0, tiled=True
+    )[0]
     outer_back = exchange(outer[0])
-    output_chain = Chain(owners(output_sent), owners(output_kept), one_way)
-    step(down_chain, up_chain)
     last.append(outer_back)
-    late_pieces = lax.all_gather(late_rows, AXES, axis=0, tiled=True)
 
     class Frames:
-        def __init__(self, rows):
-            self.rows, self.masks = rows, order[::-1]
+        def __init__(self, rows, groups):
+            self.rows, self.groups = rows, list(groups)
             self.send()
 
         def send(self):
-            self.arrived = swap_with(self.rows, self.masks.pop(0)) if self.masks else None
+            self.arrived = None
+            if self.groups:
+                group = self.groups.pop(0)
+                masks = group if len(group) == 1 else (*group, group[0] ^ group[1])
+                self.arrived = [swap_with(self.rows, mask) for mask in masks]
 
         def step(self):
             if self.arrived is not None:
-                self.rows = run(stack_rows, self.rows, self.arrived)
+                self.rows = run(stack_rows, [self.rows, *self.arrived])
                 self.send()
+
+    def ranks_of(groups):
+        masks = [0]
+        for mask in [mask for group in groups for mask in group]:
+            masks = masks + [other ^ mask for other in masks]
+        return rank ^ jnp.array(masks, jnp.int32)
+
+    late_frames = Frames(late_rows, [(mask,) for mask in reversed(order)])
+    late_frames.step()
 
     def head_back(head):
         grads, at = (outer_front, head) if head < front_heads else (outer_back, 0)
@@ -1388,77 +1497,90 @@
             attend_back, parts[head], grads, at, wide[head], totals[head], cosines, sines
         )
 
-    def head_joint(head, total):
+    heads = list(reversed(range(head_count)))
+    early_heads = heads[:2] if head_count > 3 else []
+    last_heads = heads[len(early_heads) :]
+
+    def head_joint(head, group, total, into):
         weight, offset = joint_sides[head // heads_aside], head % heads_aside
         sent, kept, total = run(
             joint_back,
             joint_parts[head],
-            normed_one_low,
+            normed_across,
             weight,
             offset,
             total,
             core_mask,
             pairs,
+            into,
+            group.index(head),
+            len(group),
         )
-        return owners(sent), owners(kept), total
-
-    joint_parts, head_chains = {}, {}
-    total = None
+        return total, (sent, kept)
+
+    joint_parts = {}
+    total = early_chain = None
     outer_front = exchange(outer[1]) if front_heads else None
-    heads = list(reversed(range(head_count)))
-    ready = []
     for number, head in enumerate(heads):
-        raw = head_back(head)
-        joint_parts[head] = exchange(raw)
+        joint_parts[head] = exchange(head_back(head))
+        if number < 3:
+            late_frames.step()
         if number == 0:
             other_rows = pick(result, 1 - side)
             if head_count > 1:
                 other_rows = run(copy_of, other_rows)
-            others = swap_with(other_rows, half)
-        if number == min(2, head_count - 1):
-            mixed = run(two_clips, result, others, LOW, frames)
-        step(down_chain, up_chain)
-        step(output_chain)
-        if number == 2:
-            for other in heads[:2]:
-                sent, kept, total = head_joint(other, total)
-                head_chains[other] = Chain(sent, kept, other_way if other % 2 else one_way)
-            mod_late, sum_late = run(
-                modulation_back, condition_of(jnp.arange(devices, dtype=jnp.int32)), late_pieces
-            )
-            step(*head_chains.values())
-    early_chains = list(head_chains.values())
-    late_chains = []
-    waiting = [head for head in heads if head not in head_chains]
-    for head in waiting:
-        sent, kept, total = head_joint(head, total)
-        head_chains[head] = Chain(sent, kept, other_way if head % 2 else one_way)
-        late_chains.append(head_chains[head])
-        step(*early_chains)
+            mixed_others = swap_with(other_rows, half)
+        if number == 2 and early_heads:
+            into = None
+            for other in early_heads:
+                total, into = head_joint(other, early_heads, total, into)
+            early_chain = Chain(owners(into[0]), owners(into[1]))
+        if number == 3:
+            early_chain.step()
+            mixed = run(two_clips, result, mixed_others, LOW, frames)
+            late_frames.step()
+        if number == 2 and early_heads:
+            early_chain.step()
+    into = None
+    for head in last_heads:
+        total, into = head_joint(head, last_heads, total, into)
+        if head == last_heads[0] and early_heads:
+            while early_chain.arrived is not None:
+                early_chain.step()
+    last_chain = Chain(owners(into[0]), owners(into[1]))
     own_rows, other_rows, early_rows = run(
         tokens_back, total, tokens, middle_grad, early, frames
     )
-    early_frames = Frames(early_rows)
-    others = swap_with(other_rows, half)
-    chains = late_chains + early_chains + [up_chain, output_chain, down_chain]
-    while any(chain.arrived is not None for chain in chains) or early_frames.arrived is not None:
-        step(*late_chains)
+    groups = [tuple(far[i : i + 2]) for i in range(0, len(far), 2)]
+    groups += [(core_mask,), (seq_masks[0], clip_masks[1])]
+    early_frames = Frames(early_rows, groups)
+    middle_row = local_rows // 2
+    others = [swap_with(other_rows[:middle_row], half)]
+    last_chain.step()
+    early_frames.step()
+    if head_count < 4:
+        mixed = run(two_clips, result, mixed_others, LOW, frames)
+    while late_frames.arrived is not None:
+        late_frames.step()
+    mod_late, sum_late = run(modulation_back, condition, late_frames.rows)
+    down_sum, up_sum, output_sum = run(settle, weight_sums, own_down, up_blocks)
+    early_frames.step()
+    last_chain.step()
+    others.append(swap_with(run(copy_of, other_rows[middle_row:]), half))
+    while early_frames.arrived is not None:
         early_frames.step()
-        step(*early_chains)
-        step(down_chain, up_chain)
-        step(output_chain)
-    if head_count < 3:
-        mod_late, sum_late = run(
-            modulation_back, condition_of(jnp.arange(devices, dtype=jnp.int32)), late_pieces
-        )
-    mod_early, sum_early = run(modulation_back, condition, early_frames.rows)
-    input_grad = run(two_clips, own_rows, others, WIDE, frames)
-
-    output_sum = output_chain.kept[0]
-    down_sum = down_chain.kept[0]
-    up_sum = up_chain.kept[0].reshape(up_blocks, own_up, D)
-    up_sum = jnp.transpose(up_sum, (1, 0, 2)).reshape(own_up, FF)
-    joint_sum = jnp.stack([head_chains[head].kept[0] for head in range(head_count)], axis=1)
+    mod_early, sum_early = run(
+        modulation_back, condition_of(ranks_of(groups)), early_frames.rows
+    )
+    while last_chain.arrived is not None:
+        last_chain.step()
+
+    joint_heads = {}
+    for chain, group in ((early_chain, early_heads), (last_chain, last_heads)):
+        for slot, head in enumerate(group):
+            width = 3 * D // head_count
+            joint_heads[head] = chain.kept[0][:, slot * width : (slot + 1) * width]
+    joint_sum = jnp.stack([joint_heads[head] for head in range(head_count)], axis=1)
     joint_sum = joint_sum.reshape(rows, head_count, 3, members, HEAD)
     joint_sum = jnp.transpose(joint_sum, (0, 2, 3, 1, 4)).reshape(rows, 3 * D)
     mod_sum = jnp.concatenate([mod_early, mod_late], axis=1)
@@ -1468,8 +1590,14 @@
 
     summed = (joint_sum, output_sum, up_sum, down_sum, mod_sum, bias_sum)
     squares = sum(jnp.sum(shard * shard) for shard in summed).reshape(1, 1)
-    for mask in order:
-        squares = squares + swap_with(squares, mask)
+    for first, second in zip(order[::2], order[1::2]):
+        squares = (squares + swap_with(squares, first)) + (
+            swap_with(squares, second) + swap_with(squares, first ^ second)
+        )
+    if len(order) % 2:
+        squares = squares + swap_with(squares, order[-1])
+    last.append(squares)
+    input_grad = run(two_clips, own_rows, jnp.concatenate(others), WIDE, frames)
     grad_norm = jnp.sqrt(squares[0, 0])
     factor = jnp.minimum(1.0, clip_limit / (grad_norm + 1e-06))
     step_rates = (

time: 1030 us -> 915 us (0.89)
  Pallas kernels: 632 us -> 543 us
  blocking collectives: 29 us -> 0 us
    pallas_call x66 -> x57, Pallas kernels: 632 us -> 543 us  [call(): pl.pallas_call(body, grid_spec=pltpu.PrefetchScalarGridSpec(num_scalar_pr...]
    all_to_all x2 -> x0, blocking collectives: 29 us -> none  [exchange(): return lax.all_to_all(value, 'seq', 0, 0, axis_index_groups=group_ids)]
    ppermute x68 -> x60, waiting for transfers between devices: 107 us -> 126 us  [swap_with(): return lax.ppermute(value, AXES, [(i, i ^ mask) for i in range(devices)])]
    all_to_all x10 -> x11, waiting for transfers between devices: 19.6 us -> 9.01 us  [exchange(): return lax.all_to_all(value, 'seq', 0, 0, axis_index_groups=group_ids)]
    unnamed x194 -> x187, local copies, waits for them, and re-layouts: 30.8 us -> 22.1 us
    ppermute x68 -> x60, starting transfers between devices: 94.8 us -> 88 us  [swap_with(): return lax.ppermute(value, AXES, [(i, i ^ mask) for i in range(devices)])]
    all_to_all x10 -> x11, starting transfers between devices: 43.2 us -> 48 us  [exchange(): return lax.all_to_all(value, 'seq', 0, 0, axis_index_groups=group_ids)]
  transfers between devices with their start and end apart: 81 -> 74, of which waited for: 19 -> 20; matrix products, arithmetic and copies ran while one was open for 3% -> 4% of each run, Pallas kernels for 53% -> 48%
where the time goes in v3:
time: 915 us; the launch traced here: 904 us
  Pallas kernels  543 us (59%)
  starting transfers between devices  142 us (16%)
  waiting for transfers between devices  135 us (15%)
  local copies, waits for them, and re-layouts  34.3 us (4%)
  between operations  25.2 us (3%)
  other arithmetic  23.2 us (3%)
    pallas_call x57, Pallas kernels, call(): pl.pallas_call(body, grid_spec=pltpu.PrefetchScalarGridSpec(num_scalar_pr...  543 us
    ppermute x60, waiting for transfers between devices, swap_with(): return lax.ppermute(value, AXES, [(i, i ^ mask) for i in range(devices)])  126 us
    ppermute x60, starting transfers between devices, swap_with(): return lax.ppermute(value, AXES, [(i, i ^ mask) for i in range(devices)])  88 us
    all_to_all x11, starting transfers between devices, exchange(): return lax.all_to_all(value, 'seq', 0, 0, axis_index_groups=group_ids)  48 us
    unnamed x187, local copies, waits for them, and re-layouts  22.1 us
  transfers between devices with their start and end apart: 74, of which 20 were waited for; matrix products, arithmetic and copies ran while one was open for 4% of the time, Pallas kernels for 48%

profile of v3, /device:TPU:0, one launch (start us, length us, event | category | flops | bytes accessed | tf_op | source)
XLA Modules:
  0.0 904.0 jit_solution(9804618577842300971)
XLA Ops:
  37.0 18.2 %collective-permute-done.1 = bf16[1,64,3072]{2,1,0:T(8,128)(2,1)S(1)} collective-permute-done((bf16[1,64,3072]{2,1,0:T(8,128)(2,1)}, bf16[1,64,3072]{2,1,0:T(8,128)(2,1)S(1)}, u32[]{:S(2)}, u32[]{:S(2)}) %collective-permute-start.1) | collective-permute-done | bytes 393248 | tf_op jit(solution)/shard_map/ppermute | solution.py:1210
  64.1 24.0 %collective-permute-done.7.refs_6_ = f32[32,2048]{1,0:T(8,128)S(1)} collective-permute-done((f32[32,2048]{1,0:T(8,128)}, f32[32,2048]{1,0:T(8,128)S(1)}, u32[]{:S(2)}, u32[]{:S(2)}) %collective-permute-start.7) | collective-permute-done | bytes 262176 | tf_op jit(solution)/shard_map/ppermute | solution.py:1210
  95.1 20.0 %collective-permute-done.10.refs_6_ = f32[16,2048]{1,0:T(8,128)S(1)} collective-permute-done((f32[16,2048]{1,0:T(8,128)}, f32[16,2048]{1,0:T(8,128)S(1)}, u32[]{:S(2)}, u32[]{:S(2)}) %collective-permute-start.10) | collective-permute-done | bytes 131104 | tf_op jit(solution)/shard_map/ppermute | solution.py:1210
  126.1 6.5 collective-permute-done.13.refs_6_
  134.3 6.6 join_and_add.15
  142.2 6.3 collective-permute-done.14.refs_2_
  175.7 6.2 project.5.refs_3_
  182.0 6.7 collective-permute-done.16.refs_2_
  193.8 6.3 collective-permute-done.17.refs_2_
  208.4 19.1 %attend.4 = (bf16[4,192,1024]{2,1,0:T(8,128)(2,1)}, f32[64,4096]{1,0:T(8,128)}, f32[1,4096]{1,0:T(1,128)}) custom-call(s32[3]{0:T(128)} %pad_add_fusion.refs_0_, bf16[4,3,64,1024]{3,2,1,0:T(8,128)(2,1)} %copy-done.7, f32[8,4096]{1,0:T(8,128)} %get-tuple-element.140.refs_2_), custom_call_target="tpu_custom_call" | custom-call | flops 20700000256 | bytes 54000000 | tf_op jit(solution)/shard_map/attend/pallas_call | solution.py:116
  230.2 6.3 project.6.refs_3_
  244.0 19.1 %attend.5 = (bf16[4,192,1024]{2,1,0:T(8,128)(2,1)}, f32[64,4096]{1,0:T(8,128)}, f32[1,4096]{1,0:T(1,128)}) custom-call(s32[3]{0:T(128)} %pad_add_fusion.refs_0_, bf16[4,3,64,1024]{3,2,1,0:T(8,128)(2,1)} %copy-done.8, bf16[4,192,1024]{2,1,0:T(8,128)(2,1)} %get-tuple-element.142.refs_2_, ...), custom_call_target="tpu_custom_call", output_to_operand_aliasing={{0}: (2, {})} | custom-call | flops 20700000256 | bytes 54000000 | tf_op jit(solution)/shard_map/attend/pallas_call | solution.py:116
  263.1 6.2 project.7.refs_3_
  277.4 16.1 %collective-permute-done.19.refs_2_ = f32[4,4096]{1,0:T(4,128)S(1)} collective-permute-done((f32[4,4096]{1,0:T(4,128)S(1)}, f32[4,4096]{1,0:T(4,128)S(1)}, u32[]{:S(2)}, u32[]{:S(2)}) %collective-permute-start.19) | collective-permute-done | bytes 65568 | tf_op jit(solution)/shard_map/ppermute | solution.py:1210
  296.3 19.0 %attend.6 = (bf16[4,192,1024]{2,1,0:T(8,128)(2,1)}, f32[64,4096]{1,0:T(8,128)}, f32[1,4096]{1,0:T(1,128)}) custom-call(s32[3]{0:T(128)} %pad_add_fusion.refs_0_, bf16[4,3,64,1024]{3,2,1,0:T(8,128)(2,1)} %copy-done.9, bf16[4,192,1024]{2,1,0:T(8,128)(2,1)} %get-tuple-element.145.refs_2_, ...), custom_call_target="tpu_custom_call", output_to_operand_aliasing={{0}: (2, {})} | custom-call | flops 20700000256 | bytes 54000000 | tf_op jit(solution)/shard_map/attend/pallas_call | solution.py:116
  315.3 8.1 all-to-all-start.4
  324.8 19.1 %attend.7 = (bf16[4,64,1024]{2,1,0:T(8,128)(2,1)}, f32[64,4096]{1,0:T(8,128)}, f32[1,4096]{1,0:T(1,128)}) custom-call(s32[3]{0:T(128)} %pad_add_fusion.refs_0_, bf16[4,3,64,1024]{3,2,1,0:T(8,128)(2,1)} %copy-done.10, f32[1,4096]{1,0:T(1,128)} %get-tuple-element.149.refs_2_.refs_4_, bf16[512,1024]{1,0:T(8,128)(2,1)} %collective-permute-done.20.refs_3_.refs_9_.refs_6_), custom_call_target="tpu_custom_call" | custom-call | flops 20700000256 | bytes 54000000 | tf_op jit(solution)/shard_map/attend/pallas_call | solution.py:116
  355.1 11.6 %middle_part.1 = (bf16[1024,1024]{1,0:T(8,128)(2,1)}, f32[1024,1024]{1,0:T(8,128)}, f32[1024,1024]{1,0:T(8,128)}, bf16[1024,1024]{1,0:T(8,128)(2,1)}, bf16[1024,1024]{1,0:T(8,128)(2,1)}) custom-call(s32[3]{0:T(128)} %pad_add_fusion.refs_0_, bf16[4,192,1024]{2,1,0:T(8,128)(2,1)} %copy-done.14, bf16[64,1024]{1,0:T(8,128)(2,1)} %get-tuple-element.257.refs_2_, ...), custom_call_target="tpu_custom_call" | custom-call | flops 13799999488 | bytes 36000000 | tf_op jit(solution)/shard_map/middle_part/pallas_call | solution.py:116
  366.6 66.8 %feed.1 = (f32[1024,1024]{1,0:T(8,128)}, f32[1024,1024]{1,0:T(8,128)}, bf16[32,288,1024]{2,1,0:T(8,128)(2,1)}) custom-call(s32[3]{0:T(128)} %pad_add_fusion.refs_0_, bf16[1024,1024]{1,0:T(8,128)(2,1)} %get-tuple-element.153.refs_1_, bf16[1024,1024]{1,0:T(8,128)(2,1)} %get-tuple-element.154.refs_2_.refs_5_, bf16[32,288,1024]{2,1,0:T(8,128)(2,1)} %bitcast.89, ...), custom_call_target="tpu_custom_call" | custom-call | flops 73600000000 | bytes 192000000 | tf_op jit(solution)/shard_map/feed/pallas_call | solution.py:116
  433.4 13.0 %middle_back.1 = (bf16[2,512,1024]{2,1,0:T(8,128)(2,1)}, f32[1024,1024]{1,0:T(8,128)}, bf16[1024,1024]{1,0:T(8,128)(2,1)}, f32[4,4096]{1,0:T(4,128)}) custom-call(s32[3]{0:T(128)} %pad_add_fusion.refs_0_, f32[1024,1024]{1,0:T(8,128)} %get-tuple-element.152.refs_1_, f32[1024,1024]{1,0:T(8,128)} %get-tuple-element.155.refs_2_, ...), custom_call_target="tpu_custom_call" | custom-call | flops 13799999488 | bytes 36000000 | tf_op jit(solution)/shard_map/middle_back/pallas_call | solution.py:116
  446.5 9.4 %hand_out.1 = (bf16[32,288,1024]{2,1,0:T(8,128)(2,1)}, bf16[4,64,1024]{2,1,0:T(8,128)(2,1)}, bf16[4,192,1024]{2,1,0:T(8,128)(2,1)}) custom-call(s32[3]{0:T(128)} %pad_add_fusion.refs_0_, bf16[32,288,1024]{2,1,0:T(8,128)(2,1)} %bitcast.91, bf16[1024,1024]{1,0:T(8,128)(2,1)} %get-tuple-element.161.refs_2_, ...), custom_call_target="tpu_custom_call", output_to_operand_aliasing={{0}: (4, {})} | custom-call | flops 10350000128 | bytes 27000000 | tf_op jit(solution)/shard_map/hand_out/pallas_call | solution.py:116
  475.8 43.3 %attend_back.4.refs_3_ = bf16[4,3,64,1024]{3,2,1,0:T(8,128)(2,1)} custom-call(s32[3]{0:T(128)} %pad_add_fusion.refs_0_, bf16[4,3,64,1024]{3,2,1,0:T(8,128)(2,1)} %copy-done.10, bf16[4,64,1024]{2,1,0:T(8,128)(2,1)} %copy-done.29, f32[64,4096]{1,0:T(8,128)} %get-tuple-element.165.refs_3_, f32[1,4096]{1,0:T(1,128)} %get-tuple-element.151.refs_11_.refs_4_, ...), custom_call_target="tpu_custom_call" | custom-call | flops 29899999232 | bytes 78000000 | tf_op jit(solution)/shard_map/attend_back/pallas_call | solution.py:116
  530.3 43.0 %attend_back.5.refs_3_ = bf16[4,3,64,1024]{3,2,1,0:T(8,128)(2,1)} custom-call(s32[3]{0:T(128)} %pad_add_fusion.refs_0_, bf16[4,3,64,1024]{3,2,1,0:T(8,128)(2,1)} %copy-done.9, bf16[4,192,1024]{2,1,0:T(8,128)(2,1)} %copy-done.11, f32[64,4096]{1,0:T(8,128)} %get-tuple-element.166.refs_3_, f32[1,4096]{1,0:T(1,128)} %get-tuple-element.149.refs_2_.refs_4_, ...), custom_call_target="tpu_custom_call" | custom-call | flops 29899999232 | bytes 78000000 | tf_op jit(solution)/shard_map/attend_back/pallas_call | solution.py:116
  585.4 43.1 %attend_back.6.refs_3_ = bf16[4,3,64,1024]{3,2,1,0:T(8,128)(2,1)} custom-call(s32[3]{0:T(128)} %pad_add_fusion.refs_0_, bf16[4,3,64,1024]{3,2,1,0:T(8,128)(2,1)} %copy-done.8, bf16[4,192,1024]{2,1,0:T(8,128)(2,1)} %copy-done.11, f32[64,4096]{1,0:T(8,128)} %get-tuple-element.167.refs_3_, f32[1,4096]{1,0:T(1,128)} %get-tuple-element.147.refs_5_.refs_4_, ...), custom_call_target="tpu_custom_call" | custom-call | flops 29899999232 | bytes 78000000 | tf_op jit(solution)/shard_map/attend_back/pallas_call | solution.py:116
  631.5 10.0 %joint_back.4 = (bf16[2,256,1536]{2,1,0:T(8,128)(2,1)}, f32[2,256,1536]{2,1,0:T(8,128)}, f32[1024,1024]{1,0:T(8,128)}) custom-call(s32[3]{0:T(128)} %pad_add_fusion.refs_0_, bf16[4,3,64,1024]{3,2,1,0:T(8,128)(2,1)} %copy-done.15, bf16[1024,1024]{1,0:T(8,128)(2,1)} %norm_one.1.refs_2_.refs_1_, bf16[1024,1536]{1,0:T(8,128)(2,1)} %bitcast.140, ...), custom_call_target="tpu_custom_call" | custom-call | flops 10350000128 | bytes 27000000 | tf_op jit(solution)/shard_map/joint_back/pallas_call | solution.py:116
  642.7 11.0 %joint_back.5 = (bf16[2,256,1536]{2,1,0:T(8,128)(2,1)}, f32[2,256,1536]{2,1,0:T(8,128)}, f32[1024,1024]{1,0:T(8,128)}) custom-call(s32[3]{0:T(128)} %pad_add_fusion.refs_0_, bf16[4,3,64,1024]{3,2,1,0:T(8,128)(2,1)} %copy-done.16, bf16[1024,1024]{1,0:T(8,128)(2,1)} %norm_one.1.refs_2_.refs_1_, ...), custom_call_target="tpu_custom_call", output_to_operand_aliasing={{0}: (5, {}), {1}: (6, {})} | custom-call | flops 10350000128 | bytes 27000000 | tf_op jit(solution)/shard_map/joint_back/pallas_call | solution.py:116
  669.6 43.0 %attend_back.7.refs_5_ = bf16[4,3,64,1024]{3,2,1,0:T(8,128)(2,1)} custom-call(s32[3]{0:T(128)} %pad_add_fusion.refs_0_, bf16[4,3,64,1024]{3,2,1,0:T(8,128)(2,1)} %copy-done.7, bf16[4,192,1024]{2,1,0:T(8,128)(2,1)} %copy-done.11, f32[64,4096]{1,0:T(8,128)} %get-tuple-element.178.refs_3_, f32[1,4096]{1,0:T(1,128)} %get-tuple-element.141.refs_2_.refs_4_, ...), custom_call_target="tpu_custom_call" | custom-call | flops 29899999232 | bytes 78000000 | tf_op jit(solution)/shard_map/attend_back/pallas_call | solution.py:116
  734.7 10.8 %joint_back.6 = (bf16[2,256,1536]{2,1,0:T(8,128)(2,1)}, f32[2,256,1536]{2,1,0:T(8,128)}, f32[1024,1024]{1,0:T(8,128)}) custom-call(s32[3]{0:T(128)} %pad_add_fusion.refs_0_, bf16[4,3,64,1024]{3,2,1,0:T(8,128)(2,1)} %copy-done.12, bf16[1024,1024]{1,0:T(8,128)(2,1)} %norm_one.1.refs_2_.refs_1_, bf16[1024,1536]{1,0:T(8,128)(2,1)} %bitcast.136, ...), custom_call_target="tpu_custom_call" | custom-call | flops 10350000128 | bytes 27000000 | tf_op jit(solution)/shard_map/joint_back/pallas_call | solution.py:116
  749.8 10.9 %joint_back.7 = (bf16[2,256,1536]{2,1,0:T(8,128)(2,1)}, f32[2,256,1536]{2,1,0:T(8,128)}, f32[1024,1024]{1,0:T(8,128)}) custom-call(s32[3]{0:T(128)} %pad_add_fusion.refs_0_, bf16[4,3,64,1024]{3,2,1,0:T(8,128)(2,1)} %copy-done.13, bf16[1024,1024]{1,0:T(8,128)(2,1)} %norm_one.1.refs_2_.refs_1_, ...), custom_call_target="tpu_custom_call", output_to_operand_aliasing={{0}: (5, {}), {1}: (6, {})} | custom-call | flops 10350000128 | bytes 27000000 | tf_op jit(solution)/shard_map/joint_back/pallas_call | solution.py:116
  761.1 8.3 tokens_back.1
  804.3 8.0 collective-permute-done.40
  851.6 11.7 %collective-permute-start.58 = (f32[1,1]{1,0:T(1,128)}, f32[1,1]{1,0:T(1,128)}, u32[]{:S(2)}, u32[]{:S(2)}) collective-permute-start(f32[1,1]{1,0:T(1,128)} %add.471), channel_id=1, source_target_pairs={{0,3},{1,2},{2,1},{3,0},{4,7},{5,6},{6,5},{7,4},{8,11},{9,10},{10,... | collective-permute-start | bytes 20 | tf_op jit(solution)/shard_map/ppermute | solution.py:1210
  (433 shorter events, 320.9 us)
Async XLA Ops:
  7.2 346.6 %all-gather.3.cloned.1.call-start = ((), (), s32[]{:S(2)}) async-start(), calls=%async_computation.14 | async-start | bytes 19464192 | tf_op jit(solution)/shard_map/all_gather | solution.py:1295
  28.7 26.5 %collective-permute-start.1 = (bf16[1,64,3072]{2,1,0:T(8,128)(2,1)}, bf16[1,64,3072]{2,1,0:T(8,128)(2,1)S(1)}, u32[]{:S(2)}, u32[]{:S(2)}) collective-permute-start(bf16[1,64,3072]{2,1,0:T(8,128)(2,1)} %bitcast.124), channel_id=1, source_target_pairs={{0,2},{1,3},{2,0},{3,1},{4,6},{5,7},{6,4},{7,5},{8,10},{9,11},{10,... | collective-permute-start | bytes 1179656 | tf_op jit(solution)/shard_map/ppermute | solution.py:1210
  31.6 83.5 %all-to-all-start = ((bf16[2,512,1024]{2,1,0:T(8,128)(2,1)}), bf16[2,512,1024]{2,1,0:T(8,128)(2,1)S(1)}, u32[]{:S(2)}, u32[]{:S(2)}) async-start(bf16[2,512,1024]{2,1,0:T(8,128)(2,1)} %param.24), calls=%async_computation | async-start | bytes 4194304 | tf_op jit(solution)/shard_map/all_to_all | solution.py:1230
  60.3 27.8 %collective-permute-start.6 = (bf16[1,128,1536]{2,1,0:T(8,128)(2,1)S(1)}, bf16[1,128,1536]{2,1,0:T(8,128)(2,1)S(1)}, u32[]{:S(2)}, u32[]{:S(2)}) collective-permute-start(bf16[1,128,1536]{2,1,0:T(8,128)(2,1)S(1)} %get-tuple-element.252.refs_3_), channel_id=1, source_target_pairs={{0,16},{1,17},{2,18},{3,19},{4,20},{5,21},{6,22},{7,23},{8,24},{9,... | collective-permute-start | bytes 1179656 | tf_op jit(solution)/shard_map/ppermute | solution.py:1210
  62.1 26.1 %collective-permute-start.5 = (bf16[1,128,1536]{2,1,0:T(8,128)(2,1)S(1)}, bf16[1,128,1536]{2,1,0:T(8,128)(2,1)S(1)}, u32[]{:S(2)}, u32[]{:S(2)}) collective-permute-start(bf16[1,128,1536]{2,1,0:T(8,128)(2,1)S(1)} %get-tuple-element.253), channel_id=1, source_target_pairs={{0,1},{1,0},{2,3},{3,2},{4,5},{5,4},{6,7},{7,6},{8,9},{9,8},{10,11... | collective-permute-start | bytes 1179656 | tf_op jit(solution)/shard_map/ppermute | solution.py:1210
  63.5 24.7 %collective-permute-start.7 = (f32[32,2048]{1,0:T(8,128)}, f32[32,2048]{1,0:T(8,128)S(1)}, u32[]{:S(2)}, u32[]{:S(2)}) collective-permute-start(f32[32,2048]{1,0:T(8,128)} %get-tuple-element.123.refs_7_), channel_id=1, source_target_pairs={{0,16},{1,17},{2,18},{3,19},{4,20},{5,21},{6,22},{7,23},{8,24},{9,... | collective-permute-start | bytes 786440 | tf_op jit(solution)/shard_map/ppermute | solution.py:1210
  167.5 37.1 %all-to-all-start.1 = ((bf16[4,3,64,1024]{3,2,1,0:T(8,128)(2,1)}), bf16[4,3,64,1024]{3,2,1,0:T(8,128)(2,1)S(1)}, u32[]{:S(2)}, u32[]{:S(2)}) async-start(bf16[4,3,64,1024]{3,2,1,0:T(8,128)(2,1)} %project.4.refs_3_), calls=%async_computation.1 | async-start | bytes 3145728 | tf_op jit(solution)/shard_map/all_to_all | solution.py:1361
  203.2 33.3 %collective-permute-start.18 = (f32[8,4096]{1,0:T(8,128)}, f32[8,4096]{1,0:T(8,128)S(1)}, u32[]{:S(2)}, u32[]{:S(2)}) collective-permute-start(f32[8,4096]{1,0:T(8,128)} %get-tuple-element.140.refs_2_), channel_id=1, source_target_pairs={{0,2},{1,3},{2,0},{3,1},{4,6},{5,7},{6,4},{7,5},{8,10},{9,11},{10,... | collective-permute-start | bytes 393224 | tf_op jit(solution)/shard_map/ppermute | solution.py:1210
  204.6 34.9 %all-to-all-start.3 = ((bf16[4,3,64,1024]{3,2,1,0:T(8,128)(2,1)}), bf16[4,3,64,1024]{3,2,1,0:T(8,128)(2,1)S(1)}, u32[]{:S(2)}, u32[]{:S(2)}) async-start(bf16[4,3,64,1024]{3,2,1,0:T(8,128)(2,1)} %project.5.refs_3_), calls=%async_computation.3 | async-start | bytes 3145728 | tf_op jit(solution)/shard_map/all_to_all | solution.py:1361
  239.5 29.9 %all-to-all-start.2 = ((bf16[4,3,64,1024]{3,2,1,0:T(8,128)(2,1)}), bf16[4,3,64,1024]{3,2,1,0:T(8,128)(2,1)S(1)}, u32[]{:S(2)}, u32[]{:S(2)}) async-start(bf16[4,3,64,1024]{3,2,1,0:T(8,128)(2,1)} %project.6.refs_3_), calls=%async_computation.2 | async-start | bytes 3145728 | tf_op jit(solution)/shard_map/all_to_all | solution.py:1361
  269.3 46.0 %all-to-all-start.5 = ((bf16[4,3,64,1024]{3,2,1,0:T(8,128)(2,1)}), bf16[4,3,64,1024]{3,2,1,0:T(8,128)(2,1)S(1)}, u32[]{:S(2)}, u32[]{:S(2)}) async-start(bf16[4,3,64,1024]{3,2,1,0:T(8,128)(2,1)} %project.7.refs_3_), calls=%async_computation.5 | async-start | bytes 3145728 | tf_op jit(solution)/shard_map/all_to_all | solution.py:1361
  277.3 47.5 %collective-permute-start.20 = (bf16[512,1024]{1,0:T(8,128)(2,1)}, bf16[512,1024]{1,0:T(8,128)(2,1)}, u32[]{:S(2)}, u32[]{:S(2)}) collective-permute-start(bf16[512,1024]{1,0:T(8,128)(2,1)} %other_clip.1.refs_5_), channel_id=1, source_target_pairs={{0,4},{1,5},{2,6},{3,7},{4,0},{5,1},{6,2},{7,3},{8,12},{9,13},{10,... | collective-permute-start | bytes 3145736 | tf_op jit(solution)/shard_map/ppermute | solution.py:1210
  315.3 38.5 %all-to-all-start.4 = ((bf16[4,192,1024]{2,1,0:T(8,128)(2,1)}), bf16[4,192,1024]{2,1,0:T(8,128)(2,1)S(1)}, u32[]{:S(2)}, u32[]{:S(2)}) async-start(bf16[4,192,1024]{2,1,0:T(8,128)(2,1)} %get-tuple-element.148), calls=%async_computation.4 | async-start | bytes 3145728 | tf_op jit(solution)/shard_map/all_to_all | solution.py:1361
  323.4 470.5 %reduce-scatter.2.cloned.1.call-start = ((), (), s32[]{:S(2)}) async-start(), calls=%async_computation.13 | async-start | bytes 19464192 | tf_op jit(solution)/shard_map/reduce_scatter | solution.py:1462
  467.1 59.3 %all-to-all-start.7 = ((bf16[4,192,1024]{2,1,0:T(8,128)(2,1)}), bf16[4,192,1024]{2,1,0:T(8,128)(2,1)S(1)}, u32[]{:S(2)}, u32[]{:S(2)}) async-start(bf16[4,192,1024]{2,1,0:T(8,128)(2,1)} %get-tuple-element.163.refs_3_), calls=%async_computation.7 | async-start | bytes 3145728 | tf_op jit(solution)/shard_map/all_to_all | solution.py:1361
  473.8 45.3 %collective-permute-start.25 = (f32[8,4096]{1,0:T(8,128)}, f32[8,4096]{1,0:T(8,128)S(1)}, u32[]{:S(2)}, u32[]{:S(2)}) collective-permute-start(f32[8,4096]{1,0:T(8,128)} %stack_rows.8.refs_7_.refs_1_), channel_id=1, source_target_pairs={{0,2},{1,3},{2,0},{3,1},{4,6},{5,7},{6,4},{7,5},{8,10},{9,11},{10,... | collective-permute-start | bytes 393224 | tf_op jit(solution)/shard_map/ppermute | solution.py:1210
  522.1 51.2 %collective-permute-start.27 = (f32[16,4096]{1,0:T(8,128)}, f32[16,4096]{1,0:T(8,128)S(1)}, u32[]{:S(2)}, u32[]{:S(2)}) collective-permute-start(f32[16,4096]{1,0:T(8,128)} %stack_rows.9.refs_2_.refs_1_), channel_id=1, source_target_pairs={{0,1},{1,0},{2,3},{3,2},{4,5},{5,4},{6,7},{7,6},{8,9},{9,8},{10,11... | collective-permute-start | bytes 786440 | tf_op jit(solution)/shard_map/ppermute | solution.py:1210
  526.5 55.0 %all-to-all-start.9 = ((bf16[4,3,64,1024]{3,2,1,0:T(8,128)(2,1)}), bf16[4,3,64,1024]{3,2,1,0:T(8,128)(2,1)S(1)}, u32[]{:S(2)}, u32[]{:S(2)}) async-start(bf16[4,3,64,1024]{3,2,1,0:T(8,128)(2,1)} %attend_back.4.refs_3_), calls=%async_computation.9 | async-start | bytes 3145728 | tf_op jit(solution)/shard_map/all_to_all | solution.py:1361
  576.5 52.0 %collective-permute-start.28 = (f32[32,4096]{1,0:T(8,128)}, f32[32,4096]{1,0:T(8,128)}, u32[]{:S(2)}, u32[]{:S(2)}) collective-permute-start(f32[32,4096]{1,0:T(8,128)} %stack_rows.10.refs_7_.refs_1_), channel_id=1, source_target_pairs={{0,16},{1,17},{2,18},{3,19},{4,20},{5,21},{6,22},{7,23},{8,24},{9,... | collective-permute-start | bytes 1572872 | tf_op jit(solution)/shard_map/ppermute | solution.py:1210
  581.4 60.1 %all-to-all-start.8 = ((bf16[4,3,64,1024]{3,2,1,0:T(8,128)(2,1)}), bf16[4,3,64,1024]{3,2,1,0:T(8,128)(2,1)S(1)}, u32[]{:S(2)}, u32[]{:S(2)}) async-start(bf16[4,3,64,1024]{3,2,1,0:T(8,128)(2,1)} %attend_back.5.refs_3_), calls=%async_computation.8 | async-start | bytes 3145728 | tf_op jit(solution)/shard_map/all_to_all | solution.py:1361
  653.7 71.6 %collective-permute-start.26 = (bf16[512,1024]{1,0:T(8,128)(2,1)}, bf16[512,1024]{1,0:T(8,128)(2,1)}, u32[]{:S(2)}, u32[]{:S(2)}) collective-permute-start(bf16[512,1024]{1,0:T(8,128)(2,1)} %copy_of.4.refs_7_), channel_id=1, source_target_pairs={{0,4},{1,5},{2,6},{3,7},{4,0},{5,1},{6,2},{7,3},{8,12},{9,13},{10,... | collective-permute-start | bytes 3145736 | tf_op jit(solution)/shard_map/ppermute | solution.py:1210
  656.2 56.4 %all-to-all-start.11 = ((bf16[4,3,64,1024]{3,2,1,0:T(8,128)(2,1)}), bf16[4,3,64,1024]{3,2,1,0:T(8,128)(2,1)S(1)}, u32[]{:S(2)}, u32[]{:S(2)}) async-start(bf16[4,3,64,1024]{3,2,1,0:T(8,128)(2,1)} %attend_back.6.refs_3_), calls=%async_computation.11 | async-start | bytes 3145728 | tf_op jit(solution)/shard_map/all_to_all | solution.py:1361
  666.1 51.0 %collective-permute-start.30 = (bf16[4,32,1536]{2,1,0:T(8,128)(2,1)}, bf16[4,32,1536]{2,1,0:T(8,128)(2,1)S(1)}, u32[]{:S(2)}, u32[]{:S(2)}) collective-permute-start(bf16[4,32,1536]{2,1,0:T(8,128)(2,1)} %bitcast.123), channel_id=1, source_target_pairs={{0,16},{1,17},{2,18},{3,19},{4,20},{5,21},{6,22},{7,23},{8,24},{9,... | collective-permute-start | bytes 1179656 | tf_op jit(solution)/shard_map/ppermute | solution.py:1210
  667.4 49.8 %collective-permute-start.31 = (bf16[4,32,1536]{2,1,0:T(8,128)(2,1)}, bf16[4,32,1536]{2,1,0:T(8,128)(2,1)}, u32[]{:S(2)}, u32[]{:S(2)}) collective-permute-start(bf16[4,32,1536]{2,1,0:T(8,128)(2,1)} %bitcast.122), channel_id=1, source_target_pairs={{0,1},{1,0},{2,3},{3,2},{4,5},{5,4},{6,7},{7,6},{8,9},{9,8},{10,11... | collective-permute-start | bytes 1179656 | tf_op jit(solution)/shard_map/ppermute | solution.py:1210
  669.4 47.8 %collective-permute-start.32 = (bf16[4,32,1536]{2,1,0:T(8,128)(2,1)}, bf16[4,32,1536]{2,1,0:T(8,128)(2,1)}, u32[]{:S(2)}, u32[]{:S(2)}) collective-permute-start(bf16[4,32,1536]{2,1,0:T(8,128)(2,1)} %bitcast.121), channel_id=1, source_target_pairs={{0,17},{1,16},{2,19},{3,18},{4,21},{5,20},{6,23},{7,22},{8,25},{9,... | collective-permute-start | bytes 1179656 | tf_op jit(solution)/shard_map/ppermute | solution.py:1210
  712.7 36.0 %all-to-all-start.10 = ((bf16[4,3,64,1024]{3,2,1,0:T(8,128)(2,1)}), bf16[4,3,64,1024]{3,2,1,0:T(8,128)(2,1)S(1)}, u32[]{:S(2)}, u32[]{:S(2)}) async-start(bf16[4,3,64,1024]{3,2,1,0:T(8,128)(2,1)} %attend_back.7.refs_5_), calls=%async_computation.10 | async-start | bytes 3145728 | tf_op jit(solution)/shard_map/all_to_all | solution.py:1361
  720.9 24.6 %collective-permute-start.34 = (bf16[1,32,1536]{2,1,0:T(8,128)(2,1)}, bf16[1,32,1536]{2,1,0:T(8,128)(2,1)S(1)}, u32[]{:S(2)}, u32[]{:S(2)}) collective-permute-start(bf16[1,32,1536]{2,1,0:T(8,128)(2,1)} %bitcast.133), channel_id=1, source_target_pairs={{0,4},{1,5},{2,6},{3,7},{4,0},{5,1},{6,2},{7,3},{8,12},{9,13},{10,... | collective-permute-start | bytes 294920 | tf_op jit(solution)/shard_map/ppermute | solution.py:1210
  721.6 23.9 %collective-permute-start.35 = (bf16[1,32,1536]{2,1,0:T(8,128)(2,1)}, bf16[1,32,1536]{2,1,0:T(8,128)(2,1)S(1)}, u32[]{:S(2)}, u32[]{:S(2)}) collective-permute-start(bf16[1,32,1536]{2,1,0:T(8,128)(2,1)} %bitcast.132), channel_id=1, source_target_pairs={{0,2},{1,3},{2,0},{3,1},{4,6},{5,7},{6,4},{7,5},{8,10},{9,11},{10,... | collective-permute-start | bytes 294920 | tf_op jit(solution)/shard_map/ppermute | solution.py:1210
  776.0 111.4 %collective-permute-start.37 = (bf16[256,1024]{1,0:T(8,128)(2,1)}, bf16[256,1024]{1,0:T(8,128)(2,1)}, u32[]{:S(2)}, u32[]{:S(2)}) collective-permute-start(bf16[256,1024]{1,0:T(8,128)(2,1)} %get-tuple-element.248), channel_id=1, source_target_pairs={{0,4},{1,5},{2,6},{3,7},{4,0},{5,1},{6,2},{7,3},{8,12},{9,13},{10,... | collective-permute-start | bytes 1572872 | tf_op jit(solution)/shard_map/ppermute | solution.py:1210
  787.1 25.2 %collective-permute-start.40 = (bf16[4,32,1536]{2,1,0:T(8,128)(2,1)S(1)}, bf16[4,32,1536]{2,1,0:T(8,128)(2,1)S(1)}, u32[]{:S(2)}, u32[]{:S(2)}) collective-permute-start(bf16[4,32,1536]{2,1,0:T(8,128)(2,1)S(1)} %bitcast.116), channel_id=1, source_target_pairs={{0,1},{1,0},{2,3},{3,2},{4,5},{5,4},{6,7},{7,6},{8,9},{9,8},{10,11... | collective-permute-start | bytes 1179656 | tf_op jit(solution)/shard_map/ppermute | solution.py:1210
  788.5 25.3 %collective-permute-start.41 = (bf16[4,32,1536]{2,1,0:T(8,128)(2,1)S(1)}, bf16[4,32,1536]{2,1,0:T(8,128)(2,1)}, u32[]{:S(2)}, u32[]{:S(2)}) collective-permute-start(bf16[4,32,1536]{2,1,0:T(8,128)(2,1)S(1)} %bitcast.115), channel_id=1, source_target_pairs={{0,17},{1,16},{2,19},{3,18},{4,21},{5,20},{6,23},{7,22},{8,25},{9,... | collective-permute-start | bytes 1179656 | tf_op jit(solution)/shard_map/ppermute | solution.py:1210
  824.8 62.6 %collective-permute-start.46 = (bf16[256,1024]{1,0:T(8,128)(2,1)}, bf16[256,1024]{1,0:T(8,128)(2,1)}, u32[]{:S(2)}, u32[]{:S(2)}) collective-permute-start(bf16[256,1024]{1,0:T(8,128)(2,1)} %copy_of.5.refs_5_), channel_id=1, source_target_pairs={{0,4},{1,5},{2,6},{3,7},{4,0},{5,1},{6,2},{7,3},{8,12},{9,13},{10,... | collective-permute-start | bytes 1572872 | tf_op jit(solution)/shard_map/ppermute | solution.py:1210
  (133 other events, 963.1 us)
Sparse Core Ops, SparseCore 0:
  11.6 161.1 all-gather.2
  456.1 262.8 reduce-scatter.1

commit v4 on v3

--- a/solution.py
+++ b/solution.py
@@ -883,34 +883,41 @@
     )
 
 
-def two_clips(ids, own, others, kind, frames, after=()):
-    rows = others.shape[0]
-    size = rows // frames
+def two_clips(ids, own, others, kind, after=()):
+    size = others[0].shape[0] // (2 // len(others))
     if own.ndim == 3:
         own_spec = pl.BlockSpec((1, size, D), lambda r, f, ids: (ids[1], f, 0))
     else:
         own_spec = pl.BlockSpec((size, D), lambda r, f, ids: (f, 0))
-
-    def kernel(ids_ref, own_ref, other_ref, out_ref):
+    if len(others) == 1:
+        other_specs = [pl.BlockSpec((size, D), lambda r, f, ids: (f, 0))]
+    else:
+        other_specs = [whole((size, D))] * 2
+
+    def kernel(ids_ref, own_ref, *refs):
+        *other_refs, out_ref = refs
         mine = pl.program_id(0) == ids_ref[1]
 
         @pl.when(mine)
         def _():
             out_ref[0] = own_ref[...].reshape(size, D).astype(kind)
 
-        @pl.when(jnp.logical_not(mine))
-        def _():
-            out_ref[0] = other_ref[...].astype(kind)
+        for number, ref in enumerate(other_refs):
+            here = pl.program_id(1) == number if len(other_refs) == 2 else True
+
+            @pl.when(jnp.logical_and(jnp.logical_not(mine), here))
+            def _(ref=ref):
+                out_ref[0] = ref[...].astype(kind)
 
     return call(
         kernel,
         "two_clips",
         ids,
-        (2, frames),
-        [own, others],
-        [own_spec, pl.BlockSpec((size, D), lambda r, f, ids: (f, 0))],
-        jax.ShapeDtypeStruct((2, rows, D), kind),
-        chunk_spec(rows, frames),
+        (2, 2),
+        [own, *others],
+        [own_spec, *other_specs],
+        jax.ShapeDtypeStruct((2, 2 * size, D), kind),
+        pl.BlockSpec((1, size, D), lambda r, f, ids: (r, f, 0)),
         after=after,
         time=4,
     )
@@ -1010,6 +1017,30 @@
         whole((len(values) * count, width)),
         after=after,
         time=1,
+    )
+
+
+def fold(ids, kept, arrived, count, after=()):
+    rows, width = kept.shape
+    part = rows // count
+
+    def kernel(ids_ref, *refs):
+        in_refs, out_refs = refs[: 1 + len(arrived)], refs[1 + len(arrived) :]
+        for number, out in enumerate(out_refs):
+            span = slice(number * part, (number + 1) * part)
+            out[...] = sum(ref[span] for ref in in_refs)
+
+    return call(
+        kernel,
+        "fold",
+        ids,
+        (1,),
+        [kept, *arrived],
+        [whole(kept.shape)] * (1 + len(arrived)),
+        [wide_array(part, width)] * count,
+        [whole((part, width))] * count,
+        after=after,
+        time=3,
     )
 
 
@@ -1360,15 +1391,26 @@
     def exchange(value):
         return lax.all_to_all(value, "seq", 0, 0, axis_index_groups=group_ids)
 
-    late_terms = Terms(run(copy_of, condition), 2 * D, 6 * D)
-
-    def late_step():
-        if late_terms.arrived is not None:
-            final = not late_terms.masks
-            outs = list(run(join_and_add, [], [late_terms.job()]))
-            late_terms.take(outs)
-            if final:
-                late_terms.arrived = None
+    class Late:
+        def __init__(self, condition):
+            terms = dot(condition, modulation_low[:, 2 * D :]) + bias_row[2 * D :]
+            self.groups = [(core_mask,)]
+            self.groups += [tuple(order[i : i + 2]) for i in range(1, len(order), 2)]
+            count = terms.shape[0] // 2
+            self.take([terms[:count], terms[count:]])
+
+        def take(self, parts):
+            self.kept, *sent = parts
+            self.arrived = None
+            if sent:
+                group = self.groups.pop(0)
+                ways = group if len(group) == 1 else (group[1], group[0], group[0] ^ group[1])
+                self.arrived = [swap_with(value, mask) for value, mask in zip(sent, ways)]
+
+        def step(self):
+            if self.arrived is not None:
+                count = 2 ** len(self.groups[0]) if self.groups else 1
+                self.take(run(fold, self.kept, self.arrived, count))
 
     def project_head(head):
         weight, offset = joint_sides[head // heads_aside], head % heads_aside
@@ -1377,18 +1419,15 @@
         )
 
     parts = {0: project_head(0)}
-    late_step()
+    late_terms = Late(run(copy_of, condition))
     wide, totals = {}, {}
     front = None
     front_heads = head_count - 1
     for head in range(head_count):
         if head + 1 < head_count:
             parts[head + 1] = project_head(head + 1)
-        else:
-            last.append(upstream[1] if head else tokens)
-        late_step()
         if head == 0:
-            late_step()
+            late_terms.step()
         if head < front_heads:
             front, wide[head], totals[head] = run(
                 attend, parts[head], front, head, front_heads, False
@@ -1397,11 +1436,18 @@
                 front = exchange(front)
         else:
             back, wide[head], totals[head] = run(attend, parts[head], None, 0, 1, True)
+        if head < 2:
+            late_terms.step()
         if head == 0:
-            upstream = (cotangent, swap_with(run(other_clip, cotangent, frames), half))
+            sent = run(other_clip, cotangent, frames)
+            cut = local_rows // 2
+            pieces = [swap_with(sent[:cut], half), swap_with(sent[cut:], half)]
+        if 0 < head < 3:
+            last.append(pieces[head - 1])
     while late_terms.arrived is not None:
-        late_step()
+        late_terms.step()
     late = late_terms.kept
+    upstream = (cotangent, jnp.concatenate(pieces))
     backs = [swap_with(back[i], i) if i else back[i] for i in range(members)]
 
     attended_across, projected, middle, normed_two_low, branch_grad = run(
@@ -1537,7 +1583,7 @@
             early_chain = Chain(owners(into[0]), owners(into[1]))
         if number == 3:
             early_chain.step()
-            mixed = run(two_clips, result, mixed_others, LOW, frames)
+            mixed = run(two_clips, result, [mixed_others], LOW)
             late_frames.step()
         if number == 2 and early_heads:
             early_chain.step()
@@ -1559,7 +1605,7 @@
     last_chain.step()
     early_frames.step()
     if head_count < 4:
-        mixed = run(two_clips, result, mixed_others, LOW, frames)
+        mixed = run(two_clips, result, [mixed_others], LOW)
     while late_frames.arrived is not None:
         late_frames.step()
     mod_late, sum_late = run(modulation_back, condition, late_frames.rows)
@@ -1594,10 +1640,10 @@
         squares = (squares + swap_with(squares, first)) + (
             swap_with(squares, second) + swap_with(squares, first ^ second)
         )
+        last.append(squares)
+    input_grad = run(two_clips, own_rows, others, WIDE)
     if len(order) % 2:
         squares = squares + swap_with(squares, order[-1])
-    last.append(squares)
-    input_grad = run(two_clips, own_rows, jnp.concatenate(others), WIDE, frames)
     grad_norm = jnp.sqrt(squares[0, 0])
     factor = jnp.minimum(1.0, clip_limit / (grad_norm + 1e-06))
     step_rates = (

time: 915 us -> 891 us (0.974)
  waiting for transfers between devices: 135 us -> 115 us
    ppermute x60 -> x63, waiting for transfers between devices: 126 us -> 96.3 us  [swap_with(): return lax.ppermute(value, AXES, [(i, i ^ mask) for i in range(devices)])]
    all_to_all x11, waiting for transfers between devices: 9.01 us -> 18.2 us  [exchange(): return lax.all_to_all(value, 'seq', 0, 0, axis_index_groups=group_ids)]
    pallas_call x57 -> x55, Pallas kernels: 543 us -> 538 us  [call(): pl.pallas_call(body, grid_spec=pltpu.PrefetchScalarGridSpec(num_scalar_pr...]
    ppermute x60 -> x63, starting transfers between devices: 88 us -> 90.3 us  [swap_with(): return lax.ppermute(value, AXES, [(i, i ^ mask) for i in range(devices)])]
    unnamed x187 -> x190, local copies, waits for them, and re-layouts: 22.1 us -> 22.2 us
  transfers between devices with their start and end apart: 74 -> 77, of which waited for: 20 -> 19; matrix products, arithmetic and copies ran while one was open for 4% -> 5% of each run, Pallas kernels for 48% -> 49%
where the time goes in v4:
time: 891 us; the launch traced here: 880 us
  Pallas kernels  538 us (60%)
  starting transfers between devices  141 us (16%)
  waiting for transfers between devices  115 us (13%)
  local copies, waits for them, and re-layouts  37.7 us (4%)
  between operations  25.3 us (3%)
  other arithmetic  21 us (2%)
    pallas_call x55, Pallas kernels, call(): pl.pallas_call(body, grid_spec=pltpu.PrefetchScalarGridSpec(num_scalar_pr...  538 us
    ppermute x63, waiting for transfers between devices, swap_with(): return lax.ppermute(value, AXES, [(i, i ^ mask) for i in range(devices)])  96.3 us
    ppermute x63, starting transfers between devices, swap_with(): return lax.ppermute(value, AXES, [(i, i ^ mask) for i in range(devices)])  90.3 us
    all_to_all x11, starting transfers between devices, exchange(): return lax.all_to_all(value, 'seq', 0, 0, axis_index_groups=group_ids)  45.3 us
    unnamed x190, local copies, waits for them, and re-layouts  22.2 us
    all_to_all x11, waiting for transfers between devices, exchange(): return lax.all_to_all(value, 'seq', 0, 0, axis_index_groups=group_ids)  18.2 us
  transfers between devices with their start and end apart: 77, of which 19 were waited for; matrix products, arithmetic and copies ran while one was open for 5% of the time, Pallas kernels for 49%

profile of v4, /device:TPU:0, one launch (start us, length us, event | category | flops | bytes accessed | tf_op | source)
XLA Modules:
  0.0 880.0 jit_solution(10260547800061716734)
XLA Ops:
  37.0 18.3 %collective-permute-done.1 = bf16[1,64,3072]{2,1,0:T(8,128)(2,1)} collective-permute-done((bf16[1,64,3072]{2,1,0:T(8,128)(2,1)}, bf16[1,64,3072]{2,1,0:T(8,128)(2,1)}, u32[]{:S(2)}, u32[]{:S(2)}) %collective-permute-start.1) | collective-permute-done | bytes 393248 | tf_op jit(solution)/shard_map/ppermute | solution.py:1241
  63.5 24.7 %collective-permute-done.7.refs_6_ = f32[32,2048]{1,0:T(8,128)S(1)} collective-permute-done((f32[32,2048]{1,0:T(8,128)}, f32[32,2048]{1,0:T(8,128)S(1)}, u32[]{:S(2)}, u32[]{:S(2)}) %collective-permute-start.7) | collective-permute-done | bytes 262176 | tf_op jit(solution)/shard_map/ppermute | solution.py:1241
  95.1 20.1 %collective-permute-done.10.refs_6_ = f32[16,2048]{1,0:T(8,128)S(1)} collective-permute-done((f32[16,2048]{1,0:T(8,128)}, f32[16,2048]{1,0:T(8,128)S(1)}, u32[]{:S(2)}, u32[]{:S(2)}) %collective-permute-start.10) | collective-permute-done | bytes 131104 | tf_op jit(solution)/shard_map/ppermute | solution.py:1241
  126.5 6.1 collective-permute-done.13.refs_6_
  134.3 6.6 join_and_add.10
  156.9 6.2 project.4.refs_2_
  171.7 6.2 project.5.refs_3_
  191.0 19.0 %attend.4 = (bf16[4,192,1024]{2,1,0:T(8,128)(2,1)}, f32[64,4096]{1,0:T(8,128)}, f32[1,4096]{1,0:T(1,128)}) custom-call(s32[3]{0:T(128)} %pad_add_fusion.refs_0_, bf16[4,3,64,1024]{3,2,1,0:T(8,128)(2,1)} %copy-done.7, f32[16,4096]{1,0:T(8,128)} %get-tuple-element.139.refs_2_), custom_call_target="tpu_custom_call" | custom-call | flops 20700000256 | bytes 54000000 | tf_op jit(solution)/shard_map/attend/pallas_call | solution.py:116
  224.8 6.2 project.6.refs_3_
  236.6 19.1 %attend.5 = (bf16[4,192,1024]{2,1,0:T(8,128)(2,1)}, f32[64,4096]{1,0:T(8,128)}, f32[1,4096]{1,0:T(1,128)}) custom-call(s32[3]{0:T(128)} %pad_add_fusion.refs_0_, bf16[4,3,64,1024]{3,2,1,0:T(8,128)(2,1)} %copy-done.8, bf16[4,192,1024]{2,1,0:T(8,128)(2,1)} %get-tuple-element.142.refs_2_, ...), custom_call_target="tpu_custom_call", output_to_operand_aliasing={{0}: (2, {})} | custom-call | flops 20700000256 | bytes 54000000 | tf_op jit(solution)/shard_map/attend/pallas_call | solution.py:116
  258.6 6.2 project.7.refs_3_
  269.3 19.0 %attend.6 = (bf16[4,192,1024]{2,1,0:T(8,128)(2,1)}, f32[64,4096]{1,0:T(8,128)}, f32[1,4096]{1,0:T(1,128)}) custom-call(s32[3]{0:T(128)} %pad_add_fusion.refs_0_, bf16[4,3,64,1024]{3,2,1,0:T(8,128)(2,1)} %copy-done.9, bf16[4,192,1024]{2,1,0:T(8,128)(2,1)} %get-tuple-element.143.refs_2_, ...), custom_call_target="tpu_custom_call", output_to_operand_aliasing={{0}: (2, {})} | custom-call | flops 20700000256 | bytes 54000000 | tf_op jit(solution)/shard_map/attend/pallas_call | solution.py:116
  288.3 9.3 %all-to-all-done.5.refs_1_ = bf16[4,3,64,1024]{3,2,1,0:T(8,128)(2,1)S(1)} async-done(((bf16[4,3,64,1024]{3,2,1,0:T(8,128)(2,1)}), bf16[4,3,64,1024]{3,2,1,0:T(8,128)(2,1)S(1)}, u32[]{:S(2)}, u32[]{:S(2)}) %all-to-all-start.5) | async-done | bytes 1572896 | tf_op jit(solution)/shard_map/all_to_all | solution.py:1392
  301.4 19.0 %attend.7 = (bf16[4,64,1024]{2,1,0:T(8,128)(2,1)}, f32[64,4096]{1,0:T(8,128)}, f32[1,4096]{1,0:T(1,128)}) custom-call(s32[3]{0:T(128)} %pad_add_fusion.refs_0_, bf16[4,3,64,1024]{3,2,1,0:T(8,128)(2,1)} %copy-done.10, f32[1,4096]{1,0:T(1,128)} %get-tuple-element.149.refs_2_.refs_4_, bf16[256,1024]{1,0:T(8,128)(2,1)} %collective-permute-done.23.refs_3_), custom_call_target="tpu_custom_call" | custom-call | flops 20700000256 | bytes 54000000 | tf_op jit(solution)/shard_map/attend/pallas_call | solution.py:116
  331.8 11.6 %middle_part.1 = (bf16[1024,1024]{1,0:T(8,128)(2,1)}, f32[1024,1024]{1,0:T(8,128)}, f32[1024,1024]{1,0:T(8,128)}, bf16[1024,1024]{1,0:T(8,128)(2,1)}, bf16[1024,1024]{1,0:T(8,128)(2,1)}) custom-call(s32[3]{0:T(128)} %pad_add_fusion.refs_0_, bf16[4,192,1024]{2,1,0:T(8,128)(2,1)} %copy-done.14, bf16[64,1024]{1,0:T(8,128)(2,1)} %get-tuple-element.259.refs_2_, ...), custom_call_target="tpu_custom_call" | custom-call | flops 13799999488 | bytes 36000000 | tf_op jit(solution)/shard_map/middle_part/pallas_call | solution.py:116
  343.4 66.7 %feed.1 = (f32[1024,1024]{1,0:T(8,128)}, f32[1024,1024]{1,0:T(8,128)}, bf16[32,288,1024]{2,1,0:T(8,128)(2,1)}) custom-call(s32[3]{0:T(128)} %pad_add_fusion.refs_0_, bf16[1024,1024]{1,0:T(8,128)(2,1)} %get-tuple-element.153.refs_1_, bf16[1024,1024]{1,0:T(8,128)(2,1)} %get-tuple-element.154.refs_2_.refs_5_, bf16[32,288,1024]{2,1,0:T(8,128)(2,1)} %bitcast.89, ...), custom_call_target="tpu_custom_call" | custom-call | flops 73600000000 | bytes 192000000 | tf_op jit(solution)/shard_map/feed/pallas_call | solution.py:116
  410.1 13.0 %middle_back.1 = (bf16[2,512,1024]{2,1,0:T(8,128)(2,1)}, f32[1024,1024]{1,0:T(8,128)}, bf16[1024,1024]{1,0:T(8,128)(2,1)}, f32[4,4096]{1,0:T(4,128)}) custom-call(s32[3]{0:T(128)} %pad_add_fusion.refs_0_, f32[1024,1024]{1,0:T(8,128)} %get-tuple-element.152.refs_1_, f32[1024,1024]{1,0:T(8,128)} %get-tuple-element.155.refs_2_, ...), custom_call_target="tpu_custom_call" | custom-call | flops 13799999488 | bytes 36000000 | tf_op jit(solution)/shard_map/middle_back/pallas_call | solution.py:116
  423.1 9.4 %hand_out.1 = (bf16[32,288,1024]{2,1,0:T(8,128)(2,1)}, bf16[4,64,1024]{2,1,0:T(8,128)(2,1)}, bf16[4,192,1024]{2,1,0:T(8,128)(2,1)}) custom-call(s32[3]{0:T(128)} %pad_add_fusion.refs_0_, bf16[32,288,1024]{2,1,0:T(8,128)(2,1)} %bitcast.91, bf16[1024,1024]{1,0:T(8,128)(2,1)} %get-tuple-element.161.refs_2_, ...), custom_call_target="tpu_custom_call", output_to_operand_aliasing={{0}: (4, {})} | custom-call | flops 10350000128 | bytes 27000000 | tf_op jit(solution)/shard_map/hand_out/pallas_call | solution.py:116
  437.4 7.3 all-to-all-done.6.refs_4_.refs_2_
  453.4 43.3 %attend_back.4.refs_3_ = bf16[4,3,64,1024]{3,2,1,0:T(8,128)(2,1)} custom-call(s32[3]{0:T(128)} %pad_add_fusion.refs_0_, bf16[4,3,64,1024]{3,2,1,0:T(8,128)(2,1)} %copy-done.10, bf16[4,64,1024]{2,1,0:T(8,128)(2,1)} %copy-done.29, f32[64,4096]{1,0:T(8,128)} %get-tuple-element.165.refs_3_, f32[1,4096]{1,0:T(1,128)} %get-tuple-element.151.refs_11_.refs_4_, ...), custom_call_target="tpu_custom_call" | custom-call | flops 29899999232 | bytes 78000000 | tf_op jit(solution)/shard_map/attend_back/pallas_call | solution.py:116
  507.9 43.0 %attend_back.5.refs_3_ = bf16[4,3,64,1024]{3,2,1,0:T(8,128)(2,1)} custom-call(s32[3]{0:T(128)} %pad_add_fusion.refs_0_, bf16[4,3,64,1024]{3,2,1,0:T(8,128)(2,1)} %copy-done.9, bf16[4,192,1024]{2,1,0:T(8,128)(2,1)} %copy-done.11, f32[64,4096]{1,0:T(8,128)} %get-tuple-element.166.refs_3_, f32[1,4096]{1,0:T(1,128)} %get-tuple-element.149.refs_2_.refs_4_, ...), custom_call_target="tpu_custom_call" | custom-call | flops 29899999232 | bytes 78000000 | tf_op jit(solution)/shard_map/attend_back/pallas_call | solution.py:116
  560.5 43.2 %attend_back.6.refs_3_ = bf16[4,3,64,1024]{3,2,1,0:T(8,128)(2,1)} custom-call(s32[3]{0:T(128)} %pad_add_fusion.refs_0_, bf16[4,3,64,1024]{3,2,1,0:T(8,128)(2,1)} %copy-done.8, bf16[4,192,1024]{2,1,0:T(8,128)(2,1)} %copy-done.11, f32[64,4096]{1,0:T(8,128)} %get-tuple-element.167.refs_3_, f32[1,4096]{1,0:T(1,128)} %get-tuple-element.147.refs_5_.refs_4_, ...), custom_call_target="tpu_custom_call" | custom-call | flops 29899999232 | bytes 78000000 | tf_op jit(solution)/shard_map/attend_back/pallas_call | solution.py:116
  606.6 10.0 %joint_back.4 = (bf16[2,256,1536]{2,1,0:T(8,128)(2,1)}, f32[2,256,1536]{2,1,0:T(8,128)}, f32[1024,1024]{1,0:T(8,128)}) custom-call(s32[3]{0:T(128)} %pad_add_fusion.refs_0_, bf16[4,3,64,1024]{3,2,1,0:T(8,128)(2,1)} %copy-done.15, bf16[1024,1024]{1,0:T(8,128)(2,1)} %norm_one.1.refs_1_.refs_5_.refs_2_, bf16[1024,1536]{1,0:T(8,128)(2,1)} %bitcast.139, ...), custom_call_target="tpu_custom_call" | custom-call | flops 10350000128 | bytes 27000000 | tf_op jit(solution)/shard_map/joint_back/pallas_call | solution.py:116
  617.7 11.1 %joint_back.5 = (bf16[2,256,1536]{2,1,0:T(8,128)(2,1)}, f32[2,256,1536]{2,1,0:T(8,128)}, f32[1024,1024]{1,0:T(8,128)}) custom-call(s32[3]{0:T(128)} %pad_add_fusion.refs_0_, bf16[4,3,64,1024]{3,2,1,0:T(8,128)(2,1)} %copy-done.16, bf16[1024,1024]{1,0:T(8,128)(2,1)} %norm_one.1.refs_1_.refs_5_.refs_2_, ...), custom_call_target="tpu_custom_call", output_to_operand_aliasing={{0}: (5, {}), {1}: (6, {})} | custom-call | flops 10350000128 | bytes 27000000 | tf_op jit(solution)/shard_map/joint_back/pallas_call | solution.py:116
  644.9 43.0 %attend_back.7.refs_5_ = bf16[4,3,64,1024]{3,2,1,0:T(8,128)(2,1)} custom-call(s32[3]{0:T(128)} %pad_add_fusion.refs_0_, bf16[4,3,64,1024]{3,2,1,0:T(8,128)(2,1)} %copy-done.7, bf16[4,192,1024]{2,1,0:T(8,128)(2,1)} %copy-done.11, f32[64,4096]{1,0:T(8,128)} %get-tuple-element.178.refs_3_, f32[1,4096]{1,0:T(1,128)} %get-tuple-element.140.refs_5_.refs_4_, ...), custom_call_target="tpu_custom_call" | custom-call | flops 29899999232 | bytes 78000000 | tf_op jit(solution)/shard_map/attend_back/pallas_call | solution.py:116
  709.6 10.8 %joint_back.6 = (bf16[2,256,1536]{2,1,0:T(8,128)(2,1)}, f32[2,256,1536]{2,1,0:T(8,128)}, f32[1024,1024]{1,0:T(8,128)}) custom-call(s32[3]{0:T(128)} %pad_add_fusion.refs_0_, bf16[4,3,64,1024]{3,2,1,0:T(8,128)(2,1)} %copy-done.12, bf16[1024,1024]{1,0:T(8,128)(2,1)} %norm_one.1.refs_1_.refs_5_.refs_2_, bf16[1024,1536]{1,0:T(8,128)(2,1)} %bitcast.135, ...), custom_call_target="tpu_custom_call" | custom-call | flops 10350000128 | bytes 27000000 | tf_op jit(solution)/shard_map/joint_back/pallas_call | solution.py:116
  728.9 11.0 %joint_back.7 = (bf16[2,256,1536]{2,1,0:T(8,128)(2,1)}, f32[2,256,1536]{2,1,0:T(8,128)}, f32[1024,1024]{1,0:T(8,128)}) custom-call(s32[3]{0:T(128)} %pad_add_fusion.refs_0_, bf16[4,3,64,1024]{3,2,1,0:T(8,128)(2,1)} %copy-done.13, bf16[1024,1024]{1,0:T(8,128)(2,1)} %norm_one.1.refs_1_.refs_5_.refs_2_, ...), custom_call_target="tpu_custom_call", output_to_operand_aliasing={{0}: (5, {}), {1}: (6, {})} | custom-call | flops 10350000128 | bytes 27000000 | tf_op jit(solution)/shard_map/joint_back/pallas_call | solution.py:116
  740.2 8.3 tokens_back.1
  782.8 7.9 collective-permute-done.43
  825.1 7.2 collective-permute-start.57
  835.3 6.4 collective-permute-start.61
  865.7 5.9 two_clips.3
  (441 shorter events, 309.7 us)
Async XLA Ops:
  7.2 323.4 %all-gather.3.cloned.1.call-start = ((), (), s32[]{:S(2)}) async-start(), calls=%async_computation.14 | async-start | bytes 19464192 | tf_op jit(solution)/shard_map/all_gather | solution.py:1326
  28.7 26.6 %collective-permute-start.1 = (bf16[1,64,3072]{2,1,0:T(8,128)(2,1)}, bf16[1,64,3072]{2,1,0:T(8,128)(2,1)}, u32[]{:S(2)}, u32[]{:S(2)}) collective-permute-start(bf16[1,64,3072]{2,1,0:T(8,128)(2,1)} %bitcast.124), channel_id=1, source_target_pairs={{0,2},{1,3},{2,0},{3,1},{4,6},{5,7},{6,4},{7,5},{8,10},{9,11},{10,... | collective-permute-start | bytes 1179656 | tf_op jit(solution)/shard_map/ppermute | solution.py:1241
  31.6 83.6 %all-to-all-start = ((bf16[2,512,1024]{2,1,0:T(8,128)(2,1)}), bf16[2,512,1024]{2,1,0:T(8,128)(2,1)S(1)}, u32[]{:S(2)}, u32[]{:S(2)}) async-start(bf16[2,512,1024]{2,1,0:T(8,128)(2,1)} %param.24), calls=%async_computation | async-start | bytes 4194304 | tf_op jit(solution)/shard_map/all_to_all | solution.py:1261
  59.7 28.5 %collective-permute-start.6 = (bf16[1,128,1536]{2,1,0:T(8,128)(2,1)S(1)}, bf16[1,128,1536]{2,1,0:T(8,128)(2,1)S(1)}, u32[]{:S(2)}, u32[]{:S(2)}) collective-permute-start(bf16[1,128,1536]{2,1,0:T(8,128)(2,1)S(1)} %get-tuple-element.254.refs_3_), channel_id=1, source_target_pairs={{0,16},{1,17},{2,18},{3,19},{4,20},{5,21},{6,22},{7,23},{8,24},{9,... | collective-permute-start | bytes 1179656 | tf_op jit(solution)/shard_map/ppermute | solution.py:1241
  61.4 26.8 %collective-permute-start.5 = (bf16[1,128,1536]{2,1,0:T(8,128)(2,1)S(1)}, bf16[1,128,1536]{2,1,0:T(8,128)(2,1)S(1)}, u32[]{:S(2)}, u32[]{:S(2)}) collective-permute-start(bf16[1,128,1536]{2,1,0:T(8,128)(2,1)S(1)} %get-tuple-element.255), channel_id=1, source_target_pairs={{0,1},{1,0},{2,3},{3,2},{4,5},{5,4},{6,7},{7,6},{8,9},{9,8},{10,11... | collective-permute-start | bytes 1179656 | tf_op jit(solution)/shard_map/ppermute | solution.py:1241
  182.1 27.9 %collective-permute-start.16 = (f32[16,4096]{1,0:T(8,128)}, f32[16,4096]{1,0:T(8,128)S(1)}, u32[]{:S(2)}, u32[]{:S(2)}) collective-permute-start(f32[16,4096]{1,0:T(8,128)} %get-tuple-element.137), channel_id=1, source_target_pairs={{0,1},{1,0},{2,3},{3,2},{4,5},{5,4},{6,7},{7,6},{8,9},{9,8},{10,11... | collective-permute-start | bytes 786440 | tf_op jit(solution)/shard_map/ppermute | solution.py:1241
  184.1 25.9 %collective-permute-start.17 = (f32[16,4096]{1,0:T(8,128)}, f32[16,4096]{1,0:T(8,128)}, u32[]{:S(2)}, u32[]{:S(2)}) collective-permute-start(f32[16,4096]{1,0:T(8,128)} %get-tuple-element.138), channel_id=1, source_target_pairs={{0,16},{1,17},{2,18},{3,19},{4,20},{5,21},{6,22},{7,23},{8,24},{9,... | collective-permute-start | bytes 786440 | tf_op jit(solution)/shard_map/ppermute | solution.py:1241
  187.2 43.9 %all-to-all-start.3 = ((bf16[4,3,64,1024]{3,2,1,0:T(8,128)(2,1)}), bf16[4,3,64,1024]{3,2,1,0:T(8,128)(2,1)S(1)}, u32[]{:S(2)}, u32[]{:S(2)}) async-start(bf16[4,3,64,1024]{3,2,1,0:T(8,128)(2,1)} %project.5.refs_3_), calls=%async_computation.3 | async-start | bytes 3145728 | tf_op jit(solution)/shard_map/all_to_all | solution.py:1392
  213.4 42.3 %collective-permute-start.19 = (f32[4,4096]{1,0:T(4,128)}, f32[4,4096]{1,0:T(4,128)S(1)}, u32[]{:S(2)}, u32[]{:S(2)}) collective-permute-start(f32[4,4096]{1,0:T(4,128)} %get-tuple-element.145), channel_id=1, source_target_pairs={{0,4},{1,5},{2,6},{3,7},{4,0},{5,1},{6,2},{7,3},{8,12},{9,13},{10,... | collective-permute-start | bytes 196616 | tf_op jit(solution)/shard_map/ppermute | solution.py:1241
  216.4 39.3 %collective-permute-start.20 = (f32[4,4096]{1,0:T(4,128)}, f32[4,4096]{1,0:T(4,128)S(1)}, u32[]{:S(2)}, u32[]{:S(2)}) collective-permute-start(f32[4,4096]{1,0:T(4,128)} %get-tuple-element.146), channel_id=1, source_target_pairs={{0,2},{1,3},{2,0},{3,1},{4,6},{5,7},{6,4},{7,5},{8,10},{9,11},{10,... | collective-permute-start | bytes 196616 | tf_op jit(solution)/shard_map/ppermute | solution.py:1241
  218.4 37.3 %collective-permute-start.21 = (f32[4,4096]{1,0:T(4,128)}, f32[4,4096]{1,0:T(4,128)S(1)}, u32[]{:S(2)}, u32[]{:S(2)}) collective-permute-start(f32[4,4096]{1,0:T(4,128)} %get-tuple-element.141.refs_2_), channel_id=1, source_target_pairs={{0,6},{1,7},{2,4},{3,5},{4,2},{5,3},{6,0},{7,1},{8,14},{9,15},{10,... | collective-permute-start | bytes 196616 | tf_op jit(solution)/shard_map/ppermute | solution.py:1241
  223.4 35.2 %collective-permute-start.22 = (bf16[256,1024]{1,0:T(8,128)(2,1)}, bf16[256,1024]{1,0:T(8,128)(2,1)}, u32[]{:S(2)}, u32[]{:S(2)}) collective-permute-start(bf16[256,1024]{1,0:T(8,128)(2,1)} %get-tuple-element.251), channel_id=1, source_target_pairs={{0,4},{1,5},{2,6},{3,7},{4,0},{5,1},{6,2},{7,3},{8,12},{9,13},{10,... | collective-permute-start | bytes 1572872 | tf_op jit(solution)/shard_map/ppermute | solution.py:1241
  231.1 33.7 %all-to-all-start.2 = ((bf16[4,3,64,1024]{3,2,1,0:T(8,128)(2,1)}), bf16[4,3,64,1024]{3,2,1,0:T(8,128)(2,1)S(1)}, u32[]{:S(2)}, u32[]{:S(2)}) async-start(bf16[4,3,64,1024]{3,2,1,0:T(8,128)(2,1)} %project.6.refs_3_), calls=%async_computation.2 | async-start | bytes 3145728 | tf_op jit(solution)/shard_map/all_to_all | solution.py:1392
  264.8 32.7 %all-to-all-start.5 = ((bf16[4,3,64,1024]{3,2,1,0:T(8,128)(2,1)}), bf16[4,3,64,1024]{3,2,1,0:T(8,128)(2,1)S(1)}, u32[]{:S(2)}, u32[]{:S(2)}) async-start(bf16[4,3,64,1024]{3,2,1,0:T(8,128)(2,1)} %project.7.refs_3_), calls=%async_computation.5 | async-start | bytes 3145728 | tf_op jit(solution)/shard_map/all_to_all | solution.py:1392
  269.2 32.2 %collective-permute-start.23 = (bf16[256,1024]{1,0:T(8,128)(2,1)}, bf16[256,1024]{1,0:T(8,128)(2,1)}, u32[]{:S(2)}, u32[]{:S(2)}) collective-permute-start(bf16[256,1024]{1,0:T(8,128)(2,1)} %get-tuple-element.250), channel_id=1, source_target_pairs={{0,4},{1,5},{2,6},{3,7},{4,0},{5,1},{6,2},{7,3},{8,12},{9,13},{10,... | collective-permute-start | bytes 1572872 | tf_op jit(solution)/shard_map/ppermute | solution.py:1241
  297.6 33.0 %all-to-all-start.4 = ((bf16[4,192,1024]{2,1,0:T(8,128)(2,1)}), bf16[4,192,1024]{2,1,0:T(8,128)(2,1)S(1)}, u32[]{:S(2)}, u32[]{:S(2)}) async-start(bf16[4,192,1024]{2,1,0:T(8,128)(2,1)} %get-tuple-element.148), calls=%async_computation.4 | async-start | bytes 3145728 | tf_op jit(solution)/shard_map/all_to_all | solution.py:1392
  301.1 471.4 %reduce-scatter.2.cloned.1.call-start = ((), (), s32[]{:S(2)}) async-start(), calls=%async_computation.13 | async-start | bytes 19464192 | tf_op jit(solution)/shard_map/reduce_scatter | solution.py:1508
  444.7 59.3 %all-to-all-start.7 = ((bf16[4,192,1024]{2,1,0:T(8,128)(2,1)}), bf16[4,192,1024]{2,1,0:T(8,128)(2,1)S(1)}, u32[]{:S(2)}, u32[]{:S(2)}) async-start(bf16[4,192,1024]{2,1,0:T(8,128)(2,1)} %get-tuple-element.163.refs_3_), calls=%async_computation.7 | async-start | bytes 3145728 | tf_op jit(solution)/shard_map/all_to_all | solution.py:1392
  451.4 45.3 %collective-permute-start.28 = (f32[8,4096]{1,0:T(8,128)}, f32[8,4096]{1,0:T(8,128)S(1)}, u32[]{:S(2)}, u32[]{:S(2)}) collective-permute-start(f32[8,4096]{1,0:T(8,128)} %stack_rows.8.refs_7_.refs_1_), channel_id=1, source_target_pairs={{0,2},{1,3},{2,0},{3,1},{4,6},{5,7},{6,4},{7,5},{8,10},{9,11},{10,... | collective-permute-start | bytes 393224 | tf_op jit(solution)/shard_map/ppermute | solution.py:1241
  499.6 51.3 %collective-permute-start.30 = (f32[16,4096]{1,0:T(8,128)}, f32[16,4096]{1,0:T(8,128)S(1)}, u32[]{:S(2)}, u32[]{:S(2)}) collective-permute-start(f32[16,4096]{1,0:T(8,128)} %stack_rows.9.refs_2_.refs_1_), channel_id=1, source_target_pairs={{0,1},{1,0},{2,3},{3,2},{4,5},{5,4},{6,7},{7,6},{8,9},{9,8},{10,11... | collective-permute-start | bytes 786440 | tf_op jit(solution)/shard_map/ppermute | solution.py:1241
  504.1 51.8 %all-to-all-start.9 = ((bf16[4,3,64,1024]{3,2,1,0:T(8,128)(2,1)}), bf16[4,3,64,1024]{3,2,1,0:T(8,128)(2,1)S(1)}, u32[]{:S(2)}, u32[]{:S(2)}) async-start(bf16[4,3,64,1024]{3,2,1,0:T(8,128)(2,1)} %attend_back.4.refs_3_), calls=%async_computation.9 | async-start | bytes 3145728 | tf_op jit(solution)/shard_map/all_to_all | solution.py:1392
  554.1 49.5 %collective-permute-start.31 = (f32[32,4096]{1,0:T(8,128)}, f32[32,4096]{1,0:T(8,128)}, u32[]{:S(2)}, u32[]{:S(2)}) collective-permute-start(f32[32,4096]{1,0:T(8,128)} %stack_rows.10.refs_7_.refs_1_), channel_id=1, source_target_pairs={{0,16},{1,17},{2,18},{3,19},{4,20},{5,21},{6,22},{7,23},{8,24},{9,... | collective-permute-start | bytes 1572872 | tf_op jit(solution)/shard_map/ppermute | solution.py:1241
  555.9 60.7 %all-to-all-start.8 = ((bf16[4,3,64,1024]{3,2,1,0:T(8,128)(2,1)}), bf16[4,3,64,1024]{3,2,1,0:T(8,128)(2,1)S(1)}, u32[]{:S(2)}, u32[]{:S(2)}) async-start(bf16[4,3,64,1024]{3,2,1,0:T(8,128)(2,1)} %attend_back.5.refs_3_), calls=%async_computation.8 | async-start | bytes 3145728 | tf_op jit(solution)/shard_map/all_to_all | solution.py:1392
  628.8 71.3 %collective-permute-start.29 = (bf16[512,1024]{1,0:T(8,128)(2,1)}, bf16[512,1024]{1,0:T(8,128)(2,1)}, u32[]{:S(2)}, u32[]{:S(2)}) collective-permute-start(bf16[512,1024]{1,0:T(8,128)(2,1)} %copy_of.4.refs_7_), channel_id=1, source_target_pairs={{0,4},{1,5},{2,6},{3,7},{4,0},{5,1},{6,2},{7,3},{8,12},{9,13},{10,... | collective-permute-start | bytes 3145736 | tf_op jit(solution)/shard_map/ppermute | solution.py:1241
  630.2 57.8 %all-to-all-start.11 = ((bf16[4,3,64,1024]{3,2,1,0:T(8,128)(2,1)}), bf16[4,3,64,1024]{3,2,1,0:T(8,128)(2,1)S(1)}, u32[]{:S(2)}, u32[]{:S(2)}) async-start(bf16[4,3,64,1024]{3,2,1,0:T(8,128)(2,1)} %attend_back.6.refs_3_), calls=%async_computation.11 | async-start | bytes 3145728 | tf_op jit(solution)/shard_map/all_to_all | solution.py:1392
  640.3 51.7 %collective-permute-start.33 = (bf16[4,32,1536]{2,1,0:T(8,128)(2,1)}, bf16[4,32,1536]{2,1,0:T(8,128)(2,1)S(1)}, u32[]{:S(2)}, u32[]{:S(2)}) collective-permute-start(bf16[4,32,1536]{2,1,0:T(8,128)(2,1)} %bitcast.123), channel_id=1, source_target_pairs={{0,16},{1,17},{2,18},{3,19},{4,20},{5,21},{6,22},{7,23},{8,24},{9,... | collective-permute-start | bytes 1179656 | tf_op jit(solution)/shard_map/ppermute | solution.py:1241
  642.9 49.1 %collective-permute-start.34 = (bf16[4,32,1536]{2,1,0:T(8,128)(2,1)}, bf16[4,32,1536]{2,1,0:T(8,128)(2,1)}, u32[]{:S(2)}, u32[]{:S(2)}) collective-permute-start(bf16[4,32,1536]{2,1,0:T(8,128)(2,1)} %bitcast.122), channel_id=1, source_target_pairs={{0,1},{1,0},{2,3},{3,2},{4,5},{5,4},{6,7},{7,6},{8,9},{9,8},{10,11... | collective-permute-start | bytes 1179656 | tf_op jit(solution)/shard_map/ppermute | solution.py:1241
  644.9 47.1 %collective-permute-start.35 = (bf16[4,32,1536]{2,1,0:T(8,128)(2,1)}, bf16[4,32,1536]{2,1,0:T(8,128)(2,1)}, u32[]{:S(2)}, u32[]{:S(2)}) collective-permute-start(bf16[4,32,1536]{2,1,0:T(8,128)(2,1)} %bitcast.121), channel_id=1, source_target_pairs={{0,17},{1,16},{2,19},{3,18},{4,21},{5,20},{6,23},{7,22},{8,25},{9,... | collective-permute-start | bytes 1179656 | tf_op jit(solution)/shard_map/ppermute | solution.py:1241
  688.0 39.7 %all-to-all-start.10 = ((bf16[4,3,64,1024]{3,2,1,0:T(8,128)(2,1)}), bf16[4,3,64,1024]{3,2,1,0:T(8,128)(2,1)S(1)}, u32[]{:S(2)}, u32[]{:S(2)}) async-start(bf16[4,3,64,1024]{3,2,1,0:T(8,128)(2,1)} %attend_back.7.refs_5_), calls=%async_computation.10 | async-start | bytes 3145728 | tf_op jit(solution)/shard_map/all_to_all | solution.py:1392
  698.7 26.0 %collective-permute-start.39 = (bf16[1,32,1536]{2,1,0:T(8,128)(2,1)}, bf16[1,32,1536]{2,1,0:T(8,128)(2,1)S(1)}, u32[]{:S(2)}, u32[]{:S(2)}) collective-permute-start(bf16[1,32,1536]{2,1,0:T(8,128)(2,1)} %bitcast.130), channel_id=1, source_target_pairs={{0,6},{1,7},{2,4},{3,5},{4,2},{5,3},{6,0},{7,1},{8,14},{9,15},{10,... | collective-permute-start | bytes 294920 | tf_op jit(solution)/shard_map/ppermute | solution.py:1241
  755.1 110.6 %collective-permute-start.40 = (bf16[256,1024]{1,0:T(8,128)(2,1)}, bf16[256,1024]{1,0:T(8,128)(2,1)}, u32[]{:S(2)}, u32[]{:S(2)}) collective-permute-start(bf16[256,1024]{1,0:T(8,128)(2,1)} %get-tuple-element.249), channel_id=1, source_target_pairs={{0,4},{1,5},{2,6},{3,7},{4,0},{5,1},{6,2},{7,3},{8,12},{9,13},{10,... | collective-permute-start | bytes 1572872 | tf_op jit(solution)/shard_map/ppermute | solution.py:1241
  803.3 62.4 %collective-permute-start.49 = (bf16[256,1024]{1,0:T(8,128)(2,1)}, bf16[256,1024]{1,0:T(8,128)(2,1)}, u32[]{:S(2)}, u32[]{:S(2)}) collective-permute-start(bf16[256,1024]{1,0:T(8,128)(2,1)} %copy_of.5.refs_5_), channel_id=1, source_target_pairs={{0,4},{1,5},{2,6},{3,7},{4,0},{5,1},{6,2},{7,3},{8,12},{9,13},{10,... | collective-permute-start | bytes 1572872 | tf_op jit(solution)/shard_map/ppermute | solution.py:1241
  (137 other events, 1055.5 us)
Sparse Core Ops, SparseCore 0:
  11.6 161.3 all-gather.2
  432.7 274.1 reduce-scatter.1

commit v5 on v4

--- a/solution.py
+++ b/solution.py
@@ -830,7 +830,7 @@
         [pltpu.VMEM((width, tokens), LOW), pltpu.VMEM((tokens, width), LOW)],
         after,
         aliases={first: 0, first + 1: 1} if held else {},
-        time=9,
+        time=13,
     )
 
 
@@ -851,7 +851,7 @@
 
         @pl.when(pl.program_id(0) == ids_ref[1])
         def _():
-            own_ref[...] = grad
+            own_ref[0] = grad
 
         @pl.when(pl.program_id(0) != ids_ref[1])
         def _():
@@ -872,9 +872,9 @@
         (2, frames),
         [gradient, tokens, middle_grad, early],
         [block, chunk_spec(rows, frames), block, whole(early.shape)],
-        [wide_array(rows, D), low_array(rows, D), wide_array(2 * frames, 2 * D)],
+        [wide_array(2, rows, D), low_array(rows, D), wide_array(2 * frames, 2 * D)],
         [
-            pl.BlockSpec((size, D), chunk_at(0)),
+            pl.BlockSpec((1, size, D), lambda r, f, ids: (ids[1], *chunk_at(0)(r, f, ids))),
             pl.BlockSpec((size, D), chunk_at(1)),
             whole((2 * frames, 2 * D)),
         ],
@@ -883,42 +883,33 @@
     )
 
 
-def two_clips(ids, own, others, kind, after=()):
-    size = others[0].shape[0] // (2 // len(others))
-    if own.ndim == 3:
-        own_spec = pl.BlockSpec((1, size, D), lambda r, f, ids: (ids[1], f, 0))
-    else:
-        own_spec = pl.BlockSpec((size, D), lambda r, f, ids: (f, 0))
+def fill_clip(ids, held, others, after=()):
+    size = held.shape[1] // 2
     if len(others) == 1:
-        other_specs = [pl.BlockSpec((size, D), lambda r, f, ids: (f, 0))]
+        other_specs = [pl.BlockSpec((size, D), lambda f, ids: (f, 0))]
     else:
         other_specs = [whole((size, D))] * 2
 
-    def kernel(ids_ref, own_ref, *refs):
+    def kernel(ids_ref, held_ref, *refs):
         *other_refs, out_ref = refs
-        mine = pl.program_id(0) == ids_ref[1]
-
-        @pl.when(mine)
-        def _():
-            out_ref[0] = own_ref[...].reshape(size, D).astype(kind)
-
         for number, ref in enumerate(other_refs):
-            here = pl.program_id(1) == number if len(other_refs) == 2 else True
-
-            @pl.when(jnp.logical_and(jnp.logical_not(mine), here))
+            here = pl.program_id(0) == number if len(other_refs) == 2 else True
+
+            @pl.when(here)
             def _(ref=ref):
-                out_ref[0] = ref[...].astype(kind)
-
-    return call(
-        kernel,
-        "two_clips",
-        ids,
-        (2, 2),
-        [own, *others],
-        [own_spec, *other_specs],
-        jax.ShapeDtypeStruct((2, 2 * size, D), kind),
-        pl.BlockSpec((1, size, D), lambda r, f, ids: (r, f, 0)),
+                out_ref[0] = ref[...].astype(held.dtype)
+
+    return call(
+        kernel,
+        "fill_clip",
+        ids,
+        (2,),
+        [held, *others],
+        [anywhere, *other_specs],
+        jax.ShapeDtypeStruct(held.shape, held.dtype),
+        pl.BlockSpec((1, size, D), lambda f, ids: (1 - ids[1], f, 0)),
         after=after,
+        aliases={1: 0},
         time=4,
     )
 
@@ -1534,7 +1525,10 @@
             masks = masks + [other ^ mask for other in masks]
         return rank ^ jnp.array(masks, jnp.int32)
 
-    late_frames = Frames(late_rows, [(mask,) for mask in reversed(order)])
+    groups = [tuple(far[i : i + 2]) for i in range(0, len(far), 2)]
+    groups += [(core_mask,), (seq_masks[0], clip_masks[1])]
+    frames_condition = condition_of(ranks_of(groups))
+    late_frames = Frames(late_rows, groups)
     late_frames.step()
 
     def head_back(head):
@@ -1572,10 +1566,7 @@
         if number < 3:
             late_frames.step()
         if number == 0:
-            other_rows = pick(result, 1 - side)
-            if head_count > 1:
-                other_rows = run(copy_of, other_rows)
-            mixed_others = swap_with(other_rows, half)
+            mixed_others = swap_with(pick(result, 1 - side), half)
         if number == 2 and early_heads:
             into = None
             for other in early_heads:
@@ -1583,7 +1574,7 @@
             early_chain = Chain(owners(into[0]), owners(into[1]))
         if number == 3:
             early_chain.step()
-            mixed = run(two_clips, result, [mixed_others], LOW)
+            mixed = run(fill_clip, result, [mixed_others])
             late_frames.step()
         if number == 2 and early_heads:
             early_chain.step()
@@ -1597,27 +1588,23 @@
     own_rows, other_rows, early_rows = run(
         tokens_back, total, tokens, middle_grad, early, frames
     )
-    groups = [tuple(far[i : i + 2]) for i in range(0, len(far), 2)]
-    groups += [(core_mask,), (seq_masks[0], clip_masks[1])]
     early_frames = Frames(early_rows, groups)
     middle_row = local_rows // 2
     others = [swap_with(other_rows[:middle_row], half)]
     last_chain.step()
     early_frames.step()
     if head_count < 4:
-        mixed = run(two_clips, result, [mixed_others], LOW)
+        mixed = run(fill_clip, result, [mixed_others])
     while late_frames.arrived is not None:
         late_frames.step()
-    mod_late, sum_late = run(modulation_back, condition, late_frames.rows)
+    mod_late, sum_late = run(modulation_back, frames_condition, late_frames.rows)
     down_sum, up_sum, output_sum = run(settle, weight_sums, own_down, up_blocks)
     early_frames.step()
     last_chain.step()
     others.append(swap_with(run(copy_of, other_rows[middle_row:]), half))
     while early_frames.arrived is not None:
         early_frames.step()
-    mod_early, sum_early = run(
-        modulation_back, condition_of(ranks_of(groups)), early_frames.rows
-    )
+    mod_early, sum_early = run(modulation_back, frames_condition, early_frames.rows)
     while last_chain.arrived is not None:
         last_chain.step()
 
@@ -1641,7 +1628,7 @@
             swap_with(squares, second) + swap_with(squares, first ^ second)
         )
         last.append(squares)
-    input_grad = run(two_clips, own_rows, others, WIDE)
+    input_grad = run(fill_clip, own_rows, others)
     if len(order) % 2:
         squares = squares + swap_with(squares, order[-1])
     grad_norm = jnp.sqrt(squares[0, 0])

time: 891 us -> 892 us (level)
  Pallas kernels: 538 us -> 526 us
  waiting for transfers between devices: 115 us -> 126 us
    pallas_call x55 -> x52, Pallas kernels: 538 us -> 526 us  [call(): pl.pallas_call(body, grid_spec=pltpu.PrefetchScalarGridSpec(num_scalar_pr...]
    ppermute x63 -> x65, waiting for transfers between devices: 96.3 us -> 108 us  [swap_with(): return lax.ppermute(value, AXES, [(i, i ^ mask) for i in range(devices)])]
    ppermute x63 -> x65, starting transfers between devices: 90.3 us -> 91.3 us  [swap_with(): return lax.ppermute(value, AXES, [(i, i ^ mask) for i in range(devices)])]
    unnamed x190 -> x188, local copies, waits for them, and re-layouts: 22.2 us -> 21.4 us
  transfers between devices with their start and end apart: 77 -> 79, of which waited for: 19 -> 20; matrix products, arithmetic and copies ran while one was open for 5% -> 5% of each run, Pallas kernels for 49% -> 48%
where the time goes in v5:
time: 892 us; the launch traced here: 881 us
  Pallas kernels  526 us (59%)
  starting transfers between devices  142 us (16%)
  waiting for transfers between devices  126 us (14%)
  local copies, waits for them, and re-layouts  38.2 us (4%)
  between operations  25.2 us (3%)
  other arithmetic  21 us (2%)
    pallas_call x52, Pallas kernels, call(): pl.pallas_call(body, grid_spec=pltpu.PrefetchScalarGridSpec(num_scalar_pr...  526 us
    ppermute x65, waiting for transfers between devices, swap_with(): return lax.ppermute(value, AXES, [(i, i ^ mask) for i in range(devices)])  108 us
    ppermute x65, starting transfers between devices, swap_with(): return lax.ppermute(value, AXES, [(i, i ^ mask) for i in range(devices)])  91.3 us
    all_to_all x11, starting transfers between devices, exchange(): return lax.all_to_all(value, 'seq', 0, 0, axis_index_groups=group_ids)  45.5 us
    unnamed x188, local copies, waits for them, and re-layouts  21.4 us
    all_to_all x11, waiting for transfers between devices, exchange(): return lax.all_to_all(value, 'seq', 0, 0, axis_index_groups=group_ids)  18 us
  transfers between devices with their start and end apart: 79, of which 20 were waited for; matrix products, arithmetic and copies ran while one was open for 5% of the time, Pallas kernels for 48%

profile of v5, /device:TPU:0, one launch (start us, length us, event | category | flops | bytes accessed | tf_op | source)
XLA Modules:
  0.0 880.8 jit_solution(9386671698293944101)
XLA Ops:
  37.0 18.3 %collective-permute-done.1 = bf16[1,64,3072]{2,1,0:T(8,128)(2,1)} collective-permute-done((bf16[1,64,3072]{2,1,0:T(8,128)(2,1)}, bf16[1,64,3072]{2,1,0:T(8,128)(2,1)}, u32[]{:S(2)}, u32[]{:S(2)}) %collective-permute-start.1) | collective-permute-done | bytes 393248 | tf_op jit(solution)/shard_map/ppermute | solution.py:1232
  63.4 24.7 %collective-permute-done.7.refs_6_ = f32[32,2048]{1,0:T(8,128)S(1)} collective-permute-done((f32[32,2048]{1,0:T(8,128)}, f32[32,2048]{1,0:T(8,128)S(1)}, u32[]{:S(2)}, u32[]{:S(2)}) %collective-permute-start.7) | collective-permute-done | bytes 262176 | tf_op jit(solution)/shard_map/ppermute | solution.py:1232
  95.1 19.8 %collective-permute-done.10.refs_6_ = f32[16,2048]{1,0:T(8,128)S(1)} collective-permute-done((f32[16,2048]{1,0:T(8,128)}, f32[16,2048]{1,0:T(8,128)S(1)}, u32[]{:S(2)}, u32[]{:S(2)}) %collective-permute-start.10) | collective-permute-done | bytes 131104 | tf_op jit(solution)/shard_map/ppermute | solution.py:1232
  126.7 6.1 collective-permute-done.13.refs_6_
  134.5 6.6 join_and_add.10
  157.1 6.2 project.4.refs_2_
  171.4 6.2 project.5.refs_3_
  191.3 19.0 %attend.4 = (bf16[4,192,1024]{2,1,0:T(8,128)(2,1)}, f32[64,4096]{1,0:T(8,128)}, f32[1,4096]{1,0:T(1,128)}) custom-call(s32[3]{0:T(128)} %pad_add_fusion.refs_0_, bf16[4,3,64,1024]{3,2,1,0:T(8,128)(2,1)} %copy-done.7, f32[16,4096]{1,0:T(8,128)} %get-tuple-element.139.refs_2_), custom_call_target="tpu_custom_call" | custom-call | flops 20700000256 | bytes 54000000 | tf_op jit(solution)/shard_map/attend/pallas_call | solution.py:116
  224.0 6.3 project.6.refs_3_
  235.8 19.1 %attend.5 = (bf16[4,192,1024]{2,1,0:T(8,128)(2,1)}, f32[64,4096]{1,0:T(8,128)}, f32[1,4096]{1,0:T(1,128)}) custom-call(s32[3]{0:T(128)} %pad_add_fusion.refs_0_, bf16[4,3,64,1024]{3,2,1,0:T(8,128)(2,1)} %copy-done.8, bf16[4,192,1024]{2,1,0:T(8,128)(2,1)} %get-tuple-element.142.refs_2_, ...), custom_call_target="tpu_custom_call", output_to_operand_aliasing={{0}: (2, {})} | custom-call | flops 20700000256 | bytes 54000000 | tf_op jit(solution)/shard_map/attend/pallas_call | solution.py:116
  257.7 6.2 project.7.refs_3_
  268.8 19.0 %attend.6 = (bf16[4,192,1024]{2,1,0:T(8,128)(2,1)}, f32[64,4096]{1,0:T(8,128)}, f32[1,4096]{1,0:T(1,128)}) custom-call(s32[3]{0:T(128)} %pad_add_fusion.refs_0_, bf16[4,3,64,1024]{3,2,1,0:T(8,128)(2,1)} %copy-done.9, bf16[4,192,1024]{2,1,0:T(8,128)(2,1)} %get-tuple-element.143.refs_2_, ...), custom_call_target="tpu_custom_call", output_to_operand_aliasing={{0}: (2, {})} | custom-call | flops 20700000256 | bytes 54000000 | tf_op jit(solution)/shard_map/attend/pallas_call | solution.py:116
  287.8 9.7 %all-to-all-done.5.refs_1_ = bf16[4,3,64,1024]{3,2,1,0:T(8,128)(2,1)S(1)} async-done(((bf16[4,3,64,1024]{3,2,1,0:T(8,128)(2,1)}), bf16[4,3,64,1024]{3,2,1,0:T(8,128)(2,1)S(1)}, u32[]{:S(2)}, u32[]{:S(2)}) %all-to-all-start.5) | async-done | bytes 1572896 | tf_op jit(solution)/shard_map/all_to_all | solution.py:1383
  301.4 19.0 %attend.7 = (bf16[4,64,1024]{2,1,0:T(8,128)(2,1)}, f32[64,4096]{1,0:T(8,128)}, f32[1,4096]{1,0:T(1,128)}) custom-call(s32[3]{0:T(128)} %pad_add_fusion.refs_0_, bf16[4,3,64,1024]{3,2,1,0:T(8,128)(2,1)} %copy-done.10, f32[1,4096]{1,0:T(1,128)} %get-tuple-element.149.refs_2_.refs_4_, bf16[256,1024]{1,0:T(8,128)(2,1)} %collective-permute-done.23.refs_3_), custom_call_target="tpu_custom_call" | custom-call | flops 20700000256 | bytes 54000000 | tf_op jit(solution)/shard_map/attend/pallas_call | solution.py:116
  331.8 11.6 %middle_part.1 = (bf16[1024,1024]{1,0:T(8,128)(2,1)}, f32[1024,1024]{1,0:T(8,128)}, f32[1024,1024]{1,0:T(8,128)}, bf16[1024,1024]{1,0:T(8,128)(2,1)}, bf16[1024,1024]{1,0:T(8,128)(2,1)}) custom-call(s32[3]{0:T(128)} %pad_add_fusion.refs_0_, bf16[4,192,1024]{2,1,0:T(8,128)(2,1)} %copy-done.14, bf16[64,1024]{1,0:T(8,128)(2,1)} %get-tuple-element.259.refs_2_, ...), custom_call_target="tpu_custom_call" | custom-call | flops 13799999488 | bytes 36000000 | tf_op jit(solution)/shard_map/middle_part/pallas_call | solution.py:116
  343.4 66.8 %feed.1 = (f32[1024,1024]{1,0:T(8,128)}, f32[1024,1024]{1,0:T(8,128)}, bf16[32,288,1024]{2,1,0:T(8,128)(2,1)}) custom-call(s32[3]{0:T(128)} %pad_add_fusion.refs_0_, bf16[1024,1024]{1,0:T(8,128)(2,1)} %get-tuple-element.153.refs_1_, bf16[1024,1024]{1,0:T(8,128)(2,1)} %get-tuple-element.154.refs_2_.refs_5_, bf16[32,288,1024]{2,1,0:T(8,128)(2,1)} %bitcast.89, ...), custom_call_target="tpu_custom_call" | custom-call | flops 73600000000 | bytes 192000000 | tf_op jit(solution)/shard_map/feed/pallas_call | solution.py:116
  410.2 13.0 %middle_back.1 = (bf16[2,512,1024]{2,1,0:T(8,128)(2,1)}, f32[1024,1024]{1,0:T(8,128)}, bf16[1024,1024]{1,0:T(8,128)(2,1)}, f32[4,4096]{1,0:T(4,128)}) custom-call(s32[3]{0:T(128)} %pad_add_fusion.refs_0_, f32[1024,1024]{1,0:T(8,128)} %get-tuple-element.152.refs_1_, f32[1024,1024]{1,0:T(8,128)} %get-tuple-element.155.refs_2_, ...), custom_call_target="tpu_custom_call" | custom-call | flops 13799999488 | bytes 36000000 | tf_op jit(solution)/shard_map/middle_back/pallas_call | solution.py:116
  423.2 9.4 %hand_out.1 = (bf16[32,288,1024]{2,1,0:T(8,128)(2,1)}, bf16[4,64,1024]{2,1,0:T(8,128)(2,1)}, bf16[4,192,1024]{2,1,0:T(8,128)(2,1)}) custom-call(s32[3]{0:T(128)} %pad_add_fusion.refs_0_, bf16[32,288,1024]{2,1,0:T(8,128)(2,1)} %bitcast.91, bf16[1024,1024]{1,0:T(8,128)(2,1)} %get-tuple-element.160.refs_2_, ...), custom_call_target="tpu_custom_call", output_to_operand_aliasing={{0}: (4, {})} | custom-call | flops 10350000128 | bytes 27000000 | tf_op jit(solution)/shard_map/hand_out/pallas_call | solution.py:116
  440.6 6.2 all-to-all-done.7.refs_6_.refs_2_
  454.2 43.3 %attend_back.4.refs_3_ = bf16[4,3,64,1024]{3,2,1,0:T(8,128)(2,1)} custom-call(s32[3]{0:T(128)} %pad_add_fusion.refs_0_, bf16[4,3,64,1024]{3,2,1,0:T(8,128)(2,1)} %copy-done.10, bf16[4,64,1024]{2,1,0:T(8,128)(2,1)} %copy-done.27, f32[64,4096]{1,0:T(8,128)} %get-tuple-element.166.refs_3_, f32[1,4096]{1,0:T(1,128)} %get-tuple-element.151.refs_11_.refs_4_, ...), custom_call_target="tpu_custom_call" | custom-call | flops 29899999232 | bytes 78000000 | tf_op jit(solution)/shard_map/attend_back/pallas_call | solution.py:116
  508.7 43.1 %attend_back.5.refs_5_ = bf16[4,3,64,1024]{3,2,1,0:T(8,128)(2,1)} custom-call(s32[3]{0:T(128)} %pad_add_fusion.refs_0_, bf16[4,3,64,1024]{3,2,1,0:T(8,128)(2,1)} %copy-done.9, bf16[4,192,1024]{2,1,0:T(8,128)(2,1)} %copy-done.11, f32[64,4096]{1,0:T(8,128)} %get-tuple-element.164.refs_3_, f32[1,4096]{1,0:T(1,128)} %get-tuple-element.149.refs_2_.refs_4_, ...), custom_call_target="tpu_custom_call" | custom-call | flops 29899999232 | bytes 78000000 | tf_op jit(solution)/shard_map/attend_back/pallas_call | solution.py:116
  560.0 43.2 %attend_back.6.refs_4_ = bf16[4,3,64,1024]{3,2,1,0:T(8,128)(2,1)} custom-call(s32[3]{0:T(128)} %pad_add_fusion.refs_0_, bf16[4,3,64,1024]{3,2,1,0:T(8,128)(2,1)} %copy-done.8, bf16[4,192,1024]{2,1,0:T(8,128)(2,1)} %copy-done.11, f32[64,4096]{1,0:T(8,128)} %get-tuple-element.167.refs_3_, f32[1,4096]{1,0:T(1,128)} %get-tuple-element.147.refs_5_.refs_4_, ...), custom_call_target="tpu_custom_call" | custom-call | flops 29899999232 | bytes 78000000 | tf_op jit(solution)/shard_map/attend_back/pallas_call | solution.py:116
  603.2 10.0 %joint_back.4 = (bf16[2,256,1536]{2,1,0:T(8,128)(2,1)}, f32[2,256,1536]{2,1,0:T(8,128)}, f32[1024,1024]{1,0:T(8,128)}) custom-call(s32[3]{0:T(128)} %pad_add_fusion.refs_0_, bf16[4,3,64,1024]{3,2,1,0:T(8,128)(2,1)} %copy-done.15, bf16[1024,1024]{1,0:T(8,128)(2,1)} %norm_one.1.refs_1_.refs_5_.refs_2_, bf16[1024,1536]{1,0:T(8,128)(2,1)} %bitcast.139, ...), custom_call_target="tpu_custom_call" | custom-call | flops 14949999616 | bytes 39000000 | tf_op jit(solution)/shard_map/joint_back/pallas_call | solution.py:116
  614.3 11.0 %joint_back.5 = (bf16[2,256,1536]{2,1,0:T(8,128)(2,1)}, f32[2,256,1536]{2,1,0:T(8,128)}, f32[1024,1024]{1,0:T(8,128)}) custom-call(s32[3]{0:T(128)} %pad_add_fusion.refs_0_, bf16[4,3,64,1024]{3,2,1,0:T(8,128)(2,1)} %copy-done.16, bf16[1024,1024]{1,0:T(8,128)(2,1)} %norm_one.1.refs_1_.refs_5_.refs_2_, ...), custom_call_target="tpu_custom_call", output_to_operand_aliasing={{0}: (5, {}), {1}: (6, {})} | custom-call | flops 14949999616 | bytes 39000000 | tf_op jit(solution)/shard_map/joint_back/pallas_call | solution.py:116
  641.2 43.0 %attend_back.7.refs_5_ = bf16[4,3,64,1024]{3,2,1,0:T(8,128)(2,1)} custom-call(s32[3]{0:T(128)} %pad_add_fusion.refs_0_, bf16[4,3,64,1024]{3,2,1,0:T(8,128)(2,1)} %copy-done.7, bf16[4,192,1024]{2,1,0:T(8,128)(2,1)} %copy-done.11, f32[64,4096]{1,0:T(8,128)} %get-tuple-element.178.refs_3_, f32[1,4096]{1,0:T(1,128)} %get-tuple-element.140.refs_5_.refs_4_, ...), custom_call_target="tpu_custom_call" | custom-call | flops 29899999232 | bytes 78000000 | tf_op jit(solution)/shard_map/attend_back/pallas_call | solution.py:116
  700.2 10.8 %joint_back.6 = (bf16[2,256,1536]{2,1,0:T(8,128)(2,1)}, f32[2,256,1536]{2,1,0:T(8,128)}, f32[1024,1024]{1,0:T(8,128)}) custom-call(s32[3]{0:T(128)} %pad_add_fusion.refs_0_, bf16[4,3,64,1024]{3,2,1,0:T(8,128)(2,1)} %copy-done.12, bf16[1024,1024]{1,0:T(8,128)(2,1)} %norm_one.1.refs_1_.refs_5_.refs_2_, bf16[1024,1536]{1,0:T(8,128)(2,1)} %bitcast.135, ...), custom_call_target="tpu_custom_call" | custom-call | flops 14949999616 | bytes 39000000 | tf_op jit(solution)/shard_map/joint_back/pallas_call | solution.py:116
  711.0 9.4 %collective-permute-done.39.refs_2_ = bf16[1,32,1536]{2,1,0:T(8,128)(2,1)S(1)} collective-permute-done((bf16[1,32,1536]{2,1,0:T(8,128)(2,1)}, bf16[1,32,1536]{2,1,0:T(8,128)(2,1)S(1)}, u32[]{:S(2)}, u32[]{:S(2)}) %collective-permute-start.39) | collective-permute-done | bytes 98336 | tf_op jit(solution)/shard_map/ppermute | solution.py:1232
  732.4 11.0 %joint_back.7 = (bf16[2,256,1536]{2,1,0:T(8,128)(2,1)}, f32[2,256,1536]{2,1,0:T(8,128)}, f32[1024,1024]{1,0:T(8,128)}) custom-call(s32[3]{0:T(128)} %pad_add_fusion.refs_0_, bf16[4,3,64,1024]{3,2,1,0:T(8,128)(2,1)} %copy-done.13, bf16[1024,1024]{1,0:T(8,128)(2,1)} %norm_one.1.refs_1_.refs_5_.refs_2_, ...), custom_call_target="tpu_custom_call", output_to_operand_aliasing={{0}: (5, {}), {1}: (6, {})} | custom-call | flops 14949999616 | bytes 39000000 | tf_op jit(solution)/shard_map/joint_back/pallas_call | solution.py:116
  743.7 8.4 tokens_back.1
  786.4 6.8 collective-permute-done.45
  828.5 7.2 collective-permute-start.59
  838.7 6.4 collective-permute-start.63
  (440 shorter events, 308.8 us)
Async XLA Ops:
  7.2 323.4 %all-gather.3.cloned.1.call-start = ((), (), s32[]{:S(2)}) async-start(), calls=%async_computation.14 | async-start | bytes 19464192 | tf_op jit(solution)/shard_map/all_gather | solution.py:1317
  31.7 83.3 %all-to-all-start = ((bf16[2,512,1024]{2,1,0:T(8,128)(2,1)}), bf16[2,512,1024]{2,1,0:T(8,128)(2,1)S(1)}, u32[]{:S(2)}, u32[]{:S(2)}) async-start(bf16[2,512,1024]{2,1,0:T(8,128)(2,1)} %param.24), calls=%async_computation | async-start | bytes 4194304 | tf_op jit(solution)/shard_map/all_to_all | solution.py:1252
  59.8 28.3 %collective-permute-start.6 = (bf16[1,128,1536]{2,1,0:T(8,128)(2,1)S(1)}, bf16[1,128,1536]{2,1,0:T(8,128)(2,1)S(1)}, u32[]{:S(2)}, u32[]{:S(2)}) collective-permute-start(bf16[1,128,1536]{2,1,0:T(8,128)(2,1)S(1)} %get-tuple-element.254.refs_3_), channel_id=1, source_target_pairs={{0,16},{1,17},{2,18},{3,19},{4,20},{5,21},{6,22},{7,23},{8,24},{9,... | collective-permute-start | bytes 1179656 | tf_op jit(solution)/shard_map/ppermute | solution.py:1232
  181.9 28.4 %collective-permute-start.16 = (f32[16,4096]{1,0:T(8,128)}, f32[16,4096]{1,0:T(8,128)S(1)}, u32[]{:S(2)}, u32[]{:S(2)}) collective-permute-start(f32[16,4096]{1,0:T(8,128)} %get-tuple-element.137), channel_id=1, source_target_pairs={{0,1},{1,0},{2,3},{3,2},{4,5},{5,4},{6,7},{7,6},{8,9},{9,8},{10,11... | collective-permute-start | bytes 786440 | tf_op jit(solution)/shard_map/ppermute | solution.py:1232
  187.5 42.8 %all-to-all-start.3 = ((bf16[4,3,64,1024]{3,2,1,0:T(8,128)(2,1)}), bf16[4,3,64,1024]{3,2,1,0:T(8,128)(2,1)S(1)}, u32[]{:S(2)}, u32[]{:S(2)}) async-start(bf16[4,3,64,1024]{3,2,1,0:T(8,128)(2,1)} %project.5.refs_3_), calls=%async_computation.3 | async-start | bytes 3145728 | tf_op jit(solution)/shard_map/all_to_all | solution.py:1383
  213.7 41.2 %collective-permute-start.19 = (f32[4,4096]{1,0:T(4,128)}, f32[4,4096]{1,0:T(4,128)S(1)}, u32[]{:S(2)}, u32[]{:S(2)}) collective-permute-start(f32[4,4096]{1,0:T(4,128)} %get-tuple-element.145), channel_id=1, source_target_pairs={{0,4},{1,5},{2,6},{3,7},{4,0},{5,1},{6,2},{7,3},{8,12},{9,13},{10,... | collective-permute-start | bytes 196616 | tf_op jit(solution)/shard_map/ppermute | solution.py:1232
  215.6 39.3 %collective-permute-start.20 = (f32[4,4096]{1,0:T(4,128)}, f32[4,4096]{1,0:T(4,128)S(1)}, u32[]{:S(2)}, u32[]{:S(2)}) collective-permute-start(f32[4,4096]{1,0:T(4,128)} %get-tuple-element.146), channel_id=1, source_target_pairs={{0,2},{1,3},{2,0},{3,1},{4,6},{5,7},{6,4},{7,5},{8,10},{9,11},{10,... | collective-permute-start | bytes 196616 | tf_op jit(solution)/shard_map/ppermute | solution.py:1232
  217.6 37.3 %collective-permute-start.21 = (f32[4,4096]{1,0:T(4,128)}, f32[4,4096]{1,0:T(4,128)S(1)}, u32[]{:S(2)}, u32[]{:S(2)}) collective-permute-start(f32[4,4096]{1,0:T(4,128)} %get-tuple-element.141.refs_2_), channel_id=1, source_target_pairs={{0,6},{1,7},{2,4},{3,5},{4,2},{5,3},{6,0},{7,1},{8,14},{9,15},{10,... | collective-permute-start | bytes 196616 | tf_op jit(solution)/shard_map/ppermute | solution.py:1232
  223.0 34.8 %collective-permute-start.22 = (bf16[256,1024]{1,0:T(8,128)(2,1)}, bf16[256,1024]{1,0:T(8,128)(2,1)}, u32[]{:S(2)}, u32[]{:S(2)}) collective-permute-start(bf16[256,1024]{1,0:T(8,128)(2,1)} %get-tuple-element.251), channel_id=1, source_target_pairs={{0,4},{1,5},{2,6},{3,7},{4,0},{5,1},{6,2},{7,3},{8,12},{9,13},{10,... | collective-permute-start | bytes 1572872 | tf_op jit(solution)/shard_map/ppermute | solution.py:1232
  230.3 33.7 %all-to-all-start.2 = ((bf16[4,3,64,1024]{3,2,1,0:T(8,128)(2,1)}), bf16[4,3,64,1024]{3,2,1,0:T(8,128)(2,1)S(1)}, u32[]{:S(2)}, u32[]{:S(2)}) async-start(bf16[4,3,64,1024]{3,2,1,0:T(8,128)(2,1)} %project.6.refs_3_), calls=%async_computation.2 | async-start | bytes 3145728 | tf_op jit(solution)/shard_map/all_to_all | solution.py:1383
  264.0 33.6 %all-to-all-start.5 = ((bf16[4,3,64,1024]{3,2,1,0:T(8,128)(2,1)}), bf16[4,3,64,1024]{3,2,1,0:T(8,128)(2,1)S(1)}, u32[]{:S(2)}, u32[]{:S(2)}) async-start(bf16[4,3,64,1024]{3,2,1,0:T(8,128)(2,1)} %project.7.refs_3_), calls=%async_computation.5 | async-start | bytes 3145728 | tf_op jit(solution)/shard_map/all_to_all | solution.py:1383
  268.4 33.1 %collective-permute-start.23 = (bf16[256,1024]{1,0:T(8,128)(2,1)}, bf16[256,1024]{1,0:T(8,128)(2,1)}, u32[]{:S(2)}, u32[]{:S(2)}) collective-permute-start(bf16[256,1024]{1,0:T(8,128)(2,1)} %get-tuple-element.250), channel_id=1, source_target_pairs={{0,4},{1,5},{2,6},{3,7},{4,0},{5,1},{6,2},{7,3},{8,12},{9,13},{10,... | collective-permute-start | bytes 1572872 | tf_op jit(solution)/shard_map/ppermute | solution.py:1232
  297.6 33.0 %all-to-all-start.4 = ((bf16[4,192,1024]{2,1,0:T(8,128)(2,1)}), bf16[4,192,1024]{2,1,0:T(8,128)(2,1)S(1)}, u32[]{:S(2)}, u32[]{:S(2)}) async-start(bf16[4,192,1024]{2,1,0:T(8,128)(2,1)} %get-tuple-element.148), calls=%async_computation.4 | async-start | bytes 3145728 | tf_op jit(solution)/shard_map/all_to_all | solution.py:1383
  301.2 475.0 %reduce-scatter.2.cloned.1.call-start = ((), (), s32[]{:S(2)}) async-start(), calls=%async_computation.13 | async-start | bytes 19464192 | tf_op jit(solution)/shard_map/reduce_scatter | solution.py:1499
  446.8 57.4 %all-to-all-start.6 = ((bf16[4,192,1024]{2,1,0:T(8,128)(2,1)}), bf16[4,192,1024]{2,1,0:T(8,128)(2,1)S(1)}, u32[]{:S(2)}, u32[]{:S(2)}) async-start(bf16[4,192,1024]{2,1,0:T(8,128)(2,1)} %get-tuple-element.163.refs_5_), calls=%async_computation.6 | async-start | bytes 3145728 | tf_op jit(solution)/shard_map/all_to_all | solution.py:1383
  454.2 43.3 %collective-permute-start.31 = (f32[16,4096]{1,0:T(8,128)}, f32[16,4096]{1,0:T(8,128)S(1)}, u32[]{:S(2)}, u32[]{:S(2)}) collective-permute-start(f32[16,4096]{1,0:T(8,128)} %stack_rows.6.refs_7_.refs_1_), channel_id=1, source_target_pairs={{0,8},{1,9},{2,10},{3,11},{4,12},{5,13},{6,14},{7,15},{8,0},{9,1},... | collective-permute-start | bytes 786440 | tf_op jit(solution)/shard_map/ppermute | solution.py:1232
  500.7 51.0 %collective-permute-start.34 = (f32[32,4096]{1,0:T(8,128)}, f32[32,4096]{1,0:T(8,128)}, u32[]{:S(2)}, u32[]{:S(2)}) collective-permute-start(f32[32,4096]{1,0:T(8,128)} %stack_rows.7.refs_7_.refs_1_), channel_id=1, source_target_pairs={{0,17},{1,16},{2,19},{3,18},{4,21},{5,20},{6,23},{7,22},{8,25},{9,... | collective-permute-start | bytes 1572872 | tf_op jit(solution)/shard_map/ppermute | solution.py:1232
  503.3 48.4 %collective-permute-start.33 = (f32[32,4096]{1,0:T(8,128)}, f32[32,4096]{1,0:T(8,128)}, u32[]{:S(2)}, u32[]{:S(2)}) collective-permute-start(f32[32,4096]{1,0:T(8,128)} %stack_rows.7.refs_7_.refs_1_), channel_id=1, source_target_pairs={{0,16},{1,17},{2,18},{3,19},{4,20},{5,21},{6,22},{7,23},{8,24},{9,... | collective-permute-start | bytes 1572872 | tf_op jit(solution)/shard_map/ppermute | solution.py:1232
  504.2 47.5 %collective-permute-start.32 = (f32[32,4096]{1,0:T(8,128)}, f32[32,4096]{1,0:T(8,128)}, u32[]{:S(2)}, u32[]{:S(2)}) collective-permute-start(f32[32,4096]{1,0:T(8,128)} %stack_rows.7.refs_7_.refs_1_), channel_id=1, source_target_pairs={{0,1},{1,0},{2,3},{3,2},{4,5},{5,4},{6,7},{7,6},{8,9},{9,8},{10,11... | collective-permute-start | bytes 1572872 | tf_op jit(solution)/shard_map/ppermute | solution.py:1232
  504.2 51.2 %all-to-all-start.9 = ((bf16[4,3,64,1024]{3,2,1,0:T(8,128)(2,1)}), bf16[4,3,64,1024]{3,2,1,0:T(8,128)(2,1)S(1)}, u32[]{:S(2)}, u32[]{:S(2)}) async-start(bf16[4,3,64,1024]{3,2,1,0:T(8,128)(2,1)} %attend_back.4.refs_3_), calls=%async_computation.9 | async-start | bytes 3145728 | tf_op jit(solution)/shard_map/all_to_all | solution.py:1383
  555.4 57.8 %all-to-all-start.8 = ((bf16[4,3,64,1024]{3,2,1,0:T(8,128)(2,1)}), bf16[4,3,64,1024]{3,2,1,0:T(8,128)(2,1)S(1)}, u32[]{:S(2)}, u32[]{:S(2)}) async-start(bf16[4,3,64,1024]{3,2,1,0:T(8,128)(2,1)} %attend_back.5.refs_5_), calls=%async_computation.8 | async-start | bytes 3145728 | tf_op jit(solution)/shard_map/all_to_all | solution.py:1383
  627.6 69.9 %collective-permute-start.27 = (bf16[512,1024]{1,0:T(8,128)(2,1)}, bf16[512,1024]{1,0:T(8,128)(2,1)}, u32[]{:S(2)}, u32[]{:S(2)}) collective-permute-start(bf16[512,1024]{1,0:T(8,128)(2,1)} %dynamic-slice_bitcast_fusion), channel_id=1, source_target_pairs={{0,4},{1,5},{2,6},{3,7},{4,0},{5,1},{6,2},{7,3},{8,12},{9,13},{10,... | collective-permute-start | bytes 3145736 | tf_op jit(solution)/shard_map/ppermute | solution.py:1232
  627.7 56.6 %all-to-all-start.11 = ((bf16[4,3,64,1024]{3,2,1,0:T(8,128)(2,1)}), bf16[4,3,64,1024]{3,2,1,0:T(8,128)(2,1)S(1)}, u32[]{:S(2)}, u32[]{:S(2)}) async-start(bf16[4,3,64,1024]{3,2,1,0:T(8,128)(2,1)} %attend_back.6.refs_4_), calls=%async_computation.11 | async-start | bytes 3145728 | tf_op jit(solution)/shard_map/all_to_all | solution.py:1383
  637.7 50.9 %collective-permute-start.36 = (bf16[4,32,1536]{2,1,0:T(8,128)(2,1)}, bf16[4,32,1536]{2,1,0:T(8,128)(2,1)S(1)}, u32[]{:S(2)}, u32[]{:S(2)}) collective-permute-start(bf16[4,32,1536]{2,1,0:T(8,128)(2,1)} %bitcast.123), channel_id=1, source_target_pairs={{0,16},{1,17},{2,18},{3,19},{4,20},{5,21},{6,22},{7,23},{8,24},{9,... | collective-permute-start | bytes 1179656 | tf_op jit(solution)/shard_map/ppermute | solution.py:1232
  638.9 49.7 %collective-permute-start.37 = (bf16[4,32,1536]{2,1,0:T(8,128)(2,1)}, bf16[4,32,1536]{2,1,0:T(8,128)(2,1)}, u32[]{:S(2)}, u32[]{:S(2)}) collective-permute-start(bf16[4,32,1536]{2,1,0:T(8,128)(2,1)} %bitcast.122), channel_id=1, source_target_pairs={{0,1},{1,0},{2,3},{3,2},{4,5},{5,4},{6,7},{7,6},{8,9},{9,8},{10,11... | collective-permute-start | bytes 1179656 | tf_op jit(solution)/shard_map/ppermute | solution.py:1232
  641.0 47.7 %collective-permute-start.38 = (bf16[4,32,1536]{2,1,0:T(8,128)(2,1)}, bf16[4,32,1536]{2,1,0:T(8,128)(2,1)}, u32[]{:S(2)}, u32[]{:S(2)}) collective-permute-start(bf16[4,32,1536]{2,1,0:T(8,128)(2,1)} %bitcast.121), channel_id=1, source_target_pairs={{0,17},{1,16},{2,19},{3,18},{4,21},{5,20},{6,23},{7,22},{8,25},{9,... | collective-permute-start | bytes 1179656 | tf_op jit(solution)/shard_map/ppermute | solution.py:1232
  684.3 47.0 %all-to-all-start.10 = ((bf16[4,3,64,1024]{3,2,1,0:T(8,128)(2,1)}), bf16[4,3,64,1024]{3,2,1,0:T(8,128)(2,1)S(1)}, u32[]{:S(2)}, u32[]{:S(2)}) async-start(bf16[4,3,64,1024]{3,2,1,0:T(8,128)(2,1)} %attend_back.7.refs_5_), calls=%async_computation.10 | async-start | bytes 3145728 | tf_op jit(solution)/shard_map/all_to_all | solution.py:1383
  692.5 28.0 %collective-permute-start.39 = (bf16[1,32,1536]{2,1,0:T(8,128)(2,1)}, bf16[1,32,1536]{2,1,0:T(8,128)(2,1)S(1)}, u32[]{:S(2)}, u32[]{:S(2)}) collective-permute-start(bf16[1,32,1536]{2,1,0:T(8,128)(2,1)} %bitcast.132), channel_id=1, source_target_pairs={{0,4},{1,5},{2,6},{3,7},{4,0},{5,1},{6,2},{7,3},{8,12},{9,13},{10,... | collective-permute-start | bytes 294920 | tf_op jit(solution)/shard_map/ppermute | solution.py:1232
  695.5 28.4 %collective-permute-start.40 = (bf16[1,32,1536]{2,1,0:T(8,128)(2,1)}, bf16[1,32,1536]{2,1,0:T(8,128)(2,1)S(1)}, u32[]{:S(2)}, u32[]{:S(2)}) collective-permute-start(bf16[1,32,1536]{2,1,0:T(8,128)(2,1)} %bitcast.131), channel_id=1, source_target_pairs={{0,2},{1,3},{2,0},{3,1},{4,6},{5,7},{6,4},{7,5},{8,10},{9,11},{10,... | collective-permute-start | bytes 294920 | tf_op jit(solution)/shard_map/ppermute | solution.py:1232
  697.5 30.6 %collective-permute-start.41 = (bf16[1,32,1536]{2,1,0:T(8,128)(2,1)}, bf16[1,32,1536]{2,1,0:T(8,128)(2,1)S(1)}, u32[]{:S(2)}, u32[]{:S(2)}) collective-permute-start(bf16[1,32,1536]{2,1,0:T(8,128)(2,1)} %bitcast.130), channel_id=1, source_target_pairs={{0,6},{1,7},{2,4},{3,5},{4,2},{5,3},{6,0},{7,1},{8,14},{9,15},{10,... | collective-permute-start | bytes 294920 | tf_op jit(solution)/shard_map/ppermute | solution.py:1232
  758.7 110.3 %collective-permute-start.42 = (bf16[256,1024]{1,0:T(8,128)(2,1)}, bf16[256,1024]{1,0:T(8,128)(2,1)}, u32[]{:S(2)}, u32[]{:S(2)}) collective-permute-start(bf16[256,1024]{1,0:T(8,128)(2,1)} %get-tuple-element.249), channel_id=1, source_target_pairs={{0,4},{1,5},{2,6},{3,7},{4,0},{5,1},{6,2},{7,3},{8,12},{9,13},{10,... | collective-permute-start | bytes 1572872 | tf_op jit(solution)/shard_map/ppermute | solution.py:1232
  806.7 62.3 %collective-permute-start.51 = (bf16[256,1024]{1,0:T(8,128)(2,1)}, bf16[256,1024]{1,0:T(8,128)(2,1)}, u32[]{:S(2)}, u32[]{:S(2)}) collective-permute-start(bf16[256,1024]{1,0:T(8,128)(2,1)} %copy_of.3.refs_5_), channel_id=1, source_target_pairs={{0,4},{1,5},{2,6},{3,7},{4,0},{5,1},{6,2},{7,3},{8,12},{9,13},{10,... | collective-permute-start | bytes 1572872 | tf_op jit(solution)/shard_map/ppermute | solution.py:1232
  (138 other events, 1104.2 us)
Sparse Core Ops, SparseCore 0:
  11.6 161.9 all-gather.2
  432.8 284.9 reduce-scatter.1
